TPU v7x, 32 devices: a whole 2x2x4 slice. The times are simulated.
32 devices in a mesh: parts: 2 (over y), table: 4 (over z), bal: 2 (over x), mp: 2 (over core).
Axes of the slice: x: 2, y: 2, z: 4, core: 2. Of those that a mesh axis runs over, the one named last changes fastest.
Arguments:
- table_rows: bfloat16 [8192, 512], P('table'), may hold values from -127 to 127
- row_scale: float32 [8192], P('table'), may hold values from 0.004 to 0.04
- hist_ids: int32 [64, 256], P('parts'), parts along dimension 0, may hold values from 0 to 8191, as said below
- lengths: int32 [64], P(('parts', 'table')), parts along dimension 0, may hold values from 32 to 256, as said below
- plan: int32 [64], P('parts'), parts along dimension 0, may hold values from 0 to 7, as said below
- time_bucket: int32 [64, 256], P(('parts', 'table')), parts along dimension 0, may hold values from 0 to 15
- embed_proj: bfloat16 [512, 1024], P(None, 'table'), may hold values from -0.25 to 0.25
- in_gain: float32 [1024], replicated, may hold values from 0.1 to 1.9
- qkvu_proj: bfloat16 [4, 1024, 1024], P(None, 'table', 'mp'), may hold values from -0.1875 to 0.1875
- out_gain: float32 [1024], P('mp'), may hold values from 0.1 to 1.9
- out_proj: bfloat16 [1024, 1024], P('mp', 'table'), may hold values from -0.1875 to 0.1875
- pos_bias: float32 [8, 32], P('mp'), may hold values from -4 to 4
- time_bias: float32 [8, 16], P('mp'), may hold values from -4 to 4
Outputs:
- layer_out: bfloat16 [64, 256, 1024], P(('parts', 'table', 'bal'), None, 'mp'), parts along dimension 0
There are 2 independent parts, one for each index of `parts`. A program takes and returns all parts, laid end to end along the dimension named above; an argument that names none is the same for every part. Nothing has to cross between parts.
Inputs may be any that keep to these rules, and one draw needn't show every extreme that they name: Within each group of 8 consecutive users, plan is a permutation of 0 to 7; slot s belongs to bal index s // 4. `lengths`: every group of 8 consecutive users has a user of length 256. `hist_ids`: take the 4 users whose slots belong to one bal index of a group, and the first or the second 128 positions of their histories: at most 256 of these ids lie in one table shard (id // 2048), and exactly 256 in some shard.
All inputs are finite; a program needn't handle non-finite values.
Results may differ from a plain program's by a relative error of at most 0.0074.
Values may be sent and summed in bfloat16 or wider, within the bound.
No kernel may reach another device: no remote copies, remote signals or barrier semaphores. Data moves between devices by JAX's collectives and lax.ppermute only.
A program may use at most 320 MiB of HBM per device.

v0:
```python
import math

import jax
import jax.numpy as jnp
from jax import lax
from jax.sharding import PartitionSpec as P

epsilon = 1e-05


def distance_bucket(length, buckets):
    pos = jnp.arange(length, dtype=jnp.int32)
    dist = jnp.maximum(pos[:, None] - pos[None, :], 0)
    count = jnp.zeros_like(dist)
    for power in range(4, 20):
        count = count + (dist >= 2**power).astype(jnp.int32)
    return jnp.minimum(jnp.where(dist < 16, dist, 15 + count), buckets - 1)


def body(
    table_rows,
    row_scale,
    hist_ids,
    lengths,
    plan,
    time_bucket,
    embed_proj,
    in_gain,
    qkvu_proj,
    out_gain,
    out_proj,
    pos_bias,
    time_bias,
):
    shards = lax.axis_size("table")
    quarters = lax.axis_size("bal")
    mp_size = lax.axis_size("mp")
    table_pos = lax.axis_index("table")
    bal_pos = lax.axis_index("bal")
    mp_pos = lax.axis_index("mp")
    rows_dev, row_width = table_rows.shape
    users, length = hist_ids.shape
    group = lengths.shape[0]
    per_pair = group // quarters
    half = length // 2
    slots_dev = per_pair * half
    capacity = per_pair * length // shards
    embed_full, qkvu_full, out_full = (
        lax.all_gather(embed_proj, "table", axis=1, tiled=True),
        lax.all_gather(qkvu_proj, "table", axis=1, tiled=True),
        lax.all_gather(out_proj, "table", axis=1, tiled=True),
    )
    plan_groups = plan.reshape(shards, group)
    wanted = bal_pos * per_pair + jnp.arange(per_pair, dtype=jnp.int32)
    members = jnp.arange(group, dtype=jnp.int32)
    picked = jnp.sum(
        jnp.where(plan_groups[:, None, :] == wanted[None, :, None], members[None, None, :], 0),
        axis=2,
    )
    chosen = jnp.take_along_axis(
        hist_ids.reshape(shards, group, length), picked[:, :, None], axis=1
    )
    chosen = lax.dynamic_slice_in_dim(chosen, mp_pos * half, half, 2).reshape(shards, slots_dev)
    owner = chosen // rows_dev
    local_row = chosen % rows_dev
    mine = owner == table_pos
    rank = jnp.cumsum(mine.astype(jnp.int32), axis=1) - 1
    target = jnp.where(mine, rank, capacity)
    dest_rows = jnp.broadcast_to(jnp.arange(shards, dtype=jnp.int32)[:, None], (shards, slots_dev))
    send_index = (
        jnp.zeros((shards, capacity), jnp.int32).at[dest_rows, target].set(local_row, mode="drop")
    )
    replies = (
        table_rows[send_index].astype(jnp.float32) * row_scale[send_index][..., None]
    ).astype(jnp.bfloat16)
    received = lax.all_to_all(replies, "table", split_axis=0, concat_axis=0, tiled=True)
    own_owner = lax.dynamic_index_in_dim(owner, table_pos, 0, keepdims=False)
    onehot = (own_owner[:, None] == jnp.arange(shards, dtype=jnp.int32)[None, :]).astype(jnp.int32)
    own_rank = jnp.sum((jnp.cumsum(onehot, axis=0) - 1) * onehot, axis=1)
    embedded = received[own_owner, own_rank].reshape(per_pair, half, row_width)
    part_x = jnp.dot(
        embedded.reshape(slots_dev, row_width), embed_full, preferred_element_type=jnp.float32
    )
    part_x = part_x.astype(jnp.bfloat16).reshape(per_pair, half, -1)
    x_rows = lax.all_gather(part_x, "mp", axis=1, tiled=True)
    width = embed_full.shape[1]
    x_flat = x_rows.reshape(per_pair * length, width)
    own_pick = lax.dynamic_index_in_dim(picked, table_pos, 0, keepdims=False)
    lens = lengths[own_pick]
    events = time_bucket[own_pick]
    xf = x_flat.astype(jnp.float32)
    mean = jnp.mean(xf, axis=1, keepdims=True)
    var = jnp.mean((xf - mean) ** 2, axis=1, keepdims=True)
    xn = ((xf - mean) * lax.rsqrt(var + epsilon) * in_gain).astype(jnp.bfloat16)
    proj = jnp.einsum("td,cde->cte", xn, qkvu_full, preferred_element_type=jnp.float32)
    act = jax.nn.silu(proj).astype(jnp.bfloat16)
    heads_dev = pos_bias.shape[0]
    head_cols = act.shape[2]
    head_size = head_cols // heads_dev
    upart = act[0]
    vpart = act[1].reshape(per_pair, length, heads_dev, head_size)
    qpart = act[2].reshape(per_pair, length, heads_dev, head_size)
    kpart = act[3].reshape(per_pair, length, heads_dev, head_size)
    scores = jnp.einsum(
        "uihe,ujhe->uhij", qpart, kpart, preferred_element_type=jnp.float32
    ) / math.sqrt(head_size)
    bucket = distance_bucket(length, pos_bias.shape[1])
    diff = jnp.abs(events[:, :, None] - events[:, None, :])
    time_term = jnp.moveaxis(jnp.take(time_bias, diff, axis=1), 0, 1)
    scores = scores + pos_bias[:, bucket][None] + time_term
    pos = jnp.arange(length, dtype=jnp.int32)
    mask = (pos[None, None, :] <= pos[None, :, None]) & (pos[None, None, :] < lens[:, None, None])
    weights = (
        jnp.where(mask[:, None], jax.nn.silu(scores), 0.0)
        / lens.astype(jnp.float32)[:, None, None, None]
    )
    weights = weights.astype(jnp.bfloat16)
    y_part = jnp.einsum("uhij,ujhe->uihe", weights, vpart, preferred_element_type=jnp.float32)
    y_part = y_part.reshape(per_pair * length, head_cols)
    total, square = lax.psum((jnp.sum(y_part, axis=1), jnp.sum(y_part * y_part, axis=1)), "mp")
    full_cols = head_cols * mp_size
    mean_y = total[:, None] / full_cols
    var_y = square[:, None] / full_cols - mean_y * mean_y
    normed = (y_part - mean_y) * lax.rsqrt(var_y + epsilon) * out_gain
    mixed = (normed * upart.astype(jnp.float32)).astype(jnp.bfloat16)
    out_cols = width // mp_size
    term = jnp.dot(mixed, out_full, preferred_element_type=jnp.float32)
    summed = lax.psum_scatter(term, "mp", scatter_dimension=1, tiled=True)
    residual = lax.dynamic_slice_in_dim(xf, mp_pos * out_cols, out_cols, 1)
    return (summed + residual).astype(jnp.bfloat16).reshape(per_pair, length, out_cols)


def solution(mesh):
    return jax.shard_map(
        body,
        mesh=mesh,
        in_specs=(
            P("table", None),
            P("table"),
            P("parts", None),
            P(("parts", "table")),
            P("parts"),
            P(("parts", "table"), None),
            P(None, "table"),
            P(),
            P(None, "table", "mp"),
            P("mp"),
            P("mp", "table"),
            P("mp", None),
            P("mp", None),
        ),
        out_specs=P(("parts", "table", "bal"), None, "mp"),
        check_vma=False,
    )
```

profile of v0, /device:TPU:0, one launch (start us, length us, event | category | flops | bytes accessed | tf_op | source)
XLA Modules:
  0.0 1319.0 jit_solution(12878451426969050760)
XLA Ops:
  6.5 0.9 eq.60
  7.8 1.4 gather_fusion.7
  9.2 1.2 reduce-window.14
  11.0 0.7 and_reduce_fusion
  11.8 0.7 multiply_reduce_fusion.2
  12.6 8.0 scatter_custom_fusion
  20.7 4.0 gather_fusion
  24.7 6.2 gather_fusion.1
  30.8 1.3 fusion.10
  32.1 6.3 all-to-all-start
  39.3 1.2 reduce-window.16
  41.0 36.8 %all-to-all-done = bf16[4,256,512]{2,1,0:T(8,128)(2,1)S(1)} async-done(((bf16[4,256,512]{2,1,0:T(8,128)(2,1)}), bf16[4,256,512]{2,1,0:T(8,128)(2,1)S(1)}, u32[]{:S(2)}, u32[]{:S(2)}) %all-to-all-start) | async-done | bytes 1048608 | tf_op jit(solution)/shard_map/all_to_all | solution.py:76
  77.9 3.9 gather_fusion.2
  81.8 2.9 convolution_convert_fusion
  88.9 860.1 %gather_fusion.6 = f32[262144,4]{1,0:T(8,128)} fusion(f32[4,16]{0,1:T(8,128)S(1)} %copy.34, s32[262144]{0:T(1024)S(1)} %broadcast_clamp_fusion), kind=kCustom, calls=%fused_computation.6 | custom fusion | bytes 9437184 | tf_op jit(solution)/shard_map/jit(_take)/gather | solution.py:109
  949.0 74.3 %copy.36 = f32[4,256,256,4]{2,1,3,0:T(8,128)} copy(f32[4,256,256,4]{3,2,1,0:T(8,128)} %bitcast.17) | data formatting | bytes 8388608 | tf_op jit(solution)/shard_map/jit(_take)/gather | solution.py:109
  1023.6 215.5 %gather_fusion.4 = f32[65536,4]{1,0:T(8,128)} fusion(f32[4,32]{0,1:T(8,128)S(1)} %copy.32, s32[65536]{0:T(1024)S(1)} %broadcast_clamp_fusion.1), kind=kCustom, calls=%fused_computation.4 | custom fusion | bytes 2359296 | tf_op jit(solution)/shard_map/gather | solution.py:110
  1239.1 19.6 %copy.33 = f32[256,256,4]{1,0,2:T(8,128)} copy(f32[256,256,4]{2,1,0:T(8,128)} %bitcast.135) | data formatting | bytes 2097152 | tf_op jit(solution)/shard_map/gather | solution.py:110
  1258.7 1.3 fusion.26
  1260.1 2.1 convert_reduce_fusion
  1262.2 2.3 multiply_reduce_fusion
  1264.5 2.5 bitcast_convert_fusion
  1267.1 8.7 fusion.3
  1275.8 2.0 copy-done.5
  1278.0 1.1 reshape_squeeze.11
  1279.2 1.1 reshape_squeeze.10
  1280.8 6.9 fusion.76
  1287.6 2.0 copy.38
  1289.7 2.5 all-reduce
  1292.2 4.8 fusion.14
  1297.1 11.8 reduce-scatter.2.cloned.1.call-done
  1308.9 3.5 add_convert_fusion
  (94 shorter events, 7.5 us)
Async XLA Ops:
  6.5 14.1 %copy-start = (bf16[2048,512]{1,0:T(8,128)(2,1)S(1)}, bf16[2048,512]{1,0:T(8,128)(2,1)}, u32[]{:S(2)}) copy-start(bf16[2048,512]{1,0:T(8,128)(2,1)} %param.13) | copy-start | bytes 6291460
  20.7 4.0 copy-start.2
  32.1 45.7 %all-to-all-start = ((bf16[4,256,512]{2,1,0:T(8,128)(2,1)}), bf16[4,256,512]{2,1,0:T(8,128)(2,1)S(1)}, u32[]{:S(2)}, u32[]{:S(2)}) async-start(bf16[4,256,512]{2,1,0:T(8,128)(2,1)} %fusion.10), calls=%async_computation | async-start | bytes 2097152 | tf_op jit(solution)/shard_map/all_to_all | solution.py:76
  38.5 43.4 %all-gather.5.cloned.1.call-start = ((), (), s32[]{:S(2)}) async-start(), calls=%async_computation.2 | async-start | bytes 1310720 | tf_op jit(solution)/shard_map/all_gather | solution.py:49
  39.2 1220.9 %all-gather.7.cloned.1.call-start = ((), (), s32[]{:S(2)}) async-start(), calls=%async_computation.3 | async-start | bytes 3145728 | tf_op jit(solution)/shard_map/all_gather | solution.py:85
  77.9 8.6 copy-start.3
  81.8 5.4 copy-start.9
  81.8 5.5 copy-start.7
  84.8 1182.3 %all-gather.9.cloned.1.call-start = ((), (), s32[]{:S(2)}) async-start(), calls=%async_computation.4 | async-start | bytes 5242880 | tf_op jit(solution)/shard_map/all_gather | solution.py:50
  85.5 1206.7 %all-gather.11.cloned.1.call-start = ((), (), s32[]{:S(2)}) async-start(), calls=%async_computation.5 | async-start | bytes 1310720 | tf_op jit(solution)/shard_map/all_gather | solution.py:51
  86.1 1222.8 %reduce-scatter.2.cloned.1.call-start = ((), (), s32[]{:S(2)}) async-start(), calls=%async_computation.6 | async-start | bytes 6291456 | tf_op jit(solution)/shard_map/reduce_scatter | solution.py:128
  949.0 74.3 %copy-start.10 = (f32[4,32]{1,0:T(4,128)S(1)}, f32[4,32]{1,0:T(4,128)}, u32[]{:S(2)}) copy-start(f32[4,32]{1,0:T(4,128)} %param.24) | copy-start | bytes 1540
  1260.1 4.4 copy-start.4
  1262.2 4.9 copy-start.11
  1275.8 2.0 copy-start.5
  1279.1 1.6 copy-start.6
  1287.6 4.6 copy-start.8
  1297.1 15.4 %copy-start.1 = (bf16[2048,512]{1,0:T(8,128)(2,1)S(1)}, bf16[2048,512]{1,0:T(8,128)(2,1)}, u32[]{:S(2)}) copy-start(bf16[2048,512]{1,0:T(8,128)(2,1)} %param.13) | copy-start | bytes 6291460
Sparse Core Ops, SparseCore 0:
  40.8 40.4 all-gather.4
  84.9 10.1 all-gather.6
  96.7 81.9 all-gather.8
  180.1 28.7 all-gather.10
  1297.2 11.6 reduce-scatter.1
where the time goes:
time: 1320 us
  local copies, waits for them, and re-layouts  1200 us (91%)
  waiting for transfers between devices  50.6 us (4%)
  matrix products  23.3 us (2%)
  other arithmetic  18.9 us (1%)
  between operations  13.6 us (1%)
    gather x2, local copies, waits for them, and re-layouts, body(): time_term = jnp.moveaxis(jnp.take(time_bias, diff, axis=1), 0, 1)  934 us
    gather x2, local copies, waits for them, and re-layouts, body(): scores = scores + pos_bias[:, bucket][None] + time_term  235 us
    all_to_all x1, waiting for transfers between devices, body(): lax.all_to_all(replies, 'table', split_axis=0, concat_axis=0, tiled=True)  36.8 us
  transfers between devices with their start and end apart: 6, of which 2 were waited for; matrix products, arithmetic and copies ran while one was open for 91% of the time, Pallas kernels for 0%

commit v1 on v0

v1 whole, which is shorter than its diff:
```python
import functools
import math

import jax
import jax.numpy as jnp
from jax import lax
from jax.experimental import pallas as pl
from jax.experimental.pallas import tpu as pltpu
from jax.sharding import PartitionSpec as P

epsilon = 1e-05
BF = jnp.bfloat16
F32 = jnp.float32
VMEM_BYTES = 56 * 1024 * 1024
FAR = -1e30


def buckets_of(length, buckets):
    found = []
    for d in range(length):
        b = d if d < 16 else 15 + sum(1 for power in range(4, 20) if d >= 2**power)
        found.append(min(b, buckets - 1))
    return found


def vspec():
    return pl.BlockSpec(memory_space=pltpu.VMEM)


def sspec():
    return pl.BlockSpec(memory_space=pltpu.SMEM)


def params():
    return pltpu.CompilerParams(vmem_limit_bytes=VMEM_BYTES)


def iota(shape, axis):
    return lax.broadcasted_iota(jnp.int32, shape, axis)


def dot(a, b):
    return jnp.dot(a, b, preferred_element_type=F32)


def dot_nt(a, b):
    return lax.dot_general(a, b, (((1,), (1,)), ((), ())), preferred_element_type=F32)


class Sizes:
    def __init__(self, mesh_sizes, table_rows, hist_ids, lengths, pos_bias):
        self.n, self.bal, self.mp = mesh_sizes
        self.rows, self.width = table_rows.shape
        self.users, self.length = hist_ids.shape
        self.group = lengths.shape[0]
        self.pair = self.group // self.bal
        self.mine = self.pair // self.mp
        self.half = self.length // self.mp
        self.tokens = self.pair * self.half
        self.cap = self.pair * self.length // self.n
        self.heads = pos_bias.shape[0] * self.mp
        self.shift = self.rows.bit_length() - 1


def member(z, plan_ref, dest, slot):
    found = jnp.int32(0)
    for j in range(z.group):
        found = found + jnp.where(plan_ref[dest * z.group + j] == slot, j, 0)
    return found


def slot_of(z, mp_pos, s):
    if s < z.mine:
        return mp_pos * z.mine + s
    return (1 - mp_pos) * z.mine + (s - z.mine)


def token_ids(z, plan_ref, hist_ref, dest, bal_pos, mp_pos):
    parts = []
    for s in range(z.pair):
        slot = bal_pos * z.pair + slot_of(z, mp_pos, s)
        user = dest * z.group + member(z, plan_ref, dest, slot)
        row = hist_ref[pl.ds(user, 1), :]
        parts.append(jnp.where(mp_pos == 0, row[:, : z.half], row[:, z.half :]))
    return jnp.concatenate(parts, axis=1)


def scaled_rows(z, table_ref, scale_ref, rows_ref):
    chunk = 128

    def step(i, carry):
        start = pl.multiple_of(i * chunk, chunk)
        row = scale_ref[pl.ds(i, 1), :]
        column = jnp.broadcast_to(row, (chunk, chunk)).T
        for c in range(z.width // chunk):
            cols = slice(c * chunk, (c + 1) * chunk)
            rows_ref[pl.ds(start, chunk), cols] = (
                table_ref[pl.ds(start, chunk), cols].astype(F32) * column
            ).astype(BF)
        return carry

    lax.fori_loop(0, z.rows // chunk, step, 0)


def two_digits(values):
    row = iota((8, values.shape[1]), 0)
    high = lax.shift_right_logical(values, 7)
    low = values & 127
    return jnp.where(row == 0, high, jnp.where(row == 1, low, 0)).astype(F32).astype(BF)


def column_of(pairs):
    return (pairs[:, 0:1] * 128.0 + pairs[:, 1:2]).astype(jnp.int32)


def triangle(tokens):
    return (iota((tokens, tokens), 0) <= iota((tokens, tokens), 1)).astype(F32).astype(BF)


def send_kernel(z, plan_ref, hist_ref, table_ref, scale_ref, *refs):
    outs, rows_ref = refs[:-1], refs[-1]
    table_pos = lax.axis_index("table")
    bal_pos = lax.axis_index("bal")
    mp_pos = lax.axis_index("mp")
    scaled_rows(z, table_ref, scale_ref, rows_ref)
    tri = triangle(z.tokens)
    for k in range(1, z.n):
        dest = lax.rem(table_pos + k, z.n)
        ids = token_ids(z, plan_ref, hist_ref, dest, bal_pos, mp_pos)
        mine = lax.shift_right_logical(ids, z.shift) == table_pos
        flags = jnp.broadcast_to(mine.astype(F32), (8, z.tokens)).astype(BF)
        rank = dot(flags, tri)[0:1, :].astype(jnp.int32) - 1
        place = jnp.where(mine, rank, -1)
        compact = (iota((z.cap, z.tokens), 0) == place).astype(F32).astype(BF)
        local = column_of(dot_nt(compact, two_digits(ids & (z.rows - 1))))
        pick = (iota((z.cap, z.rows), 1) == local).astype(F32).astype(BF)
        outs[k - 1][...] = dot(pick, rows_ref[...]).astype(BF)


def keep_kernel(z, plan_ref, hist_ref, table_ref, scale_ref, own_ref, route_ref, rows_ref):
    table_pos = lax.axis_index("table")
    bal_pos = lax.axis_index("bal")
    mp_pos = lax.axis_index("mp")
    scaled_rows(z, table_ref, scale_ref, rows_ref)
    tri = triangle(z.tokens)
    ids = token_ids(z, plan_ref, hist_ref, table_pos, bal_pos, mp_pos)
    owner = lax.shift_right_logical(ids, z.shift)
    local = ids & (z.rows - 1)
    eye = (iota((z.tokens, z.tokens), 0) == iota((z.tokens, z.tokens), 1)).astype(F32).astype(BF)
    local_col = column_of(dot_nt(eye, two_digits(jnp.where(owner == table_pos, local, z.rows))))
    pick = (iota((z.tokens, z.rows), 1) == local_col).astype(F32).astype(BF)
    own_ref[...] = dot(pick, rows_ref[...]).astype(BF)
    lanes = max(8, z.n)
    offset = iota((lanes, z.tokens), 0)
    source = table_pos - offset
    source = jnp.where(source < 0, source + z.n, source)
    flags = (owner == source) & (offset >= 1) & (offset < z.n)
    rank = dot(flags.astype(F32).astype(BF), tri).astype(jnp.int32) - 1
    slots = z.n * z.cap
    slot = jnp.sum(
        jnp.where(flags, (offset - 1) * z.cap + rank + 1, 0), axis=0, keepdims=True
    )
    slot = jnp.where(slot == 0, slots, slot - 1)
    slot_col = column_of(dot_nt(eye, two_digits(slot)))
    route_ref[...] = (
        (iota((z.tokens, (z.n - 1) * z.cap), 1) == slot_col).astype(F32).astype(BF)
    )


def place_kernel(z, own_ref, route_ref, *refs):
    got, keep_ref, give_ref = refs[: z.n - 1], refs[-2], refs[-1]
    total = own_ref[...].astype(F32)
    block = max(1, 256 // z.cap)
    for k in range(0, z.n - 1, block):
        group = range(k, min(k + block, z.n - 1))
        rows = [got[g][...] for g in group]
        rows = rows[0] if len(rows) == 1 else jnp.concatenate(rows, axis=0)
        total = total + dot(route_ref[:, k * z.cap : k * z.cap + rows.shape[0]], rows)
    total = total.astype(BF)
    cut = z.tokens // z.mp
    keep_ref[...] = total[:cut]
    give_ref[...] = total[cut:]


def bias_kernel(z, small_ref, plan_ref, lens_ref, time_ref, bias_ref, *, buckets, tbuckets):
    table_pos = lax.axis_index("table")
    bal_pos = lax.axis_index("bal")
    mp_pos = lax.axis_index("mp")
    size = z.length
    number = buckets_of(size, buckets)
    lane = iota((8, size), 1)
    dist = jnp.where(lane == 0, 0, size - lane)
    position = []
    for h in range(z.heads):
        row = jnp.zeros((8, size), F32)
        for b in sorted(set(number)):
            low, high = number.index(b), size - 1 - number[::-1].index(b)
            row = jnp.where((dist >= low) & (dist <= high), small_ref[h, b], row)
        full = jnp.broadcast_to(row[0:1], (size, size))
        position.append(pltpu.roll(full, 0, 1, stride=1, stride_axis=0))
    for h in range(z.heads):
        for u in range(z.mine):
            bias_ref[u, h] = position[h]
    block = 32
    for u in range(z.mine):
        user = member(z, plan_ref, table_pos, bal_pos * z.pair + mp_pos * z.mine + u)
        size_u = lens_ref[user]
        events = time_ref[pl.ds(user, 1), :]
        columns = jnp.broadcast_to(events, (size, size)).T

        for r in range(0, size, block):
            rows = slice(r, r + block)
            diff = jnp.abs(columns[rows] - events)
            column = iota((block, size), 1)
            valid = (column <= iota((block, size), 0) + r) & (column < size_u)
            for h in range(z.heads):
                term = jnp.zeros((block, size), F32)
                for b in range(tbuckets):
                    term = jnp.where(diff == b, small_ref[h, buckets + b], term)
                bias_ref[u, h, rows, :] = jnp.where(valid, bias_ref[u, h, rows, :] + term, FAR)


def silu(s):
    half = 0.5 * s
    return half + half * jnp.tanh(half)


def layer_kernel(
    z, load, n_weights, plan_ref, lens_ref, keep_ref, got_ref, gain_ref, out_gain_ref, bias_ref, *refs
):
    weights = refs[:n_weights]
    own_out, give_out = refs[n_weights : n_weights + 2]
    (e_ref, w_ref, o_ref, emb_ref, x_ref, xn_ref, act_ref, y_ref, z_ref, sems) = refs[n_weights + 2 :]
    table_pos = lax.axis_index("table")
    bal_pos = lax.axis_index("bal")
    mp_pos = lax.axis_index("mp")
    width = x_ref.shape[1]
    copies = load(weights, e_ref, w_ref, o_ref, sems)
    for group in copies:
        for c in group:
            c.start()
    for u in range(z.mine):
        near = pl.multiple_of(u * z.length + mp_pos * z.half, z.half)
        far = pl.multiple_of(u * z.length + (1 - mp_pos) * z.half, z.half)
        rows = slice(u * z.half, (u + 1) * z.half)
        emb_ref[pl.ds(near, z.half), :] = keep_ref[rows, :]
        emb_ref[pl.ds(far, z.half), :] = got_ref[rows, :]
    for c in copies[0]:
        c.wait()
    tokens = z.mine * z.length
    block = 256
    for r in range(0, tokens, block):
        rows = slice(r, r + block)
        x = dot(emb_ref[rows, :], e_ref[...]).astype(BF)
        x_ref[rows, :] = x
        x = x.astype(F32)
        mean = jnp.mean(x, axis=1, keepdims=True)
        centred = x - mean
        var = jnp.mean(centred * centred, axis=1, keepdims=True)
        xn_ref[rows, :] = (centred * lax.rsqrt(var + epsilon) * gain_ref[...]).astype(BF)
    for c in copies[1]:
        c.wait()
    step = 256

    def project(i, carry):
        c, nb = i // (width // step), i % (width // step)
        cols = pl.ds(pl.multiple_of(nb * step, step), step)
        s = dot(xn_ref[...], w_ref[c, :, cols])
        act_ref[c, :, cols] = silu(s).astype(BF)
        return carry

    lax.fori_loop(0, 4 * (width // step), project, 0, unroll=2)
    scale = 1.0 / math.sqrt(width // z.heads)
    size = width // z.heads
    for u in range(z.mine):
        user = member(z, plan_ref, table_pos, bal_pos * z.pair + mp_pos * z.mine + u)
        inverse = 1.0 / jnp.full((1, z.length), lens_ref[user], jnp.int32).astype(F32)
        rows = slice(u * z.length, (u + 1) * z.length)

        def attend(h, carry):
            total, square = carry
            cols = pl.ds(pl.multiple_of(h * size, size), size)
            s = dot_nt(act_ref[2, rows, cols], act_ref[3, rows, cols]) * scale + bias_ref[u, h]
            a = (silu(s) * inverse).astype(BF)
            y = dot(a, act_ref[1, rows, cols])
            y_ref[rows, cols] = y
            return (
                total + jnp.sum(y, axis=1, keepdims=True),
                square + jnp.sum(y * y, axis=1, keepdims=True),
            )

        zero = jnp.zeros((z.length, 1), F32)
        total, square = lax.fori_loop(0, z.heads, attend, (zero, zero), unroll=4)
        mean = total / width
        var = square / width - mean * mean
        factor = lax.rsqrt(var + epsilon)
        for h in range(z.heads):
            cols = slice(h * size, (h + 1) * size)
            normed = (y_ref[rows, cols] - mean) * factor * out_gain_ref[h : h + 1, :]
            z_ref[rows, cols] = (normed * act_ref[0, rows, cols].astype(F32)).astype(BF)
    for c in copies[2]:
        c.wait()
    out_cols = width // z.mp
    for which, ref in ((1 - mp_pos, give_out), (mp_pos, own_out)):
        for nb in range(out_cols // step):
            cols = pl.ds(pl.multiple_of(which * out_cols + nb * step, step), step)
            term = dot(z_ref[...], o_ref[:, cols])
            ref[:, nb * step : (nb + 1) * step] = (
                term + x_ref[:, cols].astype(F32)
            ).astype(BF)


def swap(x, axis, size, k=1):
    return lax.ppermute(x, axis, [(i, (i + k) % size) for i in range(size)])


Q_ROWS, CUT = 256, 192


def quarter_pack(z, embed_proj, qkvu_proj, out_proj):
    width = embed_proj.shape[0]
    q = lax.axis_index("parts") * z.bal + lax.axis_index("bal")
    m = lax.axis_index("mp")
    four, deep, cols = qkvu_proj.shape
    share = deep // 4
    qk = lax.dynamic_slice_in_dim(qkvu_proj, q * share, share, 1).reshape(four * share, cols)
    e_rows = width // 8
    e = lax.dynamic_slice_in_dim(embed_proj, (q * 2 + m) * e_rows, e_rows, 0)
    e = jnp.concatenate([e[: e_rows // 2], e[e_rows // 2 :]], axis=1)
    o_rows = out_proj.shape[0] // 4
    o = lax.dynamic_slice_in_dim(out_proj, q * o_rows, o_rows, 0)
    o = jnp.concatenate([o[: o_rows // 2], o[o_rows // 2 :]], axis=1)
    return jnp.concatenate([qk, e, o], axis=0)


def gather_weights(z, embed_proj, qkvu_proj, out_proj):
    pack = quarter_pack(z, embed_proj, qkvu_proj, out_proj)
    remote = [pack]
    for _ in range(z.n - 1):
        remote.append(swap(remote[-1], "table", z.n))
    pieces = [embed_proj, qkvu_proj, out_proj]
    pieces += [swap(qkvu_proj, "mp", 2), swap(out_proj, "mp", 2)]
    for r in remote[1:]:
        x = swap(r, "bal", 2)
        y = swap(r, "parts", 2)
        dx = swap(y[:CUT], "bal", 2)
        dy = swap(x[CUT:], "parts", 2)
        for piece in (r, x, y, dx, dy):
            pieces += [piece, swap(piece, "mp", 2)]
    return pieces


def load_pieces(z):
    def load(refs, e_ref, w_ref, o_ref, sems):
        t, m = lax.axis_index("table"), lax.axis_index("mp")
        parts_pos, bal_pos = lax.axis_index("parts"), lax.axis_index("bal")
        e_own, w_own, o_own, w_near, o_near = refs[:5]
        deep, cols = w_own.shape[1], w_own.shape[2]
        e_cols = e_own.shape[1]
        o_rows = o_own.shape[0]
        groups = [[], [], []]

        def add(g, src, dst):
            groups[g].append(pltpu.make_async_copy(src, dst, sems.at[g]))

        def at(x, size):
            return pl.ds(pl.multiple_of(x, size), size)

        add(0, e_own, e_ref.at[:, at(t * e_cols, e_cols)])
        for core, w, o in ((m, w_own, o_own), (1 - m, w_near, o_near)):
            add(1, w, w_ref.at[:, at(t * deep, deep), at(core * cols, cols)])
            add(2, o, o_ref.at[at(core * o_rows, o_rows), at(t * e_cols, e_cols)])
        share = deep // 4
        e_part = e_ref.shape[0] // 16
        o_part = o_rows // 8
        rest = refs[5:]
        for k in range(1, z.n):
            source = lax.rem(t + z.n - k, z.n)
            block = rest[(k - 1) * 10 : k * 10]
            for i, (dp, db) in enumerate(((0, 0), (0, 1), (1, 0), (1, 1), (1, 1))):
                pp = parts_pos if dp == 0 else 1 - parts_pos
                bb = bal_pos if db == 0 else 1 - bal_pos
                q = pp * 2 + bb
                low = CUT if i == 4 else 0
                high = CUT if i == 3 else 4 * share + e_part + o_part
                for core, ref in ((m, block[2 * i]), (1 - m, block[2 * i + 1])):
                    for c in range(4):
                        if low <= c * share < high:
                            add(
                                1,
                                ref.at[c * share - low : (c + 1) * share - low, :],
                                w_ref.at[c, at(source * deep + q * share, share), at(core * cols, cols)],
                            )
                    if high <= 4 * share:
                        continue
                    first = 4 * share - low
                    for j in range(2):
                        lanes = slice(j * e_cols, (j + 1) * e_cols)
                        add(
                            0,
                            ref.at[first : first + e_part, lanes],
                            e_ref.at[at(((q * 2 + core) * 2 + j) * e_part, e_part), at(source * e_cols, e_cols)],
                        )
                        add(
                            2,
                            ref.at[first + e_part : first + e_part + o_part, lanes],
                            o_ref.at[
                                at(core * o_rows + (q * 2 + j) * o_part, o_part), at(source * e_cols, e_cols)
                            ],
                        )
        return groups

    return load


def load_whole(refs, e_ref, w_ref, o_ref, sems):
    return [
        [pltpu.make_async_copy(src, dst, sems.at[i])]
        for i, (src, dst) in enumerate(zip(refs, (e_ref, w_ref, o_ref)))
    ]


def body(
    table_rows,
    row_scale,
    hist_ids,
    lengths,
    plan,
    time_bucket,
    embed_proj,
    in_gain,
    qkvu_proj,
    out_gain,
    out_proj,
    pos_bias,
    time_bias,
):
    axes = tuple(lax.axis_size(a) for a in ("table", "bal", "mp"))
    z = Sizes(axes, table_rows, hist_ids, lengths, pos_bias)
    width = in_gain.shape[0]
    mp_pos = lax.axis_index("mp")
    scale = row_scale.reshape(z.rows // 128, 128)
    sent = pl.pallas_call(
        functools.partial(send_kernel, z),
        out_shape=[jax.ShapeDtypeStruct((z.cap, z.width), BF)] * (z.n - 1),
        in_specs=[sspec(), vspec(), vspec(), vspec()],
        out_specs=[vspec()] * (z.n - 1),
        scratch_shapes=[pltpu.VMEM((z.rows, z.width), BF)],
        compiler_params=params(),
        name="send_rows",
    )(plan, hist_ids, table_rows, scale)
    got = [swap(s, "table", z.n, k + 1) for k, s in enumerate(sent)]
    own, route = pl.pallas_call(
        functools.partial(keep_kernel, z),
        out_shape=[
            jax.ShapeDtypeStruct((z.tokens, z.width), BF),
            jax.ShapeDtypeStruct((z.tokens, (z.n - 1) * z.cap), BF),
        ],
        in_specs=[sspec(), vspec(), vspec(), vspec()],
        out_specs=[vspec()] * 2,
        scratch_shapes=[pltpu.VMEM((z.rows, z.width), BF)],
        compiler_params=params(),
        name="keep_rows",
    )(plan, hist_ids, table_rows, scale)

    small = jnp.concatenate([pos_bias, time_bias, out_gain.reshape(pos_bias.shape[0], -1)], axis=1)
    other = swap(small, "mp", z.mp)
    small = jnp.where(
        mp_pos == 0, jnp.concatenate([small, other], 0), jnp.concatenate([other, small], 0)
    )
    buckets, tbuckets = pos_bias.shape[1], time_bias.shape[1]
    bias = pl.pallas_call(
        functools.partial(bias_kernel, z, buckets=buckets, tbuckets=tbuckets),
        out_shape=jax.ShapeDtypeStruct((z.mine, z.heads, z.length, z.length), F32),
        in_specs=[sspec(), sspec(), sspec(), vspec()],
        out_specs=vspec(),
        compiler_params=params(),
        name="bias",
    )(small[:, : buckets + tbuckets], plan, lengths, time_bucket)
    gains = small[:, buckets + tbuckets :]

    if z.n == 4 and z.bal == 2 and lax.axis_size("parts") == 2:
        weights = gather_weights(z, embed_proj, qkvu_proj, out_proj)
        load = load_pieces(z)
    else:
        q_full = lax.all_gather(qkvu_proj, "table", axis=1, tiled=True)
        o_full = lax.all_gather(out_proj, "table", axis=1, tiled=True)
        weights = [
            lax.all_gather(embed_proj, "table", axis=1, tiled=True),
            lax.all_gather(q_full, "mp", axis=2, tiled=True),
            lax.all_gather(o_full, "mp", axis=0, tiled=True),
        ]
        load = load_whole

    keep, give = pl.pallas_call(
        functools.partial(place_kernel, z),
        out_shape=[jax.ShapeDtypeStruct((z.tokens // z.mp, z.width), BF)] * 2,
        in_specs=[vspec()] * (z.n + 1),
        out_specs=[vspec()] * 2,
        compiler_params=params(),
        name="place_rows",
    )(own, route, *got)
    back = swap(give, "mp", z.mp)

    tokens = z.mine * z.length
    out_cols = width // z.mp
    out_own, out_give = pl.pallas_call(
        functools.partial(layer_kernel, z, load, len(weights)),
        out_shape=[jax.ShapeDtypeStruct((tokens, out_cols), BF)] * 2,
        in_specs=[sspec(), sspec()] + [vspec()] * 5 + [pl.BlockSpec(memory_space=pl.ANY)] * len(weights),
        out_specs=[vspec()] * 2,
        scratch_shapes=[
            pltpu.VMEM((z.width, width), BF),
            pltpu.VMEM((4, width, width), BF),
            pltpu.VMEM((width, width), BF),
            pltpu.VMEM((tokens, z.width), BF),
            pltpu.VMEM((tokens, width), BF),
            pltpu.VMEM((tokens, width), BF),
            pltpu.VMEM((4, tokens, width), BF),
            pltpu.VMEM((tokens, width), F32),
            pltpu.VMEM((tokens, width), BF),
            pltpu.SemaphoreType.DMA((3,)),
        ],
        compiler_params=params(),
        name="layer",
    )(plan, lengths, keep, back, in_gain.reshape(1, width), gains, bias, *weights)
    out_got = swap(out_give, "mp", z.mp)
    out = jnp.where(
        mp_pos == 0,
        jnp.concatenate([out_own, out_got], 0),
        jnp.concatenate([out_got, out_own], 0),
    )
    return out.reshape(z.pair, z.length, out_cols)


def solution(mesh):
    return jax.shard_map(
        body,
        mesh=mesh,
        in_specs=(
            P("table", None),
            P("table"),
            P("parts", None),
            P(("parts", "table")),
            P("parts"),
            P(("parts", "table"), None),
            P(None, "table"),
            P(),
            P(None, "table", "mp"),
            P("mp"),
            P("mp", "table"),
            P("mp", None),
            P("mp", None),
        ),
        out_specs=P(("parts", "table", "bal"), None, "mp"),
        check_vma=False,
    )
```

time: 1320 us -> 126 us (0.10)
  local copies, waits for them, and re-layouts: 1200 us -> 4.71 us
  Pallas kernels: 0 us -> 42.3 us
  starting transfers between devices: 6.48 us -> 32.9 us
  matrix products: 23.3 us -> 0 us
  other arithmetic: 18.9 us -> 2.72 us
    gather x13 -> x0, local copies, waits for them, and re-layouts: 1190 us -> none  [the longest x2 934 us: body(): time_term = jnp.moveaxis(jnp.take(time_bias, diff, axis=1), 0, 1)]
    pallas_call x0 -> x5, Pallas kernels: none -> 42.3 us  [the longest x1 18.7 us: body(): pl.pallas_call(functools.partial(layer_kernel, z, load, len(weights)), ou...]
    ppermute x0 -> x38, waiting for transfers between devices: none -> 42.1 us  [swap(): return lax.ppermute(x, axis, [(i, (i + k) % size) for i in range(size)])]
    all_to_all x1 -> x0, waiting for transfers between devices: 36.8 us -> none  [body(): lax.all_to_all(replies, 'table', split_axis=0, concat_axis=0, tiled=True)]
    ppermute x0 -> x38, starting transfers between devices: none -> 32.9 us  [swap(): return lax.ppermute(x, axis, [(i, (i + k) % size) for i in range(size)])]
    dot_general x4 -> x0, matrix products: 23.3 us -> none  [the longest x1 8.72 us: body(): jnp.einsum('td,cde->cte', xn, qkvu_full, preferred_element_type=jnp.float32)]
  transfers between devices with their start and end apart: 6 -> 38, of which waited for: 2 -> 13; matrix products, arithmetic and copies ran while one was open for 91% -> 1% of each run, Pallas kernels for 0% -> 19%
where the time goes in v1:
time: 126 us; the launch traced here: 125 us
  Pallas kernels  42.3 us (34%)
  waiting for transfers between devices  42.1 us (33%)
  starting transfers between devices  32.9 us (26%)
  local copies, waits for them, and re-layouts  4.71 us (4%)
  other arithmetic  2.72 us (2%)
    ppermute x38, waiting for transfers between devices, swap(): return lax.ppermute(x, axis, [(i, (i + k) % size) for i in range(size)])  42.1 us
    ppermute x38, starting transfers between devices, swap(): return lax.ppermute(x, axis, [(i, (i + k) % size) for i in range(size)])  32.9 us
    pallas_call x1, Pallas kernels, body(): pl.pallas_call(functools.partial(layer_kernel, z, load, len(weights)), ou...  18.7 us
    pallas_call x1, Pallas kernels, body(): pl.pallas_call(functools.partial(send_kernel, z), out_shape=[jax.ShapeDty...  7.29 us
    pallas_call x1, Pallas kernels, body(): pl.pallas_call(functools.partial(bias_kernel, z, buckets=buckets, tbucket...  7.01 us
    pallas_call x1, Pallas kernels, body(): pl.pallas_call(functools.partial(keep_kernel, z), out_shape=[jax.ShapeDty...  6.48 us
    pallas_call x1, Pallas kernels, body(): pl.pallas_call(functools.partial(place_kernel, z), out_shape=[jax.ShapeDt...  2.81 us
    select_n x1, other arithmetic, body(): jnp.where(mp_pos == 0, jnp.concatenate([out_own, out_got], 0), jnp.concat...  2.54 us
  transfers between devices with their start and end apart: 38, of which 13 were waited for; matrix products, arithmetic and copies ran while one was open for 1% of the time, Pallas kernels for 19%

profile of v1, /device:TPU:0, one launch (start us, length us, event | category | flops | bytes accessed | tf_op | source)
XLA Modules:
  0.0 125.3 jit_solution(17420574563917548648)
XLA Ops:
  2.7 3.1 %collective-permute-start.7 = (bf16[352,512]{1,0:T(8,128)(2,1)S(1)}, bf16[352,512]{1,0:T(8,128)(2,1)S(1)}, u32[]{:S(2)}, u32[]{:S(2)}) collective-permute-start(bf16[352,512]{1,0:T(8,128)(2,1)S(1)} %maximum_maximum_fusion), channel_id=1, source_target_pairs={{0,4},{4,8},{8,12},{12,0},{1,5},{5,9},{9,13},{13,1},{2,6},{6,10},{... | collective-permute-start | bytes 1081352 | tf_op jit(solution)/shard_map/ppermute | solution.py:314
  5.7 7.3 %send_rows.1 = (bf16[256,512]{1,0:T(8,128)(2,1)}, bf16[256,512]{1,0:T(8,128)(2,1)}, bf16[256,512]{1,0:T(8,128)(2,1)}) custom-call(s32[32]{0:T(128)} %plan_ref.7, s32[32,256]{1,0:T(8,128)} %hist_ref.3, bf16[2048,512]{1,0:T(8,128)(2,1)} %table_ref.3, f32[16,128]{1,0:T(8,128)} %bitcast.6), custom_call_target="tpu_custom_call" | custom-call | tf_op jit(solution)/shard_map/send_rows/pallas_call | solution.py:443
  13.0 1.6 %collective-permute-start = (bf16[256,512]{1,0:T(8,128)(2,1)}, bf16[256,512]{1,0:T(8,128)(2,1)S(1)}, u32[]{:S(2)}, u32[]{:S(2)}) collective-permute-start(bf16[256,512]{1,0:T(8,128)(2,1)} %get-tuple-element.16), channel_id=1, source_target_pairs={{0,4},{4,8},{8,12},{12,0},{1,5},{5,9},{9,13},{13,1},{2,6},{6,10},{... | collective-permute-start | bytes 786440 | tf_op jit(solution)/shard_map/ppermute | solution.py:314
  16.0 1.3 %collective-permute-done.4 = f32[4,176]{1,0:T(4,128)S(1)} collective-permute-done((f32[4,176]{1,0:T(4,128)S(1)}, f32[4,176]{1,0:T(4,128)S(1)}, u32[]{:S(2)}, u32[]{:S(2)}) %collective-permute-start.4) | collective-permute-done | bytes 2848 | tf_op jit(solution)/shard_map/ppermute | solution.py:314
  17.3 2.5 %collective-permute-start.2 = (bf16[256,512]{1,0:T(8,128)(2,1)}, bf16[256,512]{1,0:T(8,128)(2,1)S(1)}, u32[]{:S(2)}, u32[]{:S(2)}) collective-permute-start(bf16[256,512]{1,0:T(8,128)(2,1)} %get-tuple-element.18), channel_id=1, source_target_pairs={{0,12},{4,0},{8,4},{12,8},{1,13},{5,1},{9,5},{13,9},{2,14},{6,2},{... | collective-permute-start | bytes 786440 | tf_op jit(solution)/shard_map/ppermute | solution.py:314
  19.8 4.6 %collective-permute-done.refs_0_ = bf16[256,512]{1,0:T(8,128)(2,1)S(1)} collective-permute-done((bf16[256,512]{1,0:T(8,128)(2,1)}, bf16[256,512]{1,0:T(8,128)(2,1)S(1)}, u32[]{:S(2)}, u32[]{:S(2)}) %collective-permute-start) | collective-permute-done | bytes 262176 | tf_op jit(solution)/shard_map/ppermute | solution.py:314
  24.4 1.6 %collective-permute-start.9 = (bf16[352,512]{1,0:T(8,128)(2,1)S(1)}, bf16[352,512]{1,0:T(8,128)(2,1)S(1)}, u32[]{:S(2)}, u32[]{:S(2)}) collective-permute-start(bf16[352,512]{1,0:T(8,128)(2,1)S(1)} %collective-permute-done.7.refs_5_), channel_id=1, source_target_pairs={{0,2},{2,0},{1,3},{3,1},{4,6},{6,4},{5,7},{7,5},{8,10},{10,8},{9,1... | collective-permute-start | bytes 1081352 | tf_op jit(solution)/shard_map/ppermute | solution.py:314
  26.0 8.1 %collective-permute-done.1.refs_1_ = bf16[256,512]{1,0:T(8,128)(2,1)S(1)} collective-permute-done((bf16[256,512]{1,0:T(8,128)(2,1)}, bf16[256,512]{1,0:T(8,128)(2,1)S(1)}, u32[]{:S(2)}, u32[]{:S(2)}) %collective-permute-start.1) | collective-permute-done | bytes 262176 | tf_op jit(solution)/shard_map/ppermute | solution.py:314
  34.1 1.5 %collective-permute-start.11 = (bf16[352,512]{1,0:T(8,128)(2,1)S(1)}, bf16[352,512]{1,0:T(8,128)(2,1)S(1)}, u32[]{:S(2)}, u32[]{:S(2)}) collective-permute-start(bf16[352,512]{1,0:T(8,128)(2,1)S(1)} %collective-permute-done.7.refs_5_), channel_id=1, source_target_pairs={{0,16},{16,0},{1,17},{17,1},{2,18},{18,2},{3,19},{19,3},{4,20},{20... | collective-permute-start | bytes 1081352 | tf_op jit(solution)/shard_map/ppermute | solution.py:314
  35.6 4.6 %collective-permute-start.17 = (bf16[352,512]{1,0:T(8,128)(2,1)S(1)}, bf16[352,512]{1,0:T(8,128)(2,1)S(1)}, u32[]{:S(2)}, u32[]{:S(2)}) collective-permute-start(bf16[352,512]{1,0:T(8,128)(2,1)S(1)} %collective-permute-done.7.refs_5_), channel_id=1, source_target_pairs={{0,4},{4,8},{8,12},{12,0},{1,5},{5,9},{9,13},{13,1},{2,6},{6,10},{... | collective-permute-start | bytes 1081352 | tf_op jit(solution)/shard_map/ppermute | solution.py:314
  40.2 6.5 %keep_rows.1 = (bf16[512,512]{1,0:T(8,128)(2,1)}, bf16[512,768]{1,0:T(8,128)(2,1)}) custom-call(s32[32]{0:T(128)} %plan_ref.7, s32[32,256]{1,0:T(8,128)} %hist_ref.3, bf16[2048,512]{1,0:T(8,128)(2,1)} %table_ref.3, f32[16,128]{1,0:T(8,128)} %bitcast.7), custom_call_target="tpu_custom_call" | custom-call | tf_op jit(solution)/shard_map/keep_rows/pallas_call | solution.py:453
  46.7 2.8 %place_rows.1 = (bf16[256,512]{1,0:T(8,128)(2,1)}, bf16[256,512]{1,0:T(8,128)(2,1)}) custom-call(bf16[512,512]{1,0:T(8,128)(2,1)} %get-tuple-element.14.own_ref, bf16[512,768]{1,0:T(8,128)(2,1)} %get-tuple-element.15.route_ref, bf16[256,512]{1,0:T(8,128)(2,1)} %copy-done.18, bf16[256,512]{1,0:T(8,128)(2,1)} %copy-done.19, bf16[256,512]{1,0:T(8,128)(2,1)} %copy-done.20), custom_call_target="tpu_custom_call" | custom-call | tf_op jit(solution)/shard_map/place_rows/pallas_call | solution.py:495
  50.2 1.6 %collective-permute-start.15 = (bf16[160,512]{1,0:T(8,128)(2,1)S(1)}, bf16[160,512]{1,0:T(8,128)(2,1)S(1)}, u32[]{:S(2)}, u32[]{:S(2)}) collective-permute-start(bf16[160,512]{1,0:T(8,128)(2,1)S(1)} %slice.51), channel_id=1, source_target_pairs={{0,16},{16,0},{1,17},{17,1},{2,18},{18,2},{3,19},{19,3},{4,20},{20... | collective-permute-start | bytes 491528 | tf_op jit(solution)/shard_map/ppermute | solution.py:314
  51.8 1.6 %collective-permute-start.13 = (bf16[192,512]{1,0:T(8,128)(2,1)S(1)}, bf16[192,512]{1,0:T(8,128)(2,1)S(1)}, u32[]{:S(2)}, u32[]{:S(2)}) collective-permute-start(bf16[192,512]{1,0:T(8,128)(2,1)S(1)} %slice.50), channel_id=1, source_target_pairs={{0,2},{2,0},{1,3},{3,1},{4,6},{6,4},{5,7},{7,5},{8,10},{10,8},{9,1... | collective-permute-start | bytes 589832 | tf_op jit(solution)/shard_map/ppermute | solution.py:314
  53.5 2.9 %collective-permute-done.15.refs_13_ = bf16[160,512]{1,0:T(8,128)(2,1)S(1)} collective-permute-done((bf16[160,512]{1,0:T(8,128)(2,1)S(1)}, bf16[160,512]{1,0:T(8,128)(2,1)S(1)}, u32[]{:S(2)}, u32[]{:S(2)}) %collective-permute-start.15) | collective-permute-done | bytes 163872 | tf_op jit(solution)/shard_map/ppermute | solution.py:314
  56.4 1.6 %collective-permute-start.21 = (bf16[352,512]{1,0:T(8,128)(2,1)S(1)}, bf16[352,512]{1,0:T(8,128)(2,1)S(1)}, u32[]{:S(2)}, u32[]{:S(2)}) collective-permute-start(bf16[352,512]{1,0:T(8,128)(2,1)S(1)} %collective-permute-done.17.refs_15_), channel_id=1, source_target_pairs={{0,16},{16,0},{1,17},{17,1},{2,18},{18,2},{3,19},{19,3},{4,20},{20... | collective-permute-start | bytes 1081352 | tf_op jit(solution)/shard_map/ppermute | solution.py:314
  58.5 1.5 %collective-permute-start.19 = (bf16[352,512]{1,0:T(8,128)(2,1)S(1)}, bf16[352,512]{1,0:T(8,128)(2,1)S(1)}, u32[]{:S(2)}, u32[]{:S(2)}) collective-permute-start(bf16[352,512]{1,0:T(8,128)(2,1)S(1)} %collective-permute-done.17.refs_15_), channel_id=1, source_target_pairs={{0,2},{2,0},{1,3},{3,1},{4,6},{6,4},{5,7},{7,5},{8,10},{10,8},{9,1... | collective-permute-start | bytes 1081352 | tf_op jit(solution)/shard_map/ppermute | solution.py:314
  60.5 4.4 %collective-permute-done.27.refs_25_ = bf16[352,512]{1,0:T(8,128)(2,1)S(1)} collective-permute-done((bf16[352,512]{1,0:T(8,128)(2,1)S(1)}, bf16[352,512]{1,0:T(8,128)(2,1)S(1)}, u32[]{:S(2)}, u32[]{:S(2)}) %collective-permute-start.27) | collective-permute-done | bytes 360480 | tf_op jit(solution)/shard_map/ppermute | solution.py:314
  65.0 2.3 %collective-permute-done.21.refs_19_ = bf16[352,512]{1,0:T(8,128)(2,1)S(1)} collective-permute-done((bf16[352,512]{1,0:T(8,128)(2,1)S(1)}, bf16[352,512]{1,0:T(8,128)(2,1)S(1)}, u32[]{:S(2)}, u32[]{:S(2)}) %collective-permute-start.21) | collective-permute-done | bytes 360480 | tf_op jit(solution)/shard_map/ppermute | solution.py:314
  67.3 1.2 collective-permute-done.19.refs_17_
  69.5 1.2 collective-permute-start.25
  70.7 1.6 %collective-permute-start.23 = (bf16[192,512]{1,0:T(8,128)(2,1)S(1)}, bf16[192,512]{1,0:T(8,128)(2,1)}, u32[]{:S(2)}, u32[]{:S(2)}) collective-permute-start(bf16[192,512]{1,0:T(8,128)(2,1)S(1)} %slice.52), channel_id=1, source_target_pairs={{0,2},{2,0},{1,3},{3,1},{4,6},{6,4},{5,7},{7,5},{8,10},{10,8},{9,1... | collective-permute-start | bytes 589832 | tf_op jit(solution)/shard_map/ppermute | solution.py:314
  73.0 8.6 %collective-permute-done.25.refs_23_ = bf16[160,512]{1,0:T(8,128)(2,1)S(1)} collective-permute-done((bf16[160,512]{1,0:T(8,128)(2,1)S(1)}, bf16[160,512]{1,0:T(8,128)(2,1)S(1)}, u32[]{:S(2)}, u32[]{:S(2)}) %collective-permute-start.25) | collective-permute-done | bytes 163872 | tf_op jit(solution)/shard_map/ppermute | solution.py:314
  82.2 1.8 %collective-permute-done.26.refs_24_ = bf16[160,512]{1,0:T(8,128)(2,1)S(1)} collective-permute-done((bf16[160,512]{1,0:T(8,128)(2,1)S(1)}, bf16[160,512]{1,0:T(8,128)(2,1)S(1)}, u32[]{:S(2)}, u32[]{:S(2)}) %collective-permute-start.26) | collective-permute-done | bytes 163872 | tf_op jit(solution)/shard_map/ppermute | solution.py:314
  84.0 1.5 %collective-permute-start.33 = (bf16[192,512]{1,0:T(8,128)(2,1)S(1)}, bf16[192,512]{1,0:T(8,128)(2,1)}, u32[]{:S(2)}, u32[]{:S(2)}) collective-permute-start(bf16[192,512]{1,0:T(8,128)(2,1)S(1)} %slice.54), channel_id=1, source_target_pairs={{0,2},{2,0},{1,3},{3,1},{4,6},{6,4},{5,7},{7,5},{8,10},{10,8},{9,1... | collective-permute-start | bytes 589832 | tf_op jit(solution)/shard_map/ppermute | solution.py:314
  86.1 1.6 %collective-permute-start.35 = (bf16[160,512]{1,0:T(8,128)(2,1)S(1)}, bf16[160,512]{1,0:T(8,128)(2,1)}, u32[]{:S(2)}, u32[]{:S(2)}) collective-permute-start(bf16[160,512]{1,0:T(8,128)(2,1)S(1)} %slice.55), channel_id=1, source_target_pairs={{0,16},{16,0},{1,17},{17,1},{2,18},{18,2},{3,19},{19,3},{4,20},{20... | collective-permute-start | bytes 491528 | tf_op jit(solution)/shard_map/ppermute | solution.py:314
  87.8 3.3 %collective-permute-done.33.refs_31_ = bf16[192,512]{1,0:T(8,128)(2,1)} collective-permute-done((bf16[192,512]{1,0:T(8,128)(2,1)S(1)}, bf16[192,512]{1,0:T(8,128)(2,1)}, u32[]{:S(2)}, u32[]{:S(2)}) %collective-permute-start.33) | collective-permute-done | bytes 196640 | tf_op jit(solution)/shard_map/ppermute | solution.py:314
  91.1 1.3 %collective-permute-done.35.refs_33_ = bf16[160,512]{1,0:T(8,128)(2,1)} collective-permute-done((bf16[160,512]{1,0:T(8,128)(2,1)S(1)}, bf16[160,512]{1,0:T(8,128)(2,1)}, u32[]{:S(2)}, u32[]{:S(2)}) %collective-permute-start.35) | collective-permute-done | bytes 163872 | tf_op jit(solution)/shard_map/ppermute | solution.py:314
  93.9 7.0 %bias.1.bias_ref = f32[2,8,256,256]{3,2,1,0:T(8,128)} custom-call(f32[8,48]{1,0:T(8,128)} %slice.49.small_ref, s32[32]{0:T(128)} %plan_ref.7, s32[8]{0:T(128)} %lens_ref.3, s32[8,256]{1,0:T(8,128)} %time_ref.1), custom_call_target="tpu_custom_call" | custom-call | tf_op jit(solution)/shard_map/bias/pallas_call | solution.py:472
  101.7 18.7 %layer.1 = (bf16[512,512]{1,0:T(8,128)(2,1)}, bf16[512,512]{1,0:T(8,128)(2,1)}) custom-call(s32[32]{0:T(128)} %plan_ref.7, s32[8]{0:T(128)} %lens_ref.3, bf16[256,512]{1,0:T(8,128)(2,1)} %get-tuple-element.19.keep_ref, bf16[256,512]{1,0:T(8,128)(2,1)} %copy-done.22, f32[1,1024]{1,0:T(1,128)} %bitcast.10, f32[8,128]{1,0:T(8,128)} %slice.48.out_gain_ref, ...), custom_call_target="tpu_custom_call" | custom-call | tf_op jit(solution)/shard_map/layer/pallas_call | solution.py:507
  121.0 1.7 %collective-permute-done.37 = bf16[512,512]{1,0:T(8,128)(2,1)S(1)} collective-permute-done((bf16[512,512]{1,0:T(8,128)(2,1)}, bf16[512,512]{1,0:T(8,128)(2,1)S(1)}, u32[]{:S(2)}, u32[]{:S(2)}) %collective-permute-start.37) | collective-permute-done | bytes 524320 | tf_op jit(solution)/shard_map/ppermute | solution.py:314
  122.7 2.5 %maximum_select_fusion = bf16[1024,512]{1,0:T(8,128)(2,1)} fusion(bf16[512,512]{1,0:T(8,128)(2,1)S(1)} %collective-permute-done.37, bf16[512,512]{1,0:T(8,128)(2,1)} %get-tuple-element.21, pred[]{:T(512)S(6)} %eq.4), kind=kLoop, calls=%fused_computation | loop fusion | flops 4718592 | bytes 2097153 | tf_op jit(solution)/shard_map/jit(_where)/select_n | solution.py:528
  (128 shorter events, 11.4 us)
Async XLA Ops:
  2.7 21.7 %collective-permute-start.7 = (bf16[352,512]{1,0:T(8,128)(2,1)S(1)}, bf16[352,512]{1,0:T(8,128)(2,1)S(1)}, u32[]{:S(2)}, u32[]{:S(2)}) collective-permute-start(bf16[352,512]{1,0:T(8,128)(2,1)S(1)} %maximum_maximum_fusion), channel_id=1, source_target_pairs={{0,4},{4,8},{8,12},{12,0},{1,5},{5,9},{9,13},{13,1},{2,6},{6,10},{... | collective-permute-start | bytes 1081352 | tf_op jit(solution)/shard_map/ppermute | solution.py:314
  13.0 11.3 %collective-permute-start = (bf16[256,512]{1,0:T(8,128)(2,1)}, bf16[256,512]{1,0:T(8,128)(2,1)S(1)}, u32[]{:S(2)}, u32[]{:S(2)}) collective-permute-start(bf16[256,512]{1,0:T(8,128)(2,1)} %get-tuple-element.16), channel_id=1, source_target_pairs={{0,4},{4,8},{8,12},{12,0},{1,5},{5,9},{9,13},{13,1},{2,6},{6,10},{... | collective-permute-start | bytes 786440 | tf_op jit(solution)/shard_map/ppermute | solution.py:314
  14.6 45.4 %collective-permute-start.5 = (bf16[4,256,512]{2,1,0:T(8,128)(2,1)S(1)}, bf16[4,256,512]{2,1,0:T(8,128)(2,1)S(1)}, u32[]{:S(2)}, u32[]{:S(2)}) collective-permute-start(bf16[4,256,512]{2,1,0:T(8,128)(2,1)S(1)} %copy-done), channel_id=1, source_target_pairs={{0,1},{1,0},{2,3},{3,2},{4,5},{5,4},{6,7},{7,6},{8,9},{9,8},{10,11... | collective-permute-start | bytes 3145736 | tf_op jit(solution)/shard_map/ppermute | solution.py:314
  14.6 19.5 %collective-permute-start.1 = (bf16[256,512]{1,0:T(8,128)(2,1)}, bf16[256,512]{1,0:T(8,128)(2,1)S(1)}, u32[]{:S(2)}, u32[]{:S(2)}) collective-permute-start(bf16[256,512]{1,0:T(8,128)(2,1)} %get-tuple-element.17), channel_id=1, source_target_pairs={{0,8},{4,12},{8,0},{12,4},{1,9},{5,13},{9,1},{13,5},{2,10},{6,14},... | collective-permute-start | bytes 786440 | tf_op jit(solution)/shard_map/ppermute | solution.py:314
  17.3 18.3 %collective-permute-start.2 = (bf16[256,512]{1,0:T(8,128)(2,1)}, bf16[256,512]{1,0:T(8,128)(2,1)S(1)}, u32[]{:S(2)}, u32[]{:S(2)}) collective-permute-start(bf16[256,512]{1,0:T(8,128)(2,1)} %get-tuple-element.18), channel_id=1, source_target_pairs={{0,12},{4,0},{8,4},{12,8},{1,13},{5,1},{9,5},{13,9},{2,14},{6,2},{... | collective-permute-start | bytes 786440 | tf_op jit(solution)/shard_map/ppermute | solution.py:314
  24.4 25.1 %collective-permute-start.6 = (bf16[512,256]{1,0:T(8,128)(2,1)S(1)}, bf16[512,256]{1,0:T(8,128)(2,1)S(1)}, u32[]{:S(2)}, u32[]{:S(2)}) collective-permute-start(bf16[512,256]{1,0:T(8,128)(2,1)S(1)} %copy-done.8), channel_id=1, source_target_pairs={{0,1},{1,0},{2,3},{3,2},{4,5},{5,4},{6,7},{7,6},{8,9},{9,8},{10,11... | collective-permute-start | bytes 786440 | tf_op jit(solution)/shard_map/ppermute | solution.py:314
  24.4 25.2 %collective-permute-start.9 = (bf16[352,512]{1,0:T(8,128)(2,1)S(1)}, bf16[352,512]{1,0:T(8,128)(2,1)S(1)}, u32[]{:S(2)}, u32[]{:S(2)}) collective-permute-start(bf16[352,512]{1,0:T(8,128)(2,1)S(1)} %collective-permute-done.7.refs_5_), channel_id=1, source_target_pairs={{0,2},{2,0},{1,3},{3,1},{4,6},{6,4},{5,7},{7,5},{8,10},{10,8},{9,1... | collective-permute-start | bytes 1081352 | tf_op jit(solution)/shard_map/ppermute | solution.py:314
  34.1 16.1 %collective-permute-start.11 = (bf16[352,512]{1,0:T(8,128)(2,1)S(1)}, bf16[352,512]{1,0:T(8,128)(2,1)S(1)}, u32[]{:S(2)}, u32[]{:S(2)}) collective-permute-start(bf16[352,512]{1,0:T(8,128)(2,1)S(1)} %collective-permute-done.7.refs_5_), channel_id=1, source_target_pairs={{0,16},{16,0},{1,17},{17,1},{2,18},{18,2},{3,19},{19,3},{4,20},{20... | collective-permute-start | bytes 1081352 | tf_op jit(solution)/shard_map/ppermute | solution.py:314
  35.6 17.8 %collective-permute-start.17 = (bf16[352,512]{1,0:T(8,128)(2,1)S(1)}, bf16[352,512]{1,0:T(8,128)(2,1)S(1)}, u32[]{:S(2)}, u32[]{:S(2)}) collective-permute-start(bf16[352,512]{1,0:T(8,128)(2,1)S(1)} %collective-permute-done.7.refs_5_), channel_id=1, source_target_pairs={{0,4},{4,8},{8,12},{12,0},{1,5},{5,9},{9,13},{13,1},{2,6},{6,10},{... | collective-permute-start | bytes 1081352 | tf_op jit(solution)/shard_map/ppermute | solution.py:314
  49.6 6.8 %collective-permute-start.8 = (bf16[352,512]{1,0:T(8,128)(2,1)S(1)}, bf16[352,512]{1,0:T(8,128)(2,1)}, u32[]{:S(2)}, u32[]{:S(2)}) collective-permute-start(bf16[352,512]{1,0:T(8,128)(2,1)S(1)} %collective-permute-done.7.refs_5_), channel_id=1, source_target_pairs={{0,1},{1,0},{2,3},{3,2},{4,5},{5,4},{6,7},{7,6},{8,9},{9,8},{10,11... | collective-permute-start | bytes 1081352 | tf_op jit(solution)/shard_map/ppermute | solution.py:314
  50.2 6.2 %collective-permute-start.15 = (bf16[160,512]{1,0:T(8,128)(2,1)S(1)}, bf16[160,512]{1,0:T(8,128)(2,1)S(1)}, u32[]{:S(2)}, u32[]{:S(2)}) collective-permute-start(bf16[160,512]{1,0:T(8,128)(2,1)S(1)} %slice.51), channel_id=1, source_target_pairs={{0,16},{16,0},{1,17},{17,1},{2,18},{18,2},{3,19},{19,3},{4,20},{20... | collective-permute-start | bytes 491528 | tf_op jit(solution)/shard_map/ppermute | solution.py:314
  51.8 6.6 %collective-permute-start.13 = (bf16[192,512]{1,0:T(8,128)(2,1)S(1)}, bf16[192,512]{1,0:T(8,128)(2,1)S(1)}, u32[]{:S(2)}, u32[]{:S(2)}) collective-permute-start(bf16[192,512]{1,0:T(8,128)(2,1)S(1)} %slice.50), channel_id=1, source_target_pairs={{0,2},{2,0},{1,3},{3,1},{4,6},{6,4},{5,7},{7,5},{8,10},{10,8},{9,1... | collective-permute-start | bytes 589832 | tf_op jit(solution)/shard_map/ppermute | solution.py:314
  53.4 11.6 %collective-permute-start.27 = (bf16[352,512]{1,0:T(8,128)(2,1)S(1)}, bf16[352,512]{1,0:T(8,128)(2,1)S(1)}, u32[]{:S(2)}, u32[]{:S(2)}) collective-permute-start(bf16[352,512]{1,0:T(8,128)(2,1)S(1)} %collective-permute-done.17.refs_15_), channel_id=1, source_target_pairs={{0,4},{4,8},{8,12},{12,0},{1,5},{5,9},{9,13},{13,1},{2,6},{6,10},{... | collective-permute-start | bytes 1081352 | tf_op jit(solution)/shard_map/ppermute | solution.py:314
  56.4 10.8 %collective-permute-start.21 = (bf16[352,512]{1,0:T(8,128)(2,1)S(1)}, bf16[352,512]{1,0:T(8,128)(2,1)S(1)}, u32[]{:S(2)}, u32[]{:S(2)}) collective-permute-start(bf16[352,512]{1,0:T(8,128)(2,1)S(1)} %collective-permute-done.17.refs_15_), channel_id=1, source_target_pairs={{0,16},{16,0},{1,17},{17,1},{2,18},{18,2},{3,19},{19,3},{4,20},{20... | collective-permute-start | bytes 1081352 | tf_op jit(solution)/shard_map/ppermute | solution.py:314
  58.5 10.1 %collective-permute-start.19 = (bf16[352,512]{1,0:T(8,128)(2,1)S(1)}, bf16[352,512]{1,0:T(8,128)(2,1)S(1)}, u32[]{:S(2)}, u32[]{:S(2)}) collective-permute-start(bf16[352,512]{1,0:T(8,128)(2,1)S(1)} %collective-permute-done.17.refs_15_), channel_id=1, source_target_pairs={{0,2},{2,0},{1,3},{3,1},{4,6},{6,4},{5,7},{7,5},{8,10},{10,8},{9,1... | collective-permute-start | bytes 1081352 | tf_op jit(solution)/shard_map/ppermute | solution.py:314
  59.9 9.5 %collective-permute-start.18 = (bf16[352,512]{1,0:T(8,128)(2,1)S(1)}, bf16[352,512]{1,0:T(8,128)(2,1)S(1)}, u32[]{:S(2)}, u32[]{:S(2)}) collective-permute-start(bf16[352,512]{1,0:T(8,128)(2,1)S(1)} %collective-permute-done.17.refs_15_), channel_id=1, source_target_pairs={{0,1},{1,0},{2,3},{3,2},{4,5},{5,4},{6,7},{7,6},{8,9},{9,8},{10,11... | collective-permute-start | bytes 1081352 | tf_op jit(solution)/shard_map/ppermute | solution.py:314
  60.0 10.6 %collective-permute-start.12 = (bf16[352,512]{1,0:T(8,128)(2,1)S(1)}, bf16[352,512]{1,0:T(8,128)(2,1)S(1)}, u32[]{:S(2)}, u32[]{:S(2)}) collective-permute-start(bf16[352,512]{1,0:T(8,128)(2,1)S(1)} %collective-permute-done.11.refs_9_), channel_id=1, source_target_pairs={{0,1},{1,0},{2,3},{3,2},{4,5},{5,4},{6,7},{7,6},{8,9},{9,8},{10,11... | collective-permute-start | bytes 1081352 | tf_op jit(solution)/shard_map/ppermute | solution.py:314
  65.0 7.3 %collective-permute-start.10 = (bf16[352,512]{1,0:T(8,128)(2,1)S(1)}, bf16[352,512]{1,0:T(8,128)(2,1)S(1)}, u32[]{:S(2)}, u32[]{:S(2)}) collective-permute-start(bf16[352,512]{1,0:T(8,128)(2,1)S(1)} %collective-permute-done.9.refs_7_), channel_id=1, source_target_pairs={{0,1},{1,0},{2,3},{3,2},{4,5},{5,4},{6,7},{7,6},{8,9},{9,8},{10,11... | collective-permute-start | bytes 1081352 | tf_op jit(solution)/shard_map/ppermute | solution.py:314
  67.3 5.7 %collective-permute-start.14 = (bf16[192,512]{1,0:T(8,128)(2,1)S(1)}, bf16[192,512]{1,0:T(8,128)(2,1)}, u32[]{:S(2)}, u32[]{:S(2)}) collective-permute-start(bf16[192,512]{1,0:T(8,128)(2,1)S(1)} %collective-permute-done.13.refs_11_), channel_id=1, source_target_pairs={{0,1},{1,0},{2,3},{3,2},{4,5},{5,4},{6,7},{7,6},{8,9},{9,8},{10,11... | collective-permute-start | bytes 589832 | tf_op jit(solution)/shard_map/ppermute | solution.py:314
  68.5 13.6 %collective-permute-start.31 = (bf16[352,512]{1,0:T(8,128)(2,1)S(1)}, bf16[352,512]{1,0:T(8,128)(2,1)S(1)}, u32[]{:S(2)}, u32[]{:S(2)}) collective-permute-start(bf16[352,512]{1,0:T(8,128)(2,1)S(1)} %collective-permute-done.27.refs_25_), channel_id=1, source_target_pairs={{0,16},{16,0},{1,17},{17,1},{2,18},{18,2},{3,19},{19,3},{4,20},{20... | collective-permute-start | bytes 1081352 | tf_op jit(solution)/shard_map/ppermute | solution.py:314
  69.5 12.1 %collective-permute-start.25 = (bf16[160,512]{1,0:T(8,128)(2,1)S(1)}, bf16[160,512]{1,0:T(8,128)(2,1)S(1)}, u32[]{:S(2)}, u32[]{:S(2)}) collective-permute-start(bf16[160,512]{1,0:T(8,128)(2,1)S(1)} %slice.53), channel_id=1, source_target_pairs={{0,16},{16,0},{1,17},{17,1},{2,18},{18,2},{3,19},{19,3},{4,20},{20... | collective-permute-start | bytes 491528 | tf_op jit(solution)/shard_map/ppermute | solution.py:314
  70.7 10.9 %collective-permute-start.23 = (bf16[192,512]{1,0:T(8,128)(2,1)S(1)}, bf16[192,512]{1,0:T(8,128)(2,1)}, u32[]{:S(2)}, u32[]{:S(2)}) collective-permute-start(bf16[192,512]{1,0:T(8,128)(2,1)S(1)} %slice.52), channel_id=1, source_target_pairs={{0,2},{2,0},{1,3},{3,1},{4,6},{6,4},{5,7},{7,5},{8,10},{10,8},{9,1... | collective-permute-start | bytes 589832 | tf_op jit(solution)/shard_map/ppermute | solution.py:314
  72.2 13.3 %collective-permute-start.29 = (bf16[352,512]{1,0:T(8,128)(2,1)S(1)}, bf16[352,512]{1,0:T(8,128)(2,1)S(1)}, u32[]{:S(2)}, u32[]{:S(2)}) collective-permute-start(bf16[352,512]{1,0:T(8,128)(2,1)S(1)} %collective-permute-done.27.refs_25_), channel_id=1, source_target_pairs={{0,2},{2,0},{1,3},{3,1},{4,6},{6,4},{5,7},{7,5},{8,10},{10,8},{9,1... | collective-permute-start | bytes 1081352 | tf_op jit(solution)/shard_map/ppermute | solution.py:314
  72.9 12.6 %collective-permute-start.28 = (bf16[352,512]{1,0:T(8,128)(2,1)S(1)}, bf16[352,512]{1,0:T(8,128)(2,1)S(1)}, u32[]{:S(2)}, u32[]{:S(2)}) collective-permute-start(bf16[352,512]{1,0:T(8,128)(2,1)S(1)} %collective-permute-done.27.refs_25_), channel_id=1, source_target_pairs={{0,1},{1,0},{2,3},{3,2},{4,5},{5,4},{6,7},{7,6},{8,9},{9,8},{10,11... | collective-permute-start | bytes 1081352 | tf_op jit(solution)/shard_map/ppermute | solution.py:314
  81.6 6.1 %collective-permute-start.20 = (bf16[352,512]{1,0:T(8,128)(2,1)S(1)}, bf16[352,512]{1,0:T(8,128)(2,1)S(1)}, u32[]{:S(2)}, u32[]{:S(2)}) collective-permute-start(bf16[352,512]{1,0:T(8,128)(2,1)S(1)} %collective-permute-done.19.refs_17_), channel_id=1, source_target_pairs={{0,1},{1,0},{2,3},{3,2},{4,5},{5,4},{6,7},{7,6},{8,9},{9,8},{10,11... | collective-permute-start | bytes 1081352 | tf_op jit(solution)/shard_map/ppermute | solution.py:314
  84.0 7.0 %collective-permute-start.33 = (bf16[192,512]{1,0:T(8,128)(2,1)S(1)}, bf16[192,512]{1,0:T(8,128)(2,1)}, u32[]{:S(2)}, u32[]{:S(2)}) collective-permute-start(bf16[192,512]{1,0:T(8,128)(2,1)S(1)} %slice.54), channel_id=1, source_target_pairs={{0,2},{2,0},{1,3},{3,1},{4,6},{6,4},{5,7},{7,5},{8,10},{10,8},{9,1... | collective-permute-start | bytes 589832 | tf_op jit(solution)/shard_map/ppermute | solution.py:314
  85.5 15.4 %collective-permute-start.32 = (bf16[352,512]{1,0:T(8,128)(2,1)S(1)}, bf16[352,512]{1,0:T(8,128)(2,1)}, u32[]{:S(2)}, u32[]{:S(2)}) collective-permute-start(bf16[352,512]{1,0:T(8,128)(2,1)S(1)} %collective-permute-done.31.refs_29_), channel_id=1, source_target_pairs={{0,1},{1,0},{2,3},{3,2},{4,5},{5,4},{6,7},{7,6},{8,9},{9,8},{10,11... | collective-permute-start | bytes 1081352 | tf_op jit(solution)/shard_map/ppermute | solution.py:314
  85.6 15.4 %collective-permute-start.30 = (bf16[352,512]{1,0:T(8,128)(2,1)S(1)}, bf16[352,512]{1,0:T(8,128)(2,1)}, u32[]{:S(2)}, u32[]{:S(2)}) collective-permute-start(bf16[352,512]{1,0:T(8,128)(2,1)S(1)} %collective-permute-done.29.refs_27_), channel_id=1, source_target_pairs={{0,1},{1,0},{2,3},{3,2},{4,5},{5,4},{6,7},{7,6},{8,9},{9,8},{10,11... | collective-permute-start | bytes 1081352 | tf_op jit(solution)/shard_map/ppermute | solution.py:314
  86.1 6.4 %collective-permute-start.35 = (bf16[160,512]{1,0:T(8,128)(2,1)S(1)}, bf16[160,512]{1,0:T(8,128)(2,1)}, u32[]{:S(2)}, u32[]{:S(2)}) collective-permute-start(bf16[160,512]{1,0:T(8,128)(2,1)S(1)} %slice.55), channel_id=1, source_target_pairs={{0,16},{16,0},{1,17},{17,1},{2,18},{18,2},{3,19},{19,3},{4,20},{20... | collective-permute-start | bytes 491528 | tf_op jit(solution)/shard_map/ppermute | solution.py:314
  87.7 13.3 %collective-permute-start.24 = (bf16[192,512]{1,0:T(8,128)(2,1)}, bf16[192,512]{1,0:T(8,128)(2,1)}, u32[]{:S(2)}, u32[]{:S(2)}) collective-permute-start(bf16[192,512]{1,0:T(8,128)(2,1)} %collective-permute-done.23.refs_21_), channel_id=1, source_target_pairs={{0,1},{1,0},{2,3},{3,2},{4,5},{5,4},{6,7},{7,6},{8,9},{9,8},{10,11... | collective-permute-start | bytes 589832 | tf_op jit(solution)/shard_map/ppermute | solution.py:314
  91.1 9.9 %collective-permute-start.34 = (bf16[192,512]{1,0:T(8,128)(2,1)}, bf16[192,512]{1,0:T(8,128)(2,1)S(1)}, u32[]{:S(2)}, u32[]{:S(2)}) collective-permute-start(bf16[192,512]{1,0:T(8,128)(2,1)} %collective-permute-done.33.refs_31_), channel_id=1, source_target_pairs={{0,1},{1,0},{2,3},{3,2},{4,5},{5,4},{6,7},{7,6},{8,9},{9,8},{10,11... | collective-permute-start | bytes 589832 | tf_op jit(solution)/shard_map/ppermute | solution.py:314
  92.5 8.5 %collective-permute-start.36 = (bf16[160,512]{1,0:T(8,128)(2,1)}, bf16[160,512]{1,0:T(8,128)(2,1)}, u32[]{:S(2)}, u32[]{:S(2)}) collective-permute-start(bf16[160,512]{1,0:T(8,128)(2,1)} %collective-permute-done.35.refs_33_), channel_id=1, source_target_pairs={{0,1},{1,0},{2,3},{3,2},{4,5},{5,4},{6,7},{7,6},{8,9},{9,8},{10,11... | collective-permute-start | bytes 491528 | tf_op jit(solution)/shard_map/ppermute | solution.py:314
  (38 other events, 600.5 us)

commit v2 on v1

--- a/solution.py
+++ b/solution.py
@@ -45,6 +45,14 @@
 
 def dot_nt(a, b):
     return lax.dot_general(a, b, (((1,), (1,)), ((), ())), preferred_element_type=F32)
+
+
+def cost(us):
+    return pl.CostEstimate(flops=int(us * 9e8), bytes_accessed=int(us * 2e6), transcendentals=0)
+
+
+def fence(*values):
+    return lax.optimization_barrier(values)
 
 
 class Sizes:
@@ -331,23 +339,6 @@
     o = lax.dynamic_slice_in_dim(out_proj, q * o_rows, o_rows, 0)
     o = jnp.concatenate([o[: o_rows // 2], o[o_rows // 2 :]], axis=1)
     return jnp.concatenate([qk, e, o], axis=0)
-
-
-def gather_weights(z, embed_proj, qkvu_proj, out_proj):
-    pack = quarter_pack(z, embed_proj, qkvu_proj, out_proj)
-    remote = [pack]
-    for _ in range(z.n - 1):
-        remote.append(swap(remote[-1], "table", z.n))
-    pieces = [embed_proj, qkvu_proj, out_proj]
-    pieces += [swap(qkvu_proj, "mp", 2), swap(out_proj, "mp", 2)]
-    for r in remote[1:]:
-        x = swap(r, "bal", 2)
-        y = swap(r, "parts", 2)
-        dx = swap(y[:CUT], "bal", 2)
-        dy = swap(x[CUT:], "parts", 2)
-        for piece in (r, x, y, dx, dy):
-            pieces += [piece, swap(piece, "mp", 2)]
-    return pieces
 
 
 def load_pieces(z):
@@ -440,17 +431,17 @@
     width = in_gain.shape[0]
     mp_pos = lax.axis_index("mp")
     scale = row_scale.reshape(z.rows // 128, 128)
-    sent = pl.pallas_call(
+    send_rows = pl.pallas_call(
         functools.partial(send_kernel, z),
         out_shape=[jax.ShapeDtypeStruct((z.cap, z.width), BF)] * (z.n - 1),
         in_specs=[sspec(), vspec(), vspec(), vspec()],
         out_specs=[vspec()] * (z.n - 1),
         scratch_shapes=[pltpu.VMEM((z.rows, z.width), BF)],
         compiler_params=params(),
+        cost_estimate=cost(7),
         name="send_rows",
-    )(plan, hist_ids, table_rows, scale)
-    got = [swap(s, "table", z.n, k + 1) for k, s in enumerate(sent)]
-    own, route = pl.pallas_call(
+    )
+    keep_rows = pl.pallas_call(
         functools.partial(keep_kernel, z),
         out_shape=[
             jax.ShapeDtypeStruct((z.tokens, z.width), BF),
@@ -460,29 +451,97 @@
         out_specs=[vspec()] * 2,
         scratch_shapes=[pltpu.VMEM((z.rows, z.width), BF)],
         compiler_params=params(),
+        cost_estimate=cost(7),
         name="keep_rows",
-    )(plan, hist_ids, table_rows, scale)
-
-    small = jnp.concatenate([pos_bias, time_bias, out_gain.reshape(pos_bias.shape[0], -1)], axis=1)
-    other = swap(small, "mp", z.mp)
-    small = jnp.where(
-        mp_pos == 0, jnp.concatenate([small, other], 0), jnp.concatenate([other, small], 0)
     )
     buckets, tbuckets = pos_bias.shape[1], time_bias.shape[1]
-    bias = pl.pallas_call(
+    make_bias = pl.pallas_call(
         functools.partial(bias_kernel, z, buckets=buckets, tbuckets=tbuckets),
         out_shape=jax.ShapeDtypeStruct((z.mine, z.heads, z.length, z.length), F32),
         in_specs=[sspec(), sspec(), sspec(), vspec()],
         out_specs=vspec(),
         compiler_params=params(),
+        cost_estimate=cost(7),
         name="bias",
-    )(small[:, : buckets + tbuckets], plan, lengths, time_bucket)
-    gains = small[:, buckets + tbuckets :]
+    )
+    place_rows = pl.pallas_call(
+        functools.partial(place_kernel, z),
+        out_shape=[jax.ShapeDtypeStruct((z.tokens // z.mp, z.width), BF)] * 2,
+        in_specs=[vspec()] * (z.n + 1),
+        out_specs=[vspec()] * 2,
+        compiler_params=params(),
+        cost_estimate=cost(3),
+        name="place_rows",
+    )
+
+    def both(x):
+        other = swap(x, "mp", z.mp)
+        return jnp.where(
+            mp_pos == 0, jnp.concatenate([x, other], 0), jnp.concatenate([other, x], 0)
+        )
+
+    def biases():
+        small = jnp.concatenate(
+            [pos_bias, time_bias, out_gain.reshape(pos_bias.shape[0], -1)], axis=1
+        )
+        small = both(small)
+        return small[:, : buckets + tbuckets], small[:, buckets + tbuckets :]
 
     if z.n == 4 and z.bal == 2 and lax.axis_size("parts") == 2:
-        weights = gather_weights(z, embed_proj, qkvu_proj, out_proj)
+        pack = quarter_pack(z, embed_proj, qkvu_proj, out_proj)
+        near = functools.partial(swap, axis="mp", size=2)
+        hop = functools.partial(swap, axis="table", size=z.n)
+
+        def first(r):
+            return swap(r, "bal", 2), swap(r, "parts", 2)
+
+        def second(x, y):
+            return swap(y[:CUT], "bal", 2), swap(x[CUT:], "parts", 2)
+
+        table, gains = biases()
+        r1 = hop(pack)
+        sent = send_rows(plan, hist_ids, table_rows, scale)
+        w_near, o_near = near(qkvu_proj), near(out_proj)
+        r1, sent, w_near, o_near, table, gains, plan1 = fence(
+            r1, sent, w_near, o_near, table, gains, plan
+        )
+        r2 = hop(r1)
+        x1, y1 = first(r1)
+        r1n = near(r1)
+        bias = make_bias(table, plan1, lengths, time_bucket)
+        r1, r2, x1, y1, r1n, bias, sent, plan2 = fence(r1, r2, x1, y1, r1n, bias, sent, plan1)
+        r3 = hop(r2)
+        got2 = swap(sent[1], "table", z.n, 2)
+        x2, y2 = first(r2)
+        dx1, dy1 = second(x1, y1)
+        r2n, x1n, y1n = near(r2), near(x1), near(y1)
+        own, route = keep_rows(plan2, hist_ids, table_rows, scale)
+        r2, r3, got2, x2, y2, dx1, dy1, r2n, x1n, y1n, own, route, sent = fence(
+            r2, r3, got2, x2, y2, dx1, dy1, r2n, x1n, y1n, own, route, sent
+        )
+        got1 = swap(sent[0], "table", z.n, 1)
+        got3 = swap(sent[2], "table", z.n, 3)
+        x3, y3 = first(r3)
+        dx2, dy2 = second(x2, y2)
+        r3n, x2n, y2n, dx1n, dy1n = [near(v) for v in (r3, x2, y2, dx1, dy1)]
+        r3, got1, got3, x3, y3, dx2, dy2, r3n, x2n, y2n, dx1n, dy1n = fence(
+            r3, got1, got3, x3, y3, dx2, dy2, r3n, x2n, y2n, dx1n, dy1n
+        )
+        dx3, dy3 = second(x3, y3)
+        keep, give = place_rows(own, route, got1, got2, got3)
+        back = near(give)
+        x3n, y3n, dx2n, dy2n = [near(v) for v in (x3, y3, dx2, dy2)]
+        weights = [embed_proj, qkvu_proj, out_proj, w_near, o_near]
+        weights += [r1, r1n, x1, x1n, y1, y1n, dx1, dx1n, dy1, dy1n]
+        weights += [r2, r2n, x2, x2n, y2, y2n, dx2, dx2n, dy2, dy2n]
+        weights += [r3, r3n, x3, x3n, y3, y3n, dx3, near(dx3), dy3, near(dy3)]
         load = load_pieces(z)
     else:
+        table, gains = biases()
+        bias = make_bias(table, plan, lengths, time_bucket)
+        sent = send_rows(plan, hist_ids, table_rows, scale)
+        got = [swap(s, "table", z.n, k + 1) for k, s in enumerate(sent)]
+        own, route = keep_rows(plan, hist_ids, table_rows, scale)
         q_full = lax.all_gather(qkvu_proj, "table", axis=1, tiled=True)
         o_full = lax.all_gather(out_proj, "table", axis=1, tiled=True)
         weights = [
@@ -491,16 +550,8 @@
             lax.all_gather(o_full, "mp", axis=0, tiled=True),
         ]
         load = load_whole
-
-    keep, give = pl.pallas_call(
-        functools.partial(place_kernel, z),
-        out_shape=[jax.ShapeDtypeStruct((z.tokens // z.mp, z.width), BF)] * 2,
-        in_specs=[vspec()] * (z.n + 1),
-        out_specs=[vspec()] * 2,
-        compiler_params=params(),
-        name="place_rows",
-    )(own, route, *got)
-    back = swap(give, "mp", z.mp)
+        keep, give = place_rows(own, route, *got)
+        back = swap(give, "mp", z.mp)
 
     tokens = z.mine * z.length
     out_cols = width // z.mp

time: 126 us -> 117 us (0.929)
  starting transfers between devices: 32.9 us -> 24.1 us
  waiting for transfers between devices: 42.1 us -> 40.8 us
    ppermute x38, starting transfers between devices: 32.9 us -> 24.1 us  [swap(): return lax.ppermute(x, axis, [(i, (i + k) % size) for i in range(size)])]
    ppermute x38, waiting for transfers between devices: 42.1 us -> 40.8 us  [swap(): return lax.ppermute(x, axis, [(i, (i + k) % size) for i in range(size)])]
  transfers between devices with their start and end apart: 38 -> 38, of which waited for: 13 -> 20; matrix products, arithmetic and copies ran while one was open for 1% -> 3% of each run, Pallas kernels for 19% -> 21%
where the time goes in v2:
time: 117 us; the launch traced here: 116 us
  Pallas kernels  42.6 us (36%)
  waiting for transfers between devices  40.8 us (35%)
  starting transfers between devices  24.1 us (21%)
  local copies, waits for them, and re-layouts  4.89 us (4%)
  other arithmetic  3.45 us (3%)
    ppermute x38, waiting for transfers between devices, swap(): return lax.ppermute(x, axis, [(i, (i + k) % size) for i in range(size)])  40.8 us
    ppermute x38, starting transfers between devices, swap(): return lax.ppermute(x, axis, [(i, (i + k) % size) for i in range(size)])  24.1 us
    pallas_call x1, Pallas kernels, body(): pl.pallas_call(functools.partial(layer_kernel, z, load, len(weights)), ou...  18.7 us
    pallas_call x1, Pallas kernels, body(): sent = send_rows(plan, hist_ids, table_rows, scale)  7.34 us
    pallas_call x1, Pallas kernels, body(): bias = make_bias(table, plan1, lengths, time_bucket)  7.05 us
    pallas_call x1, Pallas kernels, body(): own, route = keep_rows(plan2, hist_ids, table_rows, scale)  6.62 us
    pallas_call x1, Pallas kernels, body(): keep, give = place_rows(own, route, got1, got2, got3)  2.88 us
    select_n x1, other arithmetic, body(): jnp.where(mp_pos == 0, jnp.concatenate([out_own, out_got], 0), jnp.concat...  2.56 us
  transfers between devices with their start and end apart: 38, of which 20 were waited for; matrix products, arithmetic and copies ran while one was open for 3% of the time, Pallas kernels for 21%

profile of v2, /device:TPU:0, one launch (start us, length us, event | category | flops | bytes accessed | tf_op | source)
XLA Modules:
  0.0 116.3 jit_solution(17883013638398759156)
XLA Ops:
  0.0 0.8 pad_maximum_fusion
  1.8 0.8 constant_dynamic-slice_fusion
  3.3 1.0 constant_dynamic-slice_fusion.4
  4.3 2.7 %collective-permute-start = (bf16[352,512]{1,0:T(8,128)(2,1)S(1)}, bf16[352,512]{1,0:T(8,128)(2,1)S(1)}, u32[]{:S(2)}, u32[]{:S(2)}) collective-permute-start(bf16[352,512]{1,0:T(8,128)(2,1)S(1)} %maximum_maximum_fusion), channel_id=1, source_target_pairs={{0,4},{4,8},{8,12},{12,0},{1,5},{5,9},{9,13},{13,1},{2,6},{6,10},{... | collective-permute-start | bytes 1081352 | tf_op jit(solution)/shard_map/ppermute | solution.py:322
  7.0 7.3 %send_rows.1 = (bf16[256,512]{1,0:T(8,128)(2,1)}, bf16[256,512]{1,0:T(8,128)(2,1)}, bf16[256,512]{1,0:T(8,128)(2,1)}) custom-call(s32[32]{0:T(128)} %plan_ref.5, s32[32,256]{1,0:T(8,128)} %hist_ref.3, bf16[2048,512]{1,0:T(8,128)(2,1)} %table_ref.3, f32[16,128]{1,0:T(8,128)} %bitcast.9), custom_call_target="tpu_custom_call" | custom-call | flops 6300000256 | bytes 14000000 | tf_op jit(solution)/shard_map/send_rows/pallas_call | solution.py:503
  15.7 2.3 %collective-permute-done.refs_5_ = bf16[352,512]{1,0:T(8,128)(2,1)S(1)} collective-permute-done((bf16[352,512]{1,0:T(8,128)(2,1)S(1)}, bf16[352,512]{1,0:T(8,128)(2,1)S(1)}, u32[]{:S(2)}, u32[]{:S(2)}) %collective-permute-start) | collective-permute-done | bytes 360480 | tf_op jit(solution)/shard_map/ppermute | solution.py:322
  18.1 1.6 %collective-permute-start.6 = (bf16[352,512]{1,0:T(8,128)(2,1)S(1)}, bf16[352,512]{1,0:T(8,128)(2,1)S(1)}, u32[]{:S(2)}, u32[]{:S(2)}) collective-permute-start(bf16[352,512]{1,0:T(8,128)(2,1)S(1)} %collective-permute-done.refs_5_), channel_id=1, source_target_pairs={{0,16},{16,0},{1,17},{17,1},{2,18},{18,2},{3,19},{19,3},{4,20},{20... | collective-permute-start | bytes 1081352 | tf_op jit(solution)/shard_map/ppermute | solution.py:322
  19.7 1.5 %collective-permute-start.5 = (bf16[352,512]{1,0:T(8,128)(2,1)S(1)}, bf16[352,512]{1,0:T(8,128)(2,1)S(1)}, u32[]{:S(2)}, u32[]{:S(2)}) collective-permute-start(bf16[352,512]{1,0:T(8,128)(2,1)S(1)} %collective-permute-done.refs_5_), channel_id=1, source_target_pairs={{0,2},{2,0},{1,3},{3,1},{4,6},{6,4},{5,7},{7,5},{8,10},{10,8},{9,1... | collective-permute-start | bytes 1081352 | tf_op jit(solution)/shard_map/ppermute | solution.py:322
  21.2 7.0 %bias.1.bias_ref = f32[2,8,256,256]{3,2,1,0:T(8,128)} custom-call(f32[8,48]{1,0:T(8,128)} %slice.48.small_ref, s32[32]{0:T(128)} %plan_ref.5, s32[8]{0:T(128)} %lens_ref.3, s32[8,256]{1,0:T(8,128)} %time_ref.1), custom_call_target="tpu_custom_call" | custom-call | flops 6300000256 | bytes 14000000 | tf_op jit(solution)/shard_map/bias/pallas_call | solution.py:511
  28.9 1.2 %collective-permute-done.5.refs_7_ = bf16[352,512]{1,0:T(8,128)(2,1)S(1)} collective-permute-done((bf16[352,512]{1,0:T(8,128)(2,1)S(1)}, bf16[352,512]{1,0:T(8,128)(2,1)S(1)}, u32[]{:S(2)}, u32[]{:S(2)}) %collective-permute-start.5) | collective-permute-done | bytes 360480 | tf_op jit(solution)/shard_map/ppermute | solution.py:322
  30.2 3.0 %collective-permute-done.4.refs_15_ = bf16[352,512]{1,0:T(8,128)(2,1)S(1)} collective-permute-done((bf16[352,512]{1,0:T(8,128)(2,1)S(1)}, bf16[352,512]{1,0:T(8,128)(2,1)S(1)}, u32[]{:S(2)}, u32[]{:S(2)}) %collective-permute-start.4) | collective-permute-done | bytes 360480 | tf_op jit(solution)/shard_map/ppermute | solution.py:322
  34.5 5.8 %collective-permute-done.13.refs_13_ = bf16[160,512]{1,0:T(8,128)(2,1)S(1)} collective-permute-done((bf16[160,512]{1,0:T(8,128)(2,1)S(1)}, bf16[160,512]{1,0:T(8,128)(2,1)S(1)}, u32[]{:S(2)}, u32[]{:S(2)}) %collective-permute-start.13) | collective-permute-done | bytes 163872 | tf_op jit(solution)/shard_map/ppermute | solution.py:322
  41.1 5.2 %collective-permute-done.9.refs_1_ = bf16[256,512]{1,0:T(8,128)(2,1)S(1)} collective-permute-done((bf16[256,512]{1,0:T(8,128)(2,1)S(1)}, bf16[256,512]{1,0:T(8,128)(2,1)S(1)}, u32[]{:S(2)}, u32[]{:S(2)}) %collective-permute-start.9) | collective-permute-done | bytes 262176 | tf_op jit(solution)/shard_map/ppermute | solution.py:322
  46.9 6.6 %keep_rows.1 = (bf16[512,512]{1,0:T(8,128)(2,1)}, bf16[512,768]{1,0:T(8,128)(2,1)}) custom-call(s32[32]{0:T(128)} %plan_ref.5, s32[32,256]{1,0:T(8,128)} %hist_ref.3, bf16[2048,512]{1,0:T(8,128)(2,1)} %table_ref.3, f32[16,128]{1,0:T(8,128)} %bitcast.10), custom_call_target="tpu_custom_call" | custom-call | flops 6300000256 | bytes 14000000 | tf_op jit(solution)/shard_map/keep_rows/pallas_call | solution.py:518
  53.6 3.1 %collective-permute-done.10.refs_17_ = bf16[352,512]{1,0:T(8,128)(2,1)S(1)} collective-permute-done((bf16[352,512]{1,0:T(8,128)(2,1)S(1)}, bf16[352,512]{1,0:T(8,128)(2,1)S(1)}, u32[]{:S(2)}, u32[]{:S(2)}) %collective-permute-start.10) | collective-permute-done | bytes 360480 | tf_op jit(solution)/shard_map/ppermute | solution.py:322
  56.7 2.1 %collective-permute-done.8.refs_25_ = bf16[352,512]{1,0:T(8,128)(2,1)S(1)} collective-permute-done((bf16[352,512]{1,0:T(8,128)(2,1)S(1)}, bf16[352,512]{1,0:T(8,128)(2,1)S(1)}, u32[]{:S(2)}, u32[]{:S(2)}) %collective-permute-start.8) | collective-permute-done | bytes 360480 | tf_op jit(solution)/shard_map/ppermute | solution.py:322
  59.4 3.8 %collective-permute-start.18 = (bf16[256,512]{1,0:T(8,128)(2,1)S(1)}, bf16[256,512]{1,0:T(8,128)(2,1)S(1)}, u32[]{:S(2)}, u32[]{:S(2)}) collective-permute-start(bf16[256,512]{1,0:T(8,128)(2,1)S(1)} %copy-done.36), channel_id=1, source_target_pairs={{0,12},{4,0},{8,4},{12,8},{1,13},{5,1},{9,5},{13,9},{2,14},{6,2},{... | collective-permute-start | bytes 786440 | tf_op jit(solution)/shard_map/ppermute | solution.py:322
  63.2 1.6 %collective-permute-start.21 = (bf16[192,512]{1,0:T(8,128)(2,1)S(1)}, bf16[192,512]{1,0:T(8,128)(2,1)S(1)}, u32[]{:S(2)}, u32[]{:S(2)}) collective-permute-start(bf16[192,512]{1,0:T(8,128)(2,1)S(1)} %slice.44), channel_id=1, source_target_pairs={{0,2},{2,0},{1,3},{3,1},{4,6},{6,4},{5,7},{7,5},{8,10},{10,8},{9,1... | collective-permute-start | bytes 589832 | tf_op jit(solution)/shard_map/ppermute | solution.py:322
  65.4 1.1 collective-permute-done.27.refs_14_
  66.8 2.2 %collective-permute-done.21.refs_21_ = bf16[192,512]{1,0:T(8,128)(2,1)S(1)} collective-permute-done((bf16[192,512]{1,0:T(8,128)(2,1)S(1)}, bf16[192,512]{1,0:T(8,128)(2,1)S(1)}, u32[]{:S(2)}, u32[]{:S(2)}) %collective-permute-start.21) | collective-permute-done | bytes 196640 | tf_op jit(solution)/shard_map/ppermute | solution.py:322
  69.5 0.9 collective-permute-done.17.refs_0_
  70.4 1.5 %collective-permute-start.20 = (bf16[352,512]{1,0:T(8,128)(2,1)S(1)}, bf16[352,512]{1,0:T(8,128)(2,1)S(1)}, u32[]{:S(2)}, u32[]{:S(2)}) collective-permute-start(bf16[352,512]{1,0:T(8,128)(2,1)S(1)} %collective-permute-done.8.refs_25_), channel_id=1, source_target_pairs={{0,16},{16,0},{1,17},{17,1},{2,18},{18,2},{3,19},{19,3},{4,20},{20... | collective-permute-start | bytes 1081352 | tf_op jit(solution)/shard_map/ppermute | solution.py:322
  72.1 1.5 %collective-permute-start.19 = (bf16[352,512]{1,0:T(8,128)(2,1)S(1)}, bf16[352,512]{1,0:T(8,128)(2,1)S(1)}, u32[]{:S(2)}, u32[]{:S(2)}) collective-permute-start(bf16[352,512]{1,0:T(8,128)(2,1)S(1)} %collective-permute-done.8.refs_25_), channel_id=1, source_target_pairs={{0,2},{2,0},{1,3},{3,1},{4,6},{6,4},{5,7},{7,5},{8,10},{10,8},{9,1... | collective-permute-start | bytes 1081352 | tf_op jit(solution)/shard_map/ppermute | solution.py:322
  73.6 6.3 %collective-permute-done.20.refs_29_ = bf16[352,512]{1,0:T(8,128)(2,1)S(1)} collective-permute-done((bf16[352,512]{1,0:T(8,128)(2,1)S(1)}, bf16[352,512]{1,0:T(8,128)(2,1)S(1)}, u32[]{:S(2)}, u32[]{:S(2)}) %collective-permute-start.20) | collective-permute-done | bytes 360480 | tf_op jit(solution)/shard_map/ppermute | solution.py:322
  79.9 1.2 %collective-permute-done.19.refs_27_ = bf16[352,512]{1,0:T(8,128)(2,1)S(1)} collective-permute-done((bf16[352,512]{1,0:T(8,128)(2,1)S(1)}, bf16[352,512]{1,0:T(8,128)(2,1)S(1)}, u32[]{:S(2)}, u32[]{:S(2)}) %collective-permute-start.19) | collective-permute-done | bytes 360480 | tf_op jit(solution)/shard_map/ppermute | solution.py:322
  81.2 1.1 collective-permute-start.35
  82.9 1.5 %collective-permute-start.33 = (bf16[192,512]{1,0:T(8,128)(2,1)S(1)}, bf16[192,512]{1,0:T(8,128)(2,1)S(1)}, u32[]{:S(2)}, u32[]{:S(2)}) collective-permute-start(bf16[192,512]{1,0:T(8,128)(2,1)S(1)} %slice.46), channel_id=1, source_target_pairs={{0,2},{2,0},{1,3},{3,1},{4,6},{6,4},{5,7},{7,5},{8,10},{10,8},{9,1... | collective-permute-start | bytes 589832 | tf_op jit(solution)/shard_map/ppermute | solution.py:322
  84.4 2.2 %collective-permute-done.35.refs_33_ = bf16[160,512]{1,0:T(8,128)(2,1)S(1)} collective-permute-done((bf16[160,512]{1,0:T(8,128)(2,1)S(1)}, bf16[160,512]{1,0:T(8,128)(2,1)S(1)}, u32[]{:S(2)}, u32[]{:S(2)}) %collective-permute-start.35) | collective-permute-done | bytes 163872 | tf_op jit(solution)/shard_map/ppermute | solution.py:322
  86.6 2.9 %place_rows.1 = (bf16[256,512]{1,0:T(8,128)(2,1)}, bf16[256,512]{1,0:T(8,128)(2,1)}) custom-call(bf16[512,512]{1,0:T(8,128)(2,1)} %get-tuple-element.77.own_ref, bf16[512,768]{1,0:T(8,128)(2,1)} %get-tuple-element.78.route_ref, bf16[256,512]{1,0:T(8,128)(2,1)} %copy-done.39, bf16[256,512]{1,0:T(8,128)(2,1)} %copy-done.37, bf16[256,512]{1,0:T(8,128)(2,1)} %copy-done.40), custom_call_target="tpu_custom_call" | custom-call | flops 2700000000 | bytes 6000000 | tf_op jit(solution)/shard_map/place_rows/pallas_call | solution.py:531
  92.8 18.7 %layer.1 = (bf16[512,512]{1,0:T(8,128)(2,1)}, bf16[512,512]{1,0:T(8,128)(2,1)}) custom-call(s32[32]{0:T(128)} %plan_ref.5, s32[8]{0:T(128)} %lens_ref.3, bf16[256,512]{1,0:T(8,128)(2,1)} %get-tuple-element.89.keep_ref, bf16[256,512]{1,0:T(8,128)(2,1)} %copy-done.20, f32[1,1024]{1,0:T(1,128)} %bitcast.8, f32[8,128]{1,0:T(8,128)} %slice.49.out_gain_ref, ...), custom_call_target="tpu_custom_call" | custom-call | tf_op jit(solution)/shard_map/layer/pallas_call | solution.py:558
  111.9 1.8 %collective-permute-done.37 = bf16[512,512]{1,0:T(8,128)(2,1)S(1)} collective-permute-done((bf16[512,512]{1,0:T(8,128)(2,1)}, bf16[512,512]{1,0:T(8,128)(2,1)S(1)}, u32[]{:S(2)}, u32[]{:S(2)}) %collective-permute-start.37) | collective-permute-done | bytes 524320 | tf_op jit(solution)/shard_map/ppermute | solution.py:322
  113.7 2.6 %maximum_select_fusion = bf16[1024,512]{1,0:T(8,128)(2,1)} fusion(bf16[512,512]{1,0:T(8,128)(2,1)S(1)} %collective-permute-done.37, bf16[512,512]{1,0:T(8,128)(2,1)} %get-tuple-element.111, pred[]{:T(512)S(6)} %eq.4), kind=kLoop, calls=%fused_computation | loop fusion | flops 4718592 | bytes 2097153 | tf_op jit(solution)/shard_map/jit(_where)/select_n | solution.py:579
  (148 shorter events, 13.0 us)
Async XLA Ops:
  0.8 13.5 %collective-permute-start.3 = (f32[4,176]{1,0:T(4,128)S(1)}, f32[4,176]{1,0:T(4,128)S(1)}, u32[]{:S(2)}, u32[]{:S(2)}) collective-permute-start(f32[4,176]{1,0:T(4,128)S(1)} %pad_maximum_fusion), channel_id=1, source_target_pairs={{0,1},{1,0},{2,3},{3,2},{4,5},{5,4},{6,7},{7,6},{8,9},{9,8},{10,11... | collective-permute-start | bytes 8456 | tf_op jit(solution)/shard_map/ppermute | solution.py:322
  1.2 14.4 %collective-permute-start.2 = (bf16[512,256]{1,0:T(8,128)(2,1)}, bf16[512,256]{1,0:T(8,128)(2,1)S(1)}, u32[]{:S(2)}, u32[]{:S(2)}) collective-permute-start(bf16[512,256]{1,0:T(8,128)(2,1)} %refs_2_.1), channel_id=1, source_target_pairs={{0,1},{1,0},{2,3},{3,2},{4,5},{5,4},{6,7},{7,6},{8,9},{9,8},{10,11... | collective-permute-start | bytes 786440 | tf_op jit(solution)/shard_map/ppermute | solution.py:322
  1.3 16.7 %collective-permute-start.1 = (bf16[4,256,512]{2,1,0:T(8,128)(2,1)}, bf16[4,256,512]{2,1,0:T(8,128)(2,1)S(1)}, u32[]{:S(2)}, u32[]{:S(2)}) collective-permute-start(bf16[4,256,512]{2,1,0:T(8,128)(2,1)} %refs_1_.1), channel_id=1, source_target_pairs={{0,1},{1,0},{2,3},{3,2},{4,5},{5,4},{6,7},{7,6},{8,9},{9,8},{10,11... | collective-permute-start | bytes 3145736 | tf_op jit(solution)/shard_map/ppermute | solution.py:322
  4.3 13.7 %collective-permute-start = (bf16[352,512]{1,0:T(8,128)(2,1)S(1)}, bf16[352,512]{1,0:T(8,128)(2,1)S(1)}, u32[]{:S(2)}, u32[]{:S(2)}) collective-permute-start(bf16[352,512]{1,0:T(8,128)(2,1)S(1)} %maximum_maximum_fusion), channel_id=1, source_target_pairs={{0,4},{4,8},{8,12},{12,0},{1,5},{5,9},{9,13},{13,1},{2,6},{6,10},{... | collective-permute-start | bytes 1081352 | tf_op jit(solution)/shard_map/ppermute | solution.py:322
  18.0 10.2 %collective-permute-start.7 = (bf16[352,512]{1,0:T(8,128)(2,1)S(1)}, bf16[352,512]{1,0:T(8,128)(2,1)S(1)}, u32[]{:S(2)}, u32[]{:S(2)}) collective-permute-start(bf16[352,512]{1,0:T(8,128)(2,1)S(1)} %collective-permute-done.refs_5_), channel_id=1, source_target_pairs={{0,1},{1,0},{2,3},{3,2},{4,5},{5,4},{6,7},{7,6},{8,9},{9,8},{10,11... | collective-permute-start | bytes 1081352 | tf_op jit(solution)/shard_map/ppermute | solution.py:322
  18.1 10.8 %collective-permute-start.6 = (bf16[352,512]{1,0:T(8,128)(2,1)S(1)}, bf16[352,512]{1,0:T(8,128)(2,1)S(1)}, u32[]{:S(2)}, u32[]{:S(2)}) collective-permute-start(bf16[352,512]{1,0:T(8,128)(2,1)S(1)} %collective-permute-done.refs_5_), channel_id=1, source_target_pairs={{0,16},{16,0},{1,17},{17,1},{2,18},{18,2},{3,19},{19,3},{4,20},{20... | collective-permute-start | bytes 1081352 | tf_op jit(solution)/shard_map/ppermute | solution.py:322
  19.7 10.5 %collective-permute-start.5 = (bf16[352,512]{1,0:T(8,128)(2,1)S(1)}, bf16[352,512]{1,0:T(8,128)(2,1)S(1)}, u32[]{:S(2)}, u32[]{:S(2)}) collective-permute-start(bf16[352,512]{1,0:T(8,128)(2,1)S(1)} %collective-permute-done.refs_5_), channel_id=1, source_target_pairs={{0,2},{2,0},{1,3},{3,1},{4,6},{6,4},{5,7},{7,5},{8,10},{10,8},{9,1... | collective-permute-start | bytes 1081352 | tf_op jit(solution)/shard_map/ppermute | solution.py:322
  21.2 12.0 %collective-permute-start.4 = (bf16[352,512]{1,0:T(8,128)(2,1)S(1)}, bf16[352,512]{1,0:T(8,128)(2,1)S(1)}, u32[]{:S(2)}, u32[]{:S(2)}) collective-permute-start(bf16[352,512]{1,0:T(8,128)(2,1)S(1)} %collective-permute-done.refs_5_), channel_id=1, source_target_pairs={{0,4},{4,8},{8,12},{12,0},{1,5},{5,9},{9,13},{13,1},{2,6},{6,10},{... | collective-permute-start | bytes 1081352 | tf_op jit(solution)/shard_map/ppermute | solution.py:322
  33.2 13.7 %collective-permute-start.16 = (bf16[352,512]{1,0:T(8,128)(2,1)S(1)}, bf16[352,512]{1,0:T(8,128)(2,1)S(1)}, u32[]{:S(2)}, u32[]{:S(2)}) collective-permute-start(bf16[352,512]{1,0:T(8,128)(2,1)S(1)} %collective-permute-done.6.refs_9_), channel_id=1, source_target_pairs={{0,1},{1,0},{2,3},{3,2},{4,5},{5,4},{6,7},{7,6},{8,9},{9,8},{10,11... | collective-permute-start | bytes 1081352 | tf_op jit(solution)/shard_map/ppermute | solution.py:322
  33.2 13.2 %collective-permute-start.9 = (bf16[256,512]{1,0:T(8,128)(2,1)S(1)}, bf16[256,512]{1,0:T(8,128)(2,1)S(1)}, u32[]{:S(2)}, u32[]{:S(2)}) collective-permute-start(bf16[256,512]{1,0:T(8,128)(2,1)S(1)} %copy-done.41), channel_id=1, source_target_pairs={{0,8},{4,12},{8,0},{12,4},{1,9},{5,13},{9,1},{13,5},{2,10},{6,14},... | collective-permute-start | bytes 786440 | tf_op jit(solution)/shard_map/ppermute | solution.py:322
  33.3 7.3 %collective-permute-start.12 = (bf16[192,512]{1,0:T(8,128)(2,1)S(1)}, bf16[192,512]{1,0:T(8,128)(2,1)S(1)}, u32[]{:S(2)}, u32[]{:S(2)}) collective-permute-start(bf16[192,512]{1,0:T(8,128)(2,1)S(1)} %slice.42), channel_id=1, source_target_pairs={{0,2},{2,0},{1,3},{3,1},{4,6},{6,4},{5,7},{7,5},{8,10},{10,8},{9,1... | collective-permute-start | bytes 589832 | tf_op jit(solution)/shard_map/ppermute | solution.py:322
  33.9 6.3 %collective-permute-start.13 = (bf16[160,512]{1,0:T(8,128)(2,1)S(1)}, bf16[160,512]{1,0:T(8,128)(2,1)S(1)}, u32[]{:S(2)}, u32[]{:S(2)}) collective-permute-start(bf16[160,512]{1,0:T(8,128)(2,1)S(1)} %slice.43), channel_id=1, source_target_pairs={{0,16},{16,0},{1,17},{17,1},{2,18},{18,2},{3,19},{19,3},{4,20},{20... | collective-permute-start | bytes 491528 | tf_op jit(solution)/shard_map/ppermute | solution.py:322
  34.5 19.1 %collective-permute-start.15 = (bf16[352,512]{1,0:T(8,128)(2,1)S(1)}, bf16[352,512]{1,0:T(8,128)(2,1)S(1)}, u32[]{:S(2)}, u32[]{:S(2)}) collective-permute-start(bf16[352,512]{1,0:T(8,128)(2,1)S(1)} %collective-permute-done.5.refs_7_), channel_id=1, source_target_pairs={{0,1},{1,0},{2,3},{3,2},{4,5},{5,4},{6,7},{7,6},{8,9},{9,8},{10,11... | collective-permute-start | bytes 1081352 | tf_op jit(solution)/shard_map/ppermute | solution.py:322
  40.3 13.3 %collective-permute-start.14 = (bf16[352,512]{1,0:T(8,128)(2,1)S(1)}, bf16[352,512]{1,0:T(8,128)(2,1)S(1)}, u32[]{:S(2)}, u32[]{:S(2)}) collective-permute-start(bf16[352,512]{1,0:T(8,128)(2,1)S(1)} %collective-permute-done.4.refs_15_), channel_id=1, source_target_pairs={{0,1},{1,0},{2,3},{3,2},{4,5},{5,4},{6,7},{7,6},{8,9},{9,8},{10,11... | collective-permute-start | bytes 1081352 | tf_op jit(solution)/shard_map/ppermute | solution.py:322
  40.6 13.0 %collective-permute-start.11 = (bf16[352,512]{1,0:T(8,128)(2,1)S(1)}, bf16[352,512]{1,0:T(8,128)(2,1)S(1)}, u32[]{:S(2)}, u32[]{:S(2)}) collective-permute-start(bf16[352,512]{1,0:T(8,128)(2,1)S(1)} %collective-permute-done.4.refs_15_), channel_id=1, source_target_pairs={{0,16},{16,0},{1,17},{17,1},{2,18},{18,2},{3,19},{19,3},{4,20},{20... | collective-permute-start | bytes 1081352 | tf_op jit(solution)/shard_map/ppermute | solution.py:322
  46.4 10.4 %collective-permute-start.10 = (bf16[352,512]{1,0:T(8,128)(2,1)S(1)}, bf16[352,512]{1,0:T(8,128)(2,1)S(1)}, u32[]{:S(2)}, u32[]{:S(2)}) collective-permute-start(bf16[352,512]{1,0:T(8,128)(2,1)S(1)} %collective-permute-done.4.refs_15_), channel_id=1, source_target_pairs={{0,2},{2,0},{1,3},{3,1},{4,6},{6,4},{5,7},{7,5},{8,10},{10,8},{9,1... | collective-permute-start | bytes 1081352 | tf_op jit(solution)/shard_map/ppermute | solution.py:322
  46.9 11.9 %collective-permute-start.8 = (bf16[352,512]{1,0:T(8,128)(2,1)S(1)}, bf16[352,512]{1,0:T(8,128)(2,1)S(1)}, u32[]{:S(2)}, u32[]{:S(2)}) collective-permute-start(bf16[352,512]{1,0:T(8,128)(2,1)S(1)} %collective-permute-done.4.refs_15_), channel_id=1, source_target_pairs={{0,4},{4,8},{8,12},{12,0},{1,5},{5,9},{9,13},{13,1},{2,6},{6,10},{... | collective-permute-start | bytes 1081352 | tf_op jit(solution)/shard_map/ppermute | solution.py:322
  58.8 6.0 %collective-permute-start.22 = (bf16[160,512]{1,0:T(8,128)(2,1)S(1)}, bf16[160,512]{1,0:T(8,128)(2,1)S(1)}, u32[]{:S(2)}, u32[]{:S(2)}) collective-permute-start(bf16[160,512]{1,0:T(8,128)(2,1)S(1)} %slice.45), channel_id=1, source_target_pairs={{0,16},{16,0},{1,17},{17,1},{2,18},{18,2},{3,19},{19,3},{4,20},{20... | collective-permute-start | bytes 491528 | tf_op jit(solution)/shard_map/ppermute | solution.py:322
  59.4 11.0 %collective-permute-start.17 = (bf16[256,512]{1,0:T(8,128)(2,1)S(1)}, bf16[256,512]{1,0:T(8,128)(2,1)S(1)}, u32[]{:S(2)}, u32[]{:S(2)}) collective-permute-start(bf16[256,512]{1,0:T(8,128)(2,1)S(1)} %copy-done.38), channel_id=1, source_target_pairs={{0,4},{4,8},{8,12},{12,0},{1,5},{5,9},{9,13},{13,1},{2,6},{6,10},{... | collective-permute-start | bytes 786440 | tf_op jit(solution)/shard_map/ppermute | solution.py:322
  59.4 12.7 %collective-permute-start.18 = (bf16[256,512]{1,0:T(8,128)(2,1)S(1)}, bf16[256,512]{1,0:T(8,128)(2,1)S(1)}, u32[]{:S(2)}, u32[]{:S(2)}) collective-permute-start(bf16[256,512]{1,0:T(8,128)(2,1)S(1)} %copy-done.36), channel_id=1, source_target_pairs={{0,12},{4,0},{8,4},{12,8},{1,13},{5,1},{9,5},{13,9},{2,14},{6,2},{... | collective-permute-start | bytes 786440 | tf_op jit(solution)/shard_map/ppermute | solution.py:322
  63.2 5.7 %collective-permute-start.21 = (bf16[192,512]{1,0:T(8,128)(2,1)S(1)}, bf16[192,512]{1,0:T(8,128)(2,1)S(1)}, u32[]{:S(2)}, u32[]{:S(2)}) collective-permute-start(bf16[192,512]{1,0:T(8,128)(2,1)S(1)} %slice.44), channel_id=1, source_target_pairs={{0,2},{2,0},{1,3},{3,1},{4,6},{6,4},{5,7},{7,5},{8,10},{10,8},{9,1... | collective-permute-start | bytes 589832 | tf_op jit(solution)/shard_map/ppermute | solution.py:322
  64.8 4.2 %collective-permute-start.26 = (bf16[192,512]{1,0:T(8,128)(2,1)S(1)}, bf16[192,512]{1,0:T(8,128)(2,1)S(1)}, u32[]{:S(2)}, u32[]{:S(2)}) collective-permute-start(bf16[192,512]{1,0:T(8,128)(2,1)S(1)} %collective-permute-done.12.refs_11_), channel_id=1, source_target_pairs={{0,1},{1,0},{2,3},{3,2},{4,5},{5,4},{6,7},{7,6},{8,9},{9,8},{10,11... | collective-permute-start | bytes 589832 | tf_op jit(solution)/shard_map/ppermute | solution.py:322
  66.5 7.1 %collective-permute-start.25 = (bf16[352,512]{1,0:T(8,128)(2,1)S(1)}, bf16[352,512]{1,0:T(8,128)(2,1)S(1)}, u32[]{:S(2)}, u32[]{:S(2)}) collective-permute-start(bf16[352,512]{1,0:T(8,128)(2,1)S(1)} %collective-permute-done.11.refs_19_), channel_id=1, source_target_pairs={{0,1},{1,0},{2,3},{3,2},{4,5},{5,4},{6,7},{7,6},{8,9},{9,8},{10,11... | collective-permute-start | bytes 1081352 | tf_op jit(solution)/shard_map/ppermute | solution.py:322
  69.0 4.6 %collective-permute-start.24 = (bf16[352,512]{1,0:T(8,128)(2,1)S(1)}, bf16[352,512]{1,0:T(8,128)(2,1)S(1)}, u32[]{:S(2)}, u32[]{:S(2)}) collective-permute-start(bf16[352,512]{1,0:T(8,128)(2,1)S(1)} %collective-permute-done.10.refs_17_), channel_id=1, source_target_pairs={{0,1},{1,0},{2,3},{3,2},{4,5},{5,4},{6,7},{7,6},{8,9},{9,8},{10,11... | collective-permute-start | bytes 1081352 | tf_op jit(solution)/shard_map/ppermute | solution.py:322
  69.0 4.6 %collective-permute-start.23 = (bf16[352,512]{1,0:T(8,128)(2,1)S(1)}, bf16[352,512]{1,0:T(8,128)(2,1)S(1)}, u32[]{:S(2)}, u32[]{:S(2)}) collective-permute-start(bf16[352,512]{1,0:T(8,128)(2,1)S(1)} %collective-permute-done.8.refs_25_), channel_id=1, source_target_pairs={{0,1},{1,0},{2,3},{3,2},{4,5},{5,4},{6,7},{7,6},{8,9},{9,8},{10,11... | collective-permute-start | bytes 1081352 | tf_op jit(solution)/shard_map/ppermute | solution.py:322
  70.4 9.5 %collective-permute-start.20 = (bf16[352,512]{1,0:T(8,128)(2,1)S(1)}, bf16[352,512]{1,0:T(8,128)(2,1)S(1)}, u32[]{:S(2)}, u32[]{:S(2)}) collective-permute-start(bf16[352,512]{1,0:T(8,128)(2,1)S(1)} %collective-permute-done.8.refs_25_), channel_id=1, source_target_pairs={{0,16},{16,0},{1,17},{17,1},{2,18},{18,2},{3,19},{19,3},{4,20},{20... | collective-permute-start | bytes 1081352 | tf_op jit(solution)/shard_map/ppermute | solution.py:322
  72.1 9.1 %collective-permute-start.19 = (bf16[352,512]{1,0:T(8,128)(2,1)S(1)}, bf16[352,512]{1,0:T(8,128)(2,1)S(1)}, u32[]{:S(2)}, u32[]{:S(2)}) collective-permute-start(bf16[352,512]{1,0:T(8,128)(2,1)S(1)} %collective-permute-done.8.refs_25_), channel_id=1, source_target_pairs={{0,2},{2,0},{1,3},{3,1},{4,6},{6,4},{5,7},{7,5},{8,10},{10,8},{9,1... | collective-permute-start | bytes 1081352 | tf_op jit(solution)/shard_map/ppermute | solution.py:322
  81.2 5.4 %collective-permute-start.35 = (bf16[160,512]{1,0:T(8,128)(2,1)S(1)}, bf16[160,512]{1,0:T(8,128)(2,1)S(1)}, u32[]{:S(2)}, u32[]{:S(2)}) collective-permute-start(bf16[160,512]{1,0:T(8,128)(2,1)S(1)} %slice.47), channel_id=1, source_target_pairs={{0,16},{16,0},{1,17},{17,1},{2,18},{18,2},{3,19},{19,3},{4,20},{20... | collective-permute-start | bytes 491528 | tf_op jit(solution)/shard_map/ppermute | solution.py:322
  82.2 9.6 %collective-permute-start.31 = (bf16[352,512]{1,0:T(8,128)(2,1)S(1)}, bf16[352,512]{1,0:T(8,128)(2,1)S(1)}, u32[]{:S(2)}, u32[]{:S(2)}) collective-permute-start(bf16[352,512]{1,0:T(8,128)(2,1)S(1)} %collective-permute-done.19.refs_27_), channel_id=1, source_target_pairs={{0,1},{1,0},{2,3},{3,2},{4,5},{5,4},{6,7},{7,6},{8,9},{9,8},{10,11... | collective-permute-start | bytes 1081352 | tf_op jit(solution)/shard_map/ppermute | solution.py:322
  82.2 9.6 %collective-permute-start.32 = (bf16[352,512]{1,0:T(8,128)(2,1)S(1)}, bf16[352,512]{1,0:T(8,128)(2,1)S(1)}, u32[]{:S(2)}, u32[]{:S(2)}) collective-permute-start(bf16[352,512]{1,0:T(8,128)(2,1)S(1)} %collective-permute-done.20.refs_29_), channel_id=1, source_target_pairs={{0,1},{1,0},{2,3},{3,2},{4,5},{5,4},{6,7},{7,6},{8,9},{9,8},{10,11... | collective-permute-start | bytes 1081352 | tf_op jit(solution)/shard_map/ppermute | solution.py:322
  82.8 6.8 %collective-permute-start.30 = (bf16[160,512]{1,0:T(8,128)(2,1)S(1)}, bf16[160,512]{1,0:T(8,128)(2,1)S(1)}, u32[]{:S(2)}, u32[]{:S(2)}) collective-permute-start(bf16[160,512]{1,0:T(8,128)(2,1)S(1)} %collective-permute-done.22.refs_23_), channel_id=1, source_target_pairs={{0,1},{1,0},{2,3},{3,2},{4,5},{5,4},{6,7},{7,6},{8,9},{9,8},{10,11... | collective-permute-start | bytes 491528 | tf_op jit(solution)/shard_map/ppermute | solution.py:322
  82.9 7.3 %collective-permute-start.33 = (bf16[192,512]{1,0:T(8,128)(2,1)S(1)}, bf16[192,512]{1,0:T(8,128)(2,1)S(1)}, u32[]{:S(2)}, u32[]{:S(2)}) collective-permute-start(bf16[192,512]{1,0:T(8,128)(2,1)S(1)} %slice.46), channel_id=1, source_target_pairs={{0,2},{2,0},{1,3},{3,1},{4,6},{6,4},{5,7},{7,5},{8,10},{10,8},{9,1... | collective-permute-start | bytes 589832 | tf_op jit(solution)/shard_map/ppermute | solution.py:322
  (48 other events, 659.5 us)

commit v3 on v2

--- a/solution.py
+++ b/solution.py
@@ -322,29 +322,59 @@
     return lax.ppermute(x, axis, [(i, (i + k) % size) for i in range(size)])
 
 
-Q_ROWS, CUT = 256, 192
-
-
-def quarter_pack(z, embed_proj, qkvu_proj, out_proj):
-    width = embed_proj.shape[0]
-    q = lax.axis_index("parts") * z.bal + lax.axis_index("bal")
+def cross(x, near_first):
+    pairs = []
+    for i in range(8):
+        p, b, m = i // 4, i // 2 % 2, i % 2
+        p, b = (p, 1 - b) if (m == 0) == near_first else (1 - p, b)
+        pairs.append((i, (p * 2 + b) * 2 + m))
+    return lax.ppermute(x, ("parts", "bal", "mp"), pairs)
+
+
+def pack_kernel(e_ref, w_ref, o_ref, out_ref, sems):
+    q = lax.axis_index("parts") * 2 + lax.axis_index("bal")
     m = lax.axis_index("mp")
-    four, deep, cols = qkvu_proj.shape
-    share = deep // 4
-    qk = lax.dynamic_slice_in_dim(qkvu_proj, q * share, share, 1).reshape(four * share, cols)
-    e_rows = width // 8
-    e = lax.dynamic_slice_in_dim(embed_proj, (q * 2 + m) * e_rows, e_rows, 0)
-    e = jnp.concatenate([e[: e_rows // 2], e[e_rows // 2 :]], axis=1)
-    o_rows = out_proj.shape[0] // 4
-    o = lax.dynamic_slice_in_dim(out_proj, q * o_rows, o_rows, 0)
-    o = jnp.concatenate([o[: o_rows // 2], o[o_rows // 2 :]], axis=1)
-    return jnp.concatenate([qk, e, o], axis=0)
+    share = w_ref.shape[1] // 4
+    cols = e_ref.shape[1]
+    e_part = e_ref.shape[0] // 16
+    o_part = o_ref.shape[0] // 8
+    copies = []
+
+    def add(src, dst):
+        copies.append(pltpu.make_async_copy(src, dst, sems))
+
+    def at(x, size):
+        return pl.ds(pl.multiple_of(x * size, size), size)
+
+    for c in range(4):
+        add(w_ref.at[c, at(q, share), :], out_ref.at[c * share : (c + 1) * share, :])
+    first = 4 * share
+    for j in range(2):
+        lanes = slice(j * cols, (j + 1) * cols)
+        add(e_ref.at[at((q * 2 + m) * 2 + j, e_part), :], out_ref.at[first : first + e_part, lanes])
+        add(
+            o_ref.at[at(q * 2 + j, o_part), :],
+            out_ref.at[first + e_part : first + e_part + o_part, lanes],
+        )
+    for c in copies:
+        c.start()
+    for c in copies:
+        c.wait()
+
+
+def merge_kernel(*refs):
+    out_ref, sem = refs[4:]
+    copies = [pltpu.make_async_copy(refs[i], out_ref.at[i], sem) for i in range(4)]
+    for c in copies:
+        c.start()
+    for c in copies:
+        c.wait()
 
 
 def load_pieces(z):
     def load(refs, e_ref, w_ref, o_ref, sems):
         t, m = lax.axis_index("table"), lax.axis_index("mp")
-        parts_pos, bal_pos = lax.axis_index("parts"), lax.axis_index("bal")
+        p, b = lax.axis_index("parts"), lax.axis_index("bal")
         e_own, w_own, o_own, w_near, o_near = refs[:5]
         deep, cols = w_own.shape[1], w_own.shape[2]
         e_cols = e_own.shape[1]
@@ -355,49 +385,48 @@
             groups[g].append(pltpu.make_async_copy(src, dst, sems.at[g]))
 
         def at(x, size):
-            return pl.ds(pl.multiple_of(x, size), size)
-
-        add(0, e_own, e_ref.at[:, at(t * e_cols, e_cols)])
+            return pl.ds(pl.multiple_of(x * size, size), size)
+
+        add(0, e_own, e_ref.at[:, at(t, e_cols)])
         for core, w, o in ((m, w_own, o_own), (1 - m, w_near, o_near)):
-            add(1, w, w_ref.at[:, at(t * deep, deep), at(core * cols, cols)])
-            add(2, o, o_ref.at[at(core * o_rows, o_rows), at(t * e_cols, e_cols)])
+            add(1, w, w_ref.at[:, at(t, deep), at(core, cols)])
+            add(2, o, o_ref.at[at(core, o_rows), at(t, e_cols)])
         share = deep // 4
         e_part = e_ref.shape[0] // 16
         o_part = o_rows // 8
-        rest = refs[5:]
+        first = 4 * share
+        along_b, along_p = p * 2 + 1 - b, (1 - p) * 2 + b
         for k in range(1, z.n):
             source = lax.rem(t + z.n - k, z.n)
-            block = rest[(k - 1) * 10 : k * 10]
-            for i, (dp, db) in enumerate(((0, 0), (0, 1), (1, 0), (1, 1), (1, 1))):
-                pp = parts_pos if dp == 0 else 1 - parts_pos
-                bb = bal_pos if db == 0 else 1 - bal_pos
-                q = pp * 2 + bb
-                low = CUT if i == 4 else 0
-                high = CUT if i == 3 else 4 * share + e_part + o_part
+            block = refs[9:]
+            if k < 3:
+                both = refs[5 + (k - 1) * 2 : 5 + k * 2]
+                block = [ref.at[i] for i in range(4) for ref in both]
+            for i in range(4):
                 for core, ref in ((m, block[2 * i]), (1 - m, block[2 * i + 1])):
+                    q = (
+                        p * 2 + b,
+                        jnp.where(core == 0, along_b, along_p),
+                        jnp.where(core == 0, along_p, along_b),
+                        (1 - p) * 2 + 1 - b,
+                    )[i]
                     for c in range(4):
-                        if low <= c * share < high:
-                            add(
-                                1,
-                                ref.at[c * share - low : (c + 1) * share - low, :],
-                                w_ref.at[c, at(source * deep + q * share, share), at(core * cols, cols)],
-                            )
-                    if high <= 4 * share:
-                        continue
-                    first = 4 * share - low
+                        add(
+                            1,
+                            ref.at[c * share : (c + 1) * share, :],
+                            w_ref.at[c, at(source * 4 + q, share), at(core, cols)],
+                        )
                     for j in range(2):
                         lanes = slice(j * e_cols, (j + 1) * e_cols)
                         add(
                             0,
                             ref.at[first : first + e_part, lanes],
-                            e_ref.at[at(((q * 2 + core) * 2 + j) * e_part, e_part), at(source * e_cols, e_cols)],
+                            e_ref.at[at((q * 2 + core) * 2 + j, e_part), at(source, e_cols)],
                         )
                         add(
                             2,
                             ref.at[first + e_part : first + e_part + o_part, lanes],
-                            o_ref.at[
-                                at(core * o_rows + (q * 2 + j) * o_part, o_part), at(source * e_cols, e_cols)
-                            ],
+                            o_ref.at[at(core * 8 + q * 2 + j, o_part), at(source, e_cols)],
                         )
         return groups
 
@@ -480,7 +509,7 @@
             mp_pos == 0, jnp.concatenate([x, other], 0), jnp.concatenate([other, x], 0)
         )
 
-    def biases():
+    def biases(pos_bias, time_bias, out_gain):
         small = jnp.concatenate(
             [pos_bias, time_bias, out_gain.reshape(pos_bias.shape[0], -1)], axis=1
         )
@@ -488,56 +517,64 @@
         return small[:, : buckets + tbuckets], small[:, buckets + tbuckets :]
 
     if z.n == 4 and z.bal == 2 and lax.axis_size("parts") == 2:
-        pack = quarter_pack(z, embed_proj, qkvu_proj, out_proj)
         near = functools.partial(swap, axis="mp", size=2)
         hop = functools.partial(swap, axis="table", size=z.n)
-
-        def first(r):
-            return swap(r, "bal", 2), swap(r, "parts", 2)
-
-        def second(x, y):
-            return swap(y[:CUT], "bal", 2), swap(x[CUT:], "parts", 2)
-
-        table, gains = biases()
+        rows = qkvu_proj.shape[1] + z.width // 16 + out_proj.shape[0] // 8
+        pack = pl.pallas_call(
+            pack_kernel,
+            out_shape=jax.ShapeDtypeStruct((rows, qkvu_proj.shape[2]), BF),
+            in_specs=[pl.BlockSpec(memory_space=pl.ANY)] * 3,
+            out_specs=vspec(),
+            scratch_shapes=[pltpu.SemaphoreType.DMA],
+            compiler_params=params(),
+            name="pack",
+        )(embed_proj, qkvu_proj, out_proj)
+        merge = pl.pallas_call(
+            merge_kernel,
+            out_shape=jax.ShapeDtypeStruct((4, rows, qkvu_proj.shape[2]), BF),
+            in_specs=[pl.BlockSpec(memory_space=pl.ANY)] * 4,
+            out_specs=vspec(),
+            scratch_shapes=[pltpu.SemaphoreType.DMA],
+            compiler_params=params(),
+            cost_estimate=cost(2),
+            name="merge",
+        )
         r1 = hop(pack)
         sent = send_rows(plan, hist_ids, table_rows, scale)
         w_near, o_near = near(qkvu_proj), near(out_proj)
-        r1, sent, w_near, o_near, table, gains, plan1 = fence(
-            r1, sent, w_near, o_near, table, gains, plan
+        sent, small_in = fence(sent, (pos_bias, time_bias, out_gain))
+        table, gains = biases(*small_in)
+        r1, sent, table, w_near, o_near = fence(r1, sent, table, w_near, o_near)
+        r2 = hop(r1)
+        got1 = swap(sent[0], "table", z.n, 1)
+        a1, b1 = cross(r1, True), cross(r1, False)
+        bias = make_bias(table, plan, lengths, time_bucket)
+        r1, r2, got1, a1, b1, bias, sent, plan1 = fence(r1, r2, got1, a1, b1, bias, sent, plan)
+        r3 = hop(r2)
+        got3 = swap(sent[2], "table", z.n, 3)
+        a2, b2, d1 = cross(r2, True), cross(r2, False), cross(b1, True)
+        own, route = keep_rows(plan1, hist_ids, table_rows, scale)
+        r1, a1, b1, d1, r2, r3, a2, b2, got3, own, route, sent = fence(
+            r1, a1, b1, d1, r2, r3, a2, b2, got3, own, route, sent
         )
-        r2 = hop(r1)
-        x1, y1 = first(r1)
-        r1n = near(r1)
-        bias = make_bias(table, plan1, lengths, time_bucket)
-        r1, r2, x1, y1, r1n, bias, sent, plan2 = fence(r1, r2, x1, y1, r1n, bias, sent, plan1)
-        r3 = hop(r2)
         got2 = swap(sent[1], "table", z.n, 2)
-        x2, y2 = first(r2)
-        dx1, dy1 = second(x1, y1)
-        r2n, x1n, y1n = near(r2), near(x1), near(y1)
-        own, route = keep_rows(plan2, hist_ids, table_rows, scale)
-        r2, r3, got2, x2, y2, dx1, dy1, r2n, x1n, y1n, own, route, sent = fence(
-            r2, r3, got2, x2, y2, dx1, dy1, r2n, x1n, y1n, own, route, sent
+        a3, b3, d2 = cross(r3, True), cross(r3, False), cross(b2, True)
+        chunk1 = merge(r1, a1, b1, d1)
+        near1 = near(chunk1)
+        a3, b3, d2, chunk1, near1, got2, r2, a2, b2, r3 = fence(
+            a3, b3, d2, chunk1, near1, got2, r2, a2, b2, r3
         )
-        got1 = swap(sent[0], "table", z.n, 1)
-        got3 = swap(sent[2], "table", z.n, 3)
-        x3, y3 = first(r3)
-        dx2, dy2 = second(x2, y2)
-        r3n, x2n, y2n, dx1n, dy1n = [near(v) for v in (r3, x2, y2, dx1, dy1)]
-        r3, got1, got3, x3, y3, dx2, dy2, r3n, x2n, y2n, dx1n, dy1n = fence(
-            r3, got1, got3, x3, y3, dx2, dy2, r3n, x2n, y2n, dx1n, dy1n
-        )
-        dx3, dy3 = second(x3, y3)
+        d3 = cross(b3, True)
         keep, give = place_rows(own, route, got1, got2, got3)
         back = near(give)
-        x3n, y3n, dx2n, dy2n = [near(v) for v in (x3, y3, dx2, dy2)]
-        weights = [embed_proj, qkvu_proj, out_proj, w_near, o_near]
-        weights += [r1, r1n, x1, x1n, y1, y1n, dx1, dx1n, dy1, dy1n]
-        weights += [r2, r2n, x2, x2n, y2, y2n, dx2, dx2n, dy2, dy2n]
-        weights += [r3, r3n, x3, x3n, y3, y3n, dx3, near(dx3), dy3, near(dy3)]
+        chunk2 = merge(r2, a2, b2, d2)
+        near2 = near(chunk2)
+        weights = [embed_proj, qkvu_proj, out_proj, w_near, o_near, chunk1, near1, chunk2, near2]
+        for v in (r3, a3, b3, d3):
+            weights += [v, near(v)]
         load = load_pieces(z)
     else:
-        table, gains = biases()
+        table, gains = biases(pos_bias, time_bias, out_gain)
         bias = make_bias(table, plan, lengths, time_bucket)
         sent = send_rows(plan, hist_ids, table_rows, scale)
         got = [swap(s, "table", z.n, k + 1) for k, s in enumerate(sent)]

time: 117 us -> 110 us (0.940)
  waiting for transfers between devices: 40.8 us -> 29 us
  Pallas kernels: 42.6 us -> 49.6 us
    ppermute x38 -> x17, waiting for transfers between devices: 40.8 us -> 27.8 us  [swap(): return lax.ppermute(x, axis, [(i, (i + k) % size) for i in range(size)])]
    ppermute x38 -> x17, starting transfers between devices: 24.1 us -> 13.4 us  [swap(): return lax.ppermute(x, axis, [(i, (i + k) % size) for i in range(size)])]
    ppermute x0 -> x9, starting transfers between devices: none -> 9.87 us  [cross(): return lax.ppermute(x, ('parts', 'bal', 'mp'), pairs)]
    pallas_call x2 -> x5, Pallas kernels: 13.7 us -> 20.7 us  [the longest x1 7.02 us: body(): bias = make_bias(table, plan, lengths, time_bucket)]
    unnamed x84 -> x58, local copies, waits for them, and re-layouts: 1.07 us -> 2.9 us
    slice x8 -> x0, local copies, waits for them, and re-layouts: 1.59 us -> none  [the longest x1 0.78 us: quarter_pack(): o = jnp.concatenate([o[:o_rows // 2], o[o_rows // 2:]], axis=1)]
    ppermute x0 -> x9, waiting for transfers between devices: none -> 1.2 us  [cross(): return lax.ppermute(x, ('parts', 'bal', 'mp'), pairs)]
  transfers between devices with their start and end apart: 38 -> 26, of which waited for: 20 -> 9; matrix products, arithmetic and copies ran while one was open for 3% -> 1% of each run, Pallas kernels for 21% -> 23%
where the time goes in v3:
time: 110 us; the launch traced here: 109 us
  Pallas kernels  49.6 us (45%)
  waiting for transfers between devices  29 us (26%)
  starting transfers between devices  23.3 us (21%)
  local copies, waits for them, and re-layouts  4.23 us (4%)
  other arithmetic  2.75 us (2%)
    ppermute x17, waiting for transfers between devices, swap(): return lax.ppermute(x, axis, [(i, (i + k) % size) for i in range(size)])  27.8 us
    pallas_call x1, Pallas kernels, body(): pl.pallas_call(functools.partial(layer_kernel, z, load, len(weights)), ou...  18.7 us
    ppermute x17, starting transfers between devices, swap(): return lax.ppermute(x, axis, [(i, (i + k) % size) for i in range(size)])  13.4 us
    ppermute x9, starting transfers between devices, cross(): return lax.ppermute(x, ('parts', 'bal', 'mp'), pairs)  9.87 us
    pallas_call x1, Pallas kernels, body(): sent = send_rows(plan, hist_ids, table_rows, scale)  7.34 us
    pallas_call x1, Pallas kernels, body(): bias = make_bias(table, plan, lengths, time_bucket)  7.02 us
    pallas_call x1, Pallas kernels, body(): own, route = keep_rows(plan1, hist_ids, table_rows, scale)  6.49 us
    pallas_call x1, Pallas kernels, body(): chunk2 = merge(r2, a2, b2, d2)  3.03 us
  transfers between devices with their start and end apart: 26, of which 9 were waited for; matrix products, arithmetic and copies ran while one was open for 1% of the time, Pallas kernels for 23%

profile of v3, /device:TPU:0, one launch (start us, length us, event | category | flops | bytes accessed | tf_op | source)
XLA Modules:
  0.0 109.2 jit_solution(1088110723190616334)
XLA Ops:
  0.5 1.7 %pack.1 = bf16[352,512]{1,0:T(8,128)(2,1)} custom-call(bf16[512,256]{1,0:T(8,128)(2,1)} %refs_0_.1, bf16[4,256,512]{2,1,0:T(8,128)(2,1)} %refs_1_.1, bf16[512,256]{1,0:T(8,128)(2,1)} %refs_2_.1), custom_call_target="tpu_custom_call" | custom-call | tf_op jit(solution)/shard_map/pack/pallas_call | solution.py:523
  2.2 3.1 %collective-permute-start = (bf16[352,512]{1,0:T(8,128)(2,1)}, bf16[352,512]{1,0:T(8,128)(2,1)S(1)}, u32[]{:S(2)}, u32[]{:S(2)}) collective-permute-start(bf16[352,512]{1,0:T(8,128)(2,1)} %pack.1), channel_id=1, source_target_pairs={{0,4},{4,8},{8,12},{12,0},{1,5},{5,9},{9,13},{13,1},{2,6},{6,10},{... | collective-permute-start | bytes 1081352 | tf_op jit(solution)/shard_map/ppermute | solution.py:322
  5.3 7.3 %send_rows.1 = (bf16[256,512]{1,0:T(8,128)(2,1)}, bf16[256,512]{1,0:T(8,128)(2,1)}, bf16[256,512]{1,0:T(8,128)(2,1)}) custom-call(s32[32]{0:T(128)} %plan_ref.6, s32[32,256]{1,0:T(8,128)} %hist_ref.3, bf16[2048,512]{1,0:T(8,128)(2,1)} %table_ref.3, f32[16,128]{1,0:T(8,128)} %bitcast.7), custom_call_target="tpu_custom_call" | custom-call | flops 6300000256 | bytes 14000000 | tf_op jit(solution)/shard_map/send_rows/pallas_call | solution.py:543
  12.7 1.1 %collective-permute-done.1 = f32[4,176]{1,0:T(4,128)S(1)} collective-permute-done((f32[4,176]{1,0:T(4,128)S(1)}, f32[4,176]{1,0:T(4,128)S(1)}, u32[]{:S(2)}, u32[]{:S(2)}) %collective-permute-start.1) | collective-permute-done | bytes 2848 | tf_op jit(solution)/shard_map/ppermute | solution.py:322
  14.6 1.5 %collective-permute-done.refs_0_ = bf16[352,512]{1,0:T(8,128)(2,1)S(1)} collective-permute-done((bf16[352,512]{1,0:T(8,128)(2,1)}, bf16[352,512]{1,0:T(8,128)(2,1)S(1)}, u32[]{:S(2)}, u32[]{:S(2)}) %collective-permute-start) | collective-permute-done | bytes 360480 | tf_op jit(solution)/shard_map/ppermute | solution.py:322
  16.1 1.6 %collective-permute-start.7 = (bf16[352,512]{1,0:T(8,128)(2,1)S(1)}, bf16[352,512]{1,0:T(8,128)(2,1)S(1)}, u32[]{:S(2)}, u32[]{:S(2)}) collective-permute-start(bf16[352,512]{1,0:T(8,128)(2,1)S(1)} %collective-permute-done.refs_0_), channel_id=1, source_target_pairs={{0,16},{1,3},{2,18},{3,1},{16,0},{17,19},{18,2},{19,17},{4,20},{5,... | collective-permute-start | bytes 1081352 | tf_op jit(solution)/shard_map/ppermute | solution.py:331
  17.7 1.5 %collective-permute-start.6 = (bf16[352,512]{1,0:T(8,128)(2,1)S(1)}, bf16[352,512]{1,0:T(8,128)(2,1)S(1)}, u32[]{:S(2)}, u32[]{:S(2)}) collective-permute-start(bf16[352,512]{1,0:T(8,128)(2,1)S(1)} %collective-permute-done.refs_0_), channel_id=1, source_target_pairs={{0,2},{1,17},{2,0},{3,19},{16,18},{17,1},{18,16},{19,3},{4,6},{5,2... | collective-permute-start | bytes 1081352 | tf_op jit(solution)/shard_map/ppermute | solution.py:331
  19.2 1.6 %collective-permute-start.5 = (bf16[256,512]{1,0:T(8,128)(2,1)}, bf16[256,512]{1,0:T(8,128)(2,1)S(1)}, u32[]{:S(2)}, u32[]{:S(2)}) collective-permute-start(bf16[256,512]{1,0:T(8,128)(2,1)} %get-tuple-element.68), channel_id=1, source_target_pairs={{0,4},{4,8},{8,12},{12,0},{1,5},{5,9},{9,13},{13,1},{2,6},{6,10},{... | collective-permute-start | bytes 786440 | tf_op jit(solution)/shard_map/ppermute | solution.py:322
  20.8 7.0 %bias.1.bias_ref = f32[2,8,256,256]{3,2,1,0:T(8,128)} custom-call(f32[8,48]{1,0:T(8,128)} %slice.8.small_ref, s32[32]{0:T(128)} %plan_ref.6, s32[8]{0:T(128)} %lens_ref.3, s32[8,256]{1,0:T(8,128)} %time_ref.1), custom_call_target="tpu_custom_call" | custom-call | flops 6300000256 | bytes 14000000 | tf_op jit(solution)/shard_map/bias/pallas_call | solution.py:551
  27.9 7.7 %collective-permute-done.5.refs_0_ = bf16[256,512]{1,0:T(8,128)(2,1)S(1)} collective-permute-done((bf16[256,512]{1,0:T(8,128)(2,1)}, bf16[256,512]{1,0:T(8,128)(2,1)S(1)}, u32[]{:S(2)}, u32[]{:S(2)}) %collective-permute-start.5) | collective-permute-done | bytes 262176 | tf_op jit(solution)/shard_map/ppermute | solution.py:322
  36.2 0.8 collective-permute-start.10
  37.0 3.8 %collective-permute-start.12 = (bf16[256,512]{1,0:T(8,128)(2,1)S(1)}, bf16[256,512]{1,0:T(8,128)(2,1)S(1)}, u32[]{:S(2)}, u32[]{:S(2)}) collective-permute-start(bf16[256,512]{1,0:T(8,128)(2,1)S(1)} %copy-done.26), channel_id=1, source_target_pairs={{0,12},{4,0},{8,4},{12,8},{1,13},{5,1},{9,5},{13,9},{2,14},{6,2},{... | collective-permute-start | bytes 786440 | tf_op jit(solution)/shard_map/ppermute | solution.py:322
  40.8 1.2 %collective-permute-start.8 = (bf16[352,512]{1,0:T(8,128)(2,1)S(1)}, bf16[352,512]{1,0:T(8,128)(2,1)S(1)}, u32[]{:S(2)}, u32[]{:S(2)}) collective-permute-start(bf16[352,512]{1,0:T(8,128)(2,1)S(1)} %collective-permute-done.7.refs_2_), channel_id=1, source_target_pairs={{0,2},{1,17},{2,0},{3,19},{16,18},{17,1},{18,16},{19,3},{4,6},{5,2... | collective-permute-start | bytes 1081352 | tf_op jit(solution)/shard_map/ppermute | solution.py:331
  42.0 6.5 %keep_rows.1 = (bf16[512,512]{1,0:T(8,128)(2,1)}, bf16[512,768]{1,0:T(8,128)(2,1)}) custom-call(s32[32]{0:T(128)} %plan_ref.6, s32[32,256]{1,0:T(8,128)} %hist_ref.3, bf16[2048,512]{1,0:T(8,128)(2,1)} %table_ref.3, f32[16,128]{1,0:T(8,128)} %bitcast.8), custom_call_target="tpu_custom_call" | custom-call | flops 6300000256 | bytes 14000000 | tf_op jit(solution)/shard_map/keep_rows/pallas_call | solution.py:556
  48.5 1.8 %collective-permute-done.12.refs_2_ = bf16[256,512]{1,0:T(8,128)(2,1)S(1)} collective-permute-done((bf16[256,512]{1,0:T(8,128)(2,1)S(1)}, bf16[256,512]{1,0:T(8,128)(2,1)S(1)}, u32[]{:S(2)}, u32[]{:S(2)}) %collective-permute-start.12) | collective-permute-done | bytes 262176 | tf_op jit(solution)/shard_map/ppermute | solution.py:322
  50.4 0.9 copy-done.23
  51.3 2.5 %merge.2.refs_5_ = bf16[4,352,512]{2,1,0:T(8,128)(2,1)} custom-call(bf16[352,512]{1,0:T(8,128)(2,1)} %copy-done.16, bf16[352,512]{1,0:T(8,128)(2,1)} %copy-done.21, bf16[352,512]{1,0:T(8,128)(2,1)} %copy-done.20, bf16[352,512]{1,0:T(8,128)(2,1)} %copy-done.23), custom_call_target="tpu_custom_call" | custom-call | flops 1800000000 | bytes 4000000 | tf_op jit(solution)/shard_map/merge/pallas_call | solution.py:562
  53.9 1.1 collective-permute-start.15
  55.0 1.5 %collective-permute-start.14 = (bf16[352,512]{1,0:T(8,128)(2,1)S(1)}, bf16[352,512]{1,0:T(8,128)(2,1)S(1)}, u32[]{:S(2)}, u32[]{:S(2)}) collective-permute-start(bf16[352,512]{1,0:T(8,128)(2,1)S(1)} %collective-permute-done.9.refs_9_), channel_id=1, source_target_pairs={{0,16},{1,3},{2,18},{3,1},{16,0},{17,19},{18,2},{19,17},{4,20},{5,... | collective-permute-start | bytes 1081352 | tf_op jit(solution)/shard_map/ppermute | solution.py:331
  57.0 2.4 %collective-permute-start.17 = (bf16[256,512]{1,0:T(8,128)(2,1)S(1)}, bf16[256,512]{1,0:T(8,128)(2,1)S(1)}, u32[]{:S(2)}, u32[]{:S(2)}) collective-permute-start(bf16[256,512]{1,0:T(8,128)(2,1)S(1)} %copy-done.24), channel_id=1, source_target_pairs={{0,8},{4,12},{8,0},{12,4},{1,9},{5,13},{9,1},{13,5},{2,10},{6,14},... | collective-permute-start | bytes 786440 | tf_op jit(solution)/shard_map/ppermute | solution.py:322
  59.4 11.9 %collective-permute-done.17.refs_1_ = bf16[256,512]{1,0:T(8,128)(2,1)S(1)} collective-permute-done((bf16[256,512]{1,0:T(8,128)(2,1)S(1)}, bf16[256,512]{1,0:T(8,128)(2,1)S(1)}, u32[]{:S(2)}, u32[]{:S(2)}) %collective-permute-start.17) | collective-permute-done | bytes 262176 | tf_op jit(solution)/shard_map/ppermute | solution.py:322
  71.4 0.8 copy-done.22
  72.1 3.0 %merge.3.refs_7_ = bf16[4,352,512]{2,1,0:T(8,128)(2,1)} custom-call(bf16[352,512]{1,0:T(8,128)(2,1)} %copy-done.17, bf16[352,512]{1,0:T(8,128)(2,1)} %copy-done.19, bf16[352,512]{1,0:T(8,128)(2,1)} %copy-done.18, bf16[352,512]{1,0:T(8,128)(2,1)} %copy-done.22), custom_call_target="tpu_custom_call" | custom-call | flops 1800000000 | bytes 4000000 | tf_op jit(solution)/shard_map/merge/pallas_call | solution.py:570
  75.3 1.1 collective-permute-start.23
  76.3 2.8 %place_rows.1 = (bf16[256,512]{1,0:T(8,128)(2,1)}, bf16[256,512]{1,0:T(8,128)(2,1)}) custom-call(bf16[512,512]{1,0:T(8,128)(2,1)} %get-tuple-element.81.own_ref, bf16[512,768]{1,0:T(8,128)(2,1)} %get-tuple-element.82.route_ref, bf16[256,512]{1,0:T(8,128)(2,1)} %copy-done.25, bf16[256,512]{1,0:T(8,128)(2,1)} %copy-done.28, bf16[256,512]{1,0:T(8,128)(2,1)} %copy-done.27), custom_call_target="tpu_custom_call" | custom-call | flops 2700000000 | bytes 6000000 | tf_op jit(solution)/shard_map/place_rows/pallas_call | solution.py:568
  80.3 0.9 collective-permute-done.18.got_ref
  81.6 1.2 %collective-permute-done.23.refs_15_ = bf16[352,512]{1,0:T(8,128)(2,1)S(1)} collective-permute-done((bf16[352,512]{1,0:T(8,128)(2,1)S(1)}, bf16[352,512]{1,0:T(8,128)(2,1)S(1)}, u32[]{:S(2)}, u32[]{:S(2)}) %collective-permute-start.23) | collective-permute-done | bytes 360480 | tf_op jit(solution)/shard_map/ppermute | solution.py:331
  82.8 0.7 slice.9.out_gain_ref
  83.5 0.9 collective-permute-done.24.refs_16_
  85.7 18.7 %layer.1 = (bf16[512,512]{1,0:T(8,128)(2,1)}, bf16[512,512]{1,0:T(8,128)(2,1)}) custom-call(s32[32]{0:T(128)} %plan_ref.6, s32[8]{0:T(128)} %lens_ref.3, bf16[256,512]{1,0:T(8,128)(2,1)} %get-tuple-element.95.keep_ref, bf16[256,512]{1,0:T(8,128)(2,1)} %copy-done.12, f32[1,1024]{1,0:T(1,128)} %bitcast.6, f32[8,128]{1,0:T(8,128)} %slice.9.out_gain_ref, ...), custom_call_target="tpu_custom_call" | custom-call | tf_op jit(solution)/shard_map/layer/pallas_call | solution.py:595
  104.6 2.0 %collective-permute-done.25 = bf16[512,512]{1,0:T(8,128)(2,1)S(1)} collective-permute-done((bf16[512,512]{1,0:T(8,128)(2,1)}, bf16[512,512]{1,0:T(8,128)(2,1)S(1)}, u32[]{:S(2)}, u32[]{:S(2)}) %collective-permute-start.25) | collective-permute-done | bytes 524320 | tf_op jit(solution)/shard_map/ppermute | solution.py:322
  106.6 2.6 %maximum_select_fusion = bf16[1024,512]{1,0:T(8,128)(2,1)} fusion(bf16[512,512]{1,0:T(8,128)(2,1)S(1)} %collective-permute-done.25, bf16[512,512]{1,0:T(8,128)(2,1)} %get-tuple-element.109, pred[]{:T(512)S(6)} %eq.4), kind=kLoop, calls=%fused_computation | loop fusion | flops 4718592 | bytes 2097153 | tf_op jit(solution)/shard_map/jit(_where)/select_n | solution.py:616
  (91 shorter events, 5.7 us)
Async XLA Ops:
  0.0 16.1 %collective-permute-start.2 = (bf16[4,256,512]{2,1,0:T(8,128)(2,1)}, bf16[4,256,512]{2,1,0:T(8,128)(2,1)S(1)}, u32[]{:S(2)}, u32[]{:S(2)}) collective-permute-start(bf16[4,256,512]{2,1,0:T(8,128)(2,1)} %refs_1_.1), channel_id=1, source_target_pairs={{0,1},{1,0},{2,3},{3,2},{4,5},{5,4},{6,7},{7,6},{8,9},{9,8},{10,11... | collective-permute-start | bytes 3145736 | tf_op jit(solution)/shard_map/ppermute | solution.py:322
  0.5 14.1 %collective-permute-start.3 = (bf16[512,256]{1,0:T(8,128)(2,1)}, bf16[512,256]{1,0:T(8,128)(2,1)S(1)}, u32[]{:S(2)}, u32[]{:S(2)}) collective-permute-start(bf16[512,256]{1,0:T(8,128)(2,1)} %refs_2_.1), channel_id=1, source_target_pairs={{0,1},{1,0},{2,3},{3,2},{4,5},{5,4},{6,7},{7,6},{8,9},{9,8},{10,11... | collective-permute-start | bytes 786440 | tf_op jit(solution)/shard_map/ppermute | solution.py:322
  2.2 13.9 %collective-permute-start = (bf16[352,512]{1,0:T(8,128)(2,1)}, bf16[352,512]{1,0:T(8,128)(2,1)S(1)}, u32[]{:S(2)}, u32[]{:S(2)}) collective-permute-start(bf16[352,512]{1,0:T(8,128)(2,1)} %pack.1), channel_id=1, source_target_pairs={{0,4},{4,8},{8,12},{12,0},{1,5},{5,9},{9,13},{13,1},{2,6},{6,10},{... | collective-permute-start | bytes 1081352 | tf_op jit(solution)/shard_map/ppermute | solution.py:322
  12.7 1.2 %collective-permute-start.1 = (f32[4,176]{1,0:T(4,128)S(1)}, f32[4,176]{1,0:T(4,128)S(1)}, u32[]{:S(2)}, u32[]{:S(2)}) collective-permute-start(f32[4,176]{1,0:T(4,128)S(1)} %pad_maximum_fusion), channel_id=1, source_target_pairs={{0,1},{1,0},{2,3},{3,2},{4,5},{5,4},{6,7},{7,6},{8,9},{9,8},{10,11... | collective-permute-start | bytes 8456 | tf_op jit(solution)/shard_map/ppermute | solution.py:322
  14.6 22.4 %copy-start.26 = (bf16[256,512]{1,0:T(8,128)(2,1)S(1)}, bf16[256,512]{1,0:T(8,128)(2,1)}, u32[]{:S(2)}) copy-start(bf16[256,512]{1,0:T(8,128)(2,1)} %get-tuple-element.76) | copy-start | bytes 786436
  14.6 13.3 %copy-start.11 = (bf16[512,256]{1,0:T(8,128)(2,1)}, bf16[512,256]{1,0:T(8,128)(2,1)S(1)}, u32[]{:S(2)}) copy-start(bf16[512,256]{1,0:T(8,128)(2,1)S(1)} %collective-permute-done.3.refs_4_) | copy-start | bytes 786436
  16.1 19.5 %collective-permute-start.7 = (bf16[352,512]{1,0:T(8,128)(2,1)S(1)}, bf16[352,512]{1,0:T(8,128)(2,1)S(1)}, u32[]{:S(2)}, u32[]{:S(2)}) collective-permute-start(bf16[352,512]{1,0:T(8,128)(2,1)S(1)} %collective-permute-done.refs_0_), channel_id=1, source_target_pairs={{0,16},{1,3},{2,18},{3,1},{16,0},{17,19},{18,2},{19,17},{4,20},{5,... | collective-permute-start | bytes 1081352 | tf_op jit(solution)/shard_map/ppermute | solution.py:331
  17.7 17.9 %collective-permute-start.6 = (bf16[352,512]{1,0:T(8,128)(2,1)S(1)}, bf16[352,512]{1,0:T(8,128)(2,1)S(1)}, u32[]{:S(2)}, u32[]{:S(2)}) collective-permute-start(bf16[352,512]{1,0:T(8,128)(2,1)S(1)} %collective-permute-done.refs_0_), channel_id=1, source_target_pairs={{0,2},{1,17},{2,0},{3,19},{16,18},{17,1},{18,16},{19,3},{4,6},{5,2... | collective-permute-start | bytes 1081352 | tf_op jit(solution)/shard_map/ppermute | solution.py:331
  19.2 16.4 %collective-permute-start.4 = (bf16[352,512]{1,0:T(8,128)(2,1)S(1)}, bf16[352,512]{1,0:T(8,128)(2,1)S(1)}, u32[]{:S(2)}, u32[]{:S(2)}) collective-permute-start(bf16[352,512]{1,0:T(8,128)(2,1)S(1)} %collective-permute-done.refs_0_), channel_id=1, source_target_pairs={{0,4},{4,8},{8,12},{12,0},{1,5},{5,9},{9,13},{13,1},{2,6},{6,10},{... | collective-permute-start | bytes 1081352 | tf_op jit(solution)/shard_map/ppermute | solution.py:322
  19.2 16.3 %collective-permute-start.5 = (bf16[256,512]{1,0:T(8,128)(2,1)}, bf16[256,512]{1,0:T(8,128)(2,1)S(1)}, u32[]{:S(2)}, u32[]{:S(2)}) collective-permute-start(bf16[256,512]{1,0:T(8,128)(2,1)} %get-tuple-element.68), channel_id=1, source_target_pairs={{0,4},{4,8},{8,12},{12,0},{1,5},{5,9},{9,13},{13,1},{2,6},{6,10},{... | collective-permute-start | bytes 786440 | tf_op jit(solution)/shard_map/ppermute | solution.py:322
  35.6 13.0 %copy-start.25 = (bf16[256,512]{1,0:T(8,128)(2,1)}, bf16[256,512]{1,0:T(8,128)(2,1)S(1)}, u32[]{:S(2)}) copy-start(bf16[256,512]{1,0:T(8,128)(2,1)S(1)} %collective-permute-done.5.refs_0_) | copy-start | bytes 786436
  35.6 13.0 %copy-start.20 = (bf16[352,512]{1,0:T(8,128)(2,1)}, bf16[352,512]{1,0:T(8,128)(2,1)S(1)}, u32[]{:S(2)}) copy-start(bf16[352,512]{1,0:T(8,128)(2,1)S(1)} %collective-permute-done.7.refs_2_) | copy-start | bytes 1081348
  35.6 14.7 %collective-permute-start.11 = (bf16[352,512]{1,0:T(8,128)(2,1)S(1)}, bf16[352,512]{1,0:T(8,128)(2,1)S(1)}, u32[]{:S(2)}, u32[]{:S(2)}) collective-permute-start(bf16[352,512]{1,0:T(8,128)(2,1)S(1)} %collective-permute-done.4.refs_0_), channel_id=1, source_target_pairs={{0,16},{1,3},{2,18},{3,1},{16,0},{17,19},{18,2},{19,17},{4,20},{5,... | collective-permute-start | bytes 1081352 | tf_op jit(solution)/shard_map/ppermute | solution.py:331
  36.2 14.2 %collective-permute-start.10 = (bf16[352,512]{1,0:T(8,128)(2,1)S(1)}, bf16[352,512]{1,0:T(8,128)(2,1)S(1)}, u32[]{:S(2)}, u32[]{:S(2)}) collective-permute-start(bf16[352,512]{1,0:T(8,128)(2,1)S(1)} %collective-permute-done.4.refs_0_), channel_id=1, source_target_pairs={{0,2},{1,17},{2,0},{3,19},{16,18},{17,1},{18,16},{19,3},{4,6},{5,2... | collective-permute-start | bytes 1081352 | tf_op jit(solution)/shard_map/ppermute | solution.py:331
  37.0 13.4 %collective-permute-start.9 = (bf16[352,512]{1,0:T(8,128)(2,1)S(1)}, bf16[352,512]{1,0:T(8,128)(2,1)S(1)}, u32[]{:S(2)}, u32[]{:S(2)}) collective-permute-start(bf16[352,512]{1,0:T(8,128)(2,1)S(1)} %collective-permute-done.4.refs_0_), channel_id=1, source_target_pairs={{0,4},{4,8},{8,12},{12,0},{1,5},{5,9},{9,13},{13,1},{2,6},{6,10},{... | collective-permute-start | bytes 1081352 | tf_op jit(solution)/shard_map/ppermute | solution.py:322
  37.0 13.4 %collective-permute-start.12 = (bf16[256,512]{1,0:T(8,128)(2,1)S(1)}, bf16[256,512]{1,0:T(8,128)(2,1)S(1)}, u32[]{:S(2)}, u32[]{:S(2)}) collective-permute-start(bf16[256,512]{1,0:T(8,128)(2,1)S(1)} %copy-done.26), channel_id=1, source_target_pairs={{0,12},{4,0},{8,4},{12,8},{1,13},{5,1},{9,5},{13,9},{2,14},{6,2},{... | collective-permute-start | bytes 786440 | tf_op jit(solution)/shard_map/ppermute | solution.py:322
  40.8 9.5 %collective-permute-start.8 = (bf16[352,512]{1,0:T(8,128)(2,1)S(1)}, bf16[352,512]{1,0:T(8,128)(2,1)S(1)}, u32[]{:S(2)}, u32[]{:S(2)}) collective-permute-start(bf16[352,512]{1,0:T(8,128)(2,1)S(1)} %collective-permute-done.7.refs_2_), channel_id=1, source_target_pairs={{0,2},{1,17},{2,0},{3,19},{16,18},{17,1},{18,16},{19,3},{4,6},{5,2... | collective-permute-start | bytes 1081352 | tf_op jit(solution)/shard_map/ppermute | solution.py:331
  50.3 24.8 %copy-start.27 = (bf16[256,512]{1,0:T(8,128)(2,1)}, bf16[256,512]{1,0:T(8,128)(2,1)S(1)}, u32[]{:S(2)}) copy-start(bf16[256,512]{1,0:T(8,128)(2,1)S(1)} %collective-permute-done.12.refs_2_) | copy-start | bytes 786436
  50.4 29.5 %copy-start.3 = (bf16[352,512]{1,0:T(8,128)(2,1)}, bf16[352,512]{1,0:T(8,128)(2,1)S(1)}, u32[]{:S(2)}) copy-start(bf16[352,512]{1,0:T(8,128)(2,1)S(1)} %collective-permute-done.9.refs_9_) | copy-start | bytes 1081348
  53.8 17.6 %collective-permute-start.16 = (bf16[4,352,512]{2,1,0:T(8,128)(2,1)}, bf16[4,352,512]{2,1,0:T(8,128)(2,1)S(1)}, u32[]{:S(2)}, u32[]{:S(2)}) collective-permute-start(bf16[4,352,512]{2,1,0:T(8,128)(2,1)} %merge.2.refs_5_), channel_id=1, source_target_pairs={{0,1},{1,0},{2,3},{3,2},{4,5},{5,4},{6,7},{7,6},{8,9},{9,8},{10,11... | collective-permute-start | bytes 4325384 | tf_op jit(solution)/shard_map/ppermute | solution.py:322
  53.9 17.4 %collective-permute-start.15 = (bf16[352,512]{1,0:T(8,128)(2,1)S(1)}, bf16[352,512]{1,0:T(8,128)(2,1)S(1)}, u32[]{:S(2)}, u32[]{:S(2)}) collective-permute-start(bf16[352,512]{1,0:T(8,128)(2,1)S(1)} %collective-permute-done.11.refs_2_), channel_id=1, source_target_pairs={{0,2},{1,17},{2,0},{3,19},{16,18},{17,1},{18,16},{19,3},{4,6},{5,2... | collective-permute-start | bytes 1081352 | tf_op jit(solution)/shard_map/ppermute | solution.py:331
  55.0 16.4 %collective-permute-start.14 = (bf16[352,512]{1,0:T(8,128)(2,1)S(1)}, bf16[352,512]{1,0:T(8,128)(2,1)S(1)}, u32[]{:S(2)}, u32[]{:S(2)}) collective-permute-start(bf16[352,512]{1,0:T(8,128)(2,1)S(1)} %collective-permute-done.9.refs_9_), channel_id=1, source_target_pairs={{0,16},{1,3},{2,18},{3,1},{16,0},{17,19},{18,2},{19,17},{4,20},{5,... | collective-permute-start | bytes 1081352 | tf_op jit(solution)/shard_map/ppermute | solution.py:331
  56.5 14.8 %collective-permute-start.13 = (bf16[352,512]{1,0:T(8,128)(2,1)S(1)}, bf16[352,512]{1,0:T(8,128)(2,1)S(1)}, u32[]{:S(2)}, u32[]{:S(2)}) collective-permute-start(bf16[352,512]{1,0:T(8,128)(2,1)S(1)} %collective-permute-done.9.refs_9_), channel_id=1, source_target_pairs={{0,2},{1,17},{2,0},{3,19},{16,18},{17,1},{18,16},{19,3},{4,6},{5,2... | collective-permute-start | bytes 1081352 | tf_op jit(solution)/shard_map/ppermute | solution.py:331
  57.0 14.3 %collective-permute-start.17 = (bf16[256,512]{1,0:T(8,128)(2,1)S(1)}, bf16[256,512]{1,0:T(8,128)(2,1)S(1)}, u32[]{:S(2)}, u32[]{:S(2)}) collective-permute-start(bf16[256,512]{1,0:T(8,128)(2,1)S(1)} %copy-done.24), channel_id=1, source_target_pairs={{0,8},{4,12},{8,0},{12,4},{1,9},{5,13},{9,1},{13,5},{2,10},{6,14},... | collective-permute-start | bytes 786440 | tf_op jit(solution)/shard_map/ppermute | solution.py:322
  75.2 9.3 %collective-permute-start.19 = (bf16[4,352,512]{2,1,0:T(8,128)(2,1)}, bf16[4,352,512]{2,1,0:T(8,128)(2,1)S(1)}, u32[]{:S(2)}, u32[]{:S(2)}) collective-permute-start(bf16[4,352,512]{2,1,0:T(8,128)(2,1)} %merge.3.refs_7_), channel_id=1, source_target_pairs={{0,1},{1,0},{2,3},{3,2},{4,5},{5,4},{6,7},{7,6},{8,9},{9,8},{10,11... | collective-permute-start | bytes 4325384 | tf_op jit(solution)/shard_map/ppermute | solution.py:322
  75.3 7.5 %collective-permute-start.23 = (bf16[352,512]{1,0:T(8,128)(2,1)S(1)}, bf16[352,512]{1,0:T(8,128)(2,1)S(1)}, u32[]{:S(2)}, u32[]{:S(2)}) collective-permute-start(bf16[352,512]{1,0:T(8,128)(2,1)S(1)} %collective-permute-done.14.refs_13_), channel_id=1, source_target_pairs={{0,2},{1,17},{2,0},{3,19},{16,18},{17,1},{18,16},{19,3},{4,6},{5,2... | collective-permute-start | bytes 1081352 | tf_op jit(solution)/shard_map/ppermute | solution.py:331
  79.2 2.0 %collective-permute-start.18 = (bf16[256,512]{1,0:T(8,128)(2,1)}, bf16[256,512]{1,0:T(8,128)(2,1)S(1)}, u32[]{:S(2)}, u32[]{:S(2)}) collective-permute-start(bf16[256,512]{1,0:T(8,128)(2,1)} %get-tuple-element.96), channel_id=1, source_target_pairs={{0,1},{1,0},{2,3},{3,2},{4,5},{5,4},{6,7},{7,6},{8,9},{9,8},{10,11... | collective-permute-start | bytes 786440 | tf_op jit(solution)/shard_map/ppermute | solution.py:322
  79.8 3.7 %collective-permute-start.22 = (bf16[352,512]{1,0:T(8,128)(2,1)S(1)}, bf16[352,512]{1,0:T(8,128)(2,1)S(1)}, u32[]{:S(2)}, u32[]{:S(2)}) collective-permute-start(bf16[352,512]{1,0:T(8,128)(2,1)S(1)} %collective-permute-done.14.refs_13_), channel_id=1, source_target_pairs={{0,1},{1,0},{2,3},{3,2},{4,5},{5,4},{6,7},{7,6},{8,9},{9,8},{10,11... | collective-permute-start | bytes 1081352 | tf_op jit(solution)/shard_map/ppermute | solution.py:322
  79.9 3.6 %collective-permute-start.20 = (bf16[352,512]{1,0:T(8,128)(2,1)S(1)}, bf16[352,512]{1,0:T(8,128)(2,1)S(1)}, u32[]{:S(2)}, u32[]{:S(2)}) collective-permute-start(bf16[352,512]{1,0:T(8,128)(2,1)S(1)} %collective-permute-done.9.refs_9_), channel_id=1, source_target_pairs={{0,1},{1,0},{2,3},{3,2},{4,5},{5,4},{6,7},{7,6},{8,9},{9,8},{10,11... | collective-permute-start | bytes 1081352 | tf_op jit(solution)/shard_map/ppermute | solution.py:322
  81.2 2.3 %collective-permute-start.21 = (bf16[352,512]{1,0:T(8,128)(2,1)S(1)}, bf16[352,512]{1,0:T(8,128)(2,1)S(1)}, u32[]{:S(2)}, u32[]{:S(2)}) collective-permute-start(bf16[352,512]{1,0:T(8,128)(2,1)S(1)} %collective-permute-done.13.refs_11_), channel_id=1, source_target_pairs={{0,1},{1,0},{2,3},{3,2},{4,5},{5,4},{6,7},{7,6},{8,9},{9,8},{10,11... | collective-permute-start | bytes 1081352 | tf_op jit(solution)/shard_map/ppermute | solution.py:322
  82.8 1.7 %collective-permute-start.24 = (bf16[352,512]{1,0:T(8,128)(2,1)S(1)}, bf16[352,512]{1,0:T(8,128)(2,1)S(1)}, u32[]{:S(2)}, u32[]{:S(2)}) collective-permute-start(bf16[352,512]{1,0:T(8,128)(2,1)S(1)} %collective-permute-done.23.refs_15_), channel_id=1, source_target_pairs={{0,1},{1,0},{2,3},{3,2},{4,5},{5,4},{6,7},{7,6},{8,9},{9,8},{10,11... | collective-permute-start | bytes 1081352 | tf_op jit(solution)/shard_map/ppermute | solution.py:322
  104.4 2.2 %collective-permute-start.25 = (bf16[512,512]{1,0:T(8,128)(2,1)}, bf16[512,512]{1,0:T(8,128)(2,1)S(1)}, u32[]{:S(2)}, u32[]{:S(2)}) collective-permute-start(bf16[512,512]{1,0:T(8,128)(2,1)} %get-tuple-element.110), channel_id=1, source_target_pairs={{0,1},{1,0},{2,3},{3,2},{4,5},{5,4},{6,7},{7,6},{8,9},{9,8},{10,11... | collective-permute-start | bytes 1572872 | tf_op jit(solution)/shard_map/ppermute | solution.py:322
  (23 other events, 122.1 us)

commit v4 on v3

--- a/solution.py
+++ b/solution.py
@@ -11,7 +11,7 @@
 epsilon = 1e-05
 BF = jnp.bfloat16
 F32 = jnp.float32
-VMEM_BYTES = 56 * 1024 * 1024
+MIB = 1024 * 1024
 FAR = -1e30
 
 
@@ -31,8 +31,8 @@
     return pl.BlockSpec(memory_space=pltpu.SMEM)
 
 
-def params():
-    return pltpu.CompilerParams(vmem_limit_bytes=VMEM_BYTES)
+def params(mib):
+    return pltpu.CompilerParams(vmem_limit_bytes=mib * MIB)
 
 
 def iota(shape, axis):
@@ -234,16 +234,17 @@
 
 
 def layer_kernel(
-    z, load, n_weights, plan_ref, lens_ref, keep_ref, got_ref, gain_ref, out_gain_ref, bias_ref, *refs
+    z, load, n_weights, plan_ref, lens_ref, keep_ref, got_ref, gain_ref, out_gain_ref, bias_hbm, *refs
 ):
     weights = refs[:n_weights]
     own_out, give_out = refs[n_weights : n_weights + 2]
-    (e_ref, w_ref, o_ref, emb_ref, x_ref, xn_ref, act_ref, y_ref, z_ref, sems) = refs[n_weights + 2 :]
+    (e_ref, w_ref, o_ref, emb_ref, x_ref, xn_ref, act_ref, y_ref, z_ref, bias_ref, sems) = refs[n_weights + 2 :]
     table_pos = lax.axis_index("table")
     bal_pos = lax.axis_index("bal")
     mp_pos = lax.axis_index("mp")
     width = x_ref.shape[1]
     copies = load(weights, e_ref, w_ref, o_ref, sems)
+    copies.insert(5, [pltpu.make_async_copy(bias_hbm, bias_ref, sems.at[6])])
     for group in copies:
         for c in group:
             c.start()
@@ -266,18 +267,20 @@
         centred = x - mean
         var = jnp.mean(centred * centred, axis=1, keepdims=True)
         xn_ref[rows, :] = (centred * lax.rsqrt(var + epsilon) * gain_ref[...]).astype(BF)
-    for c in copies[1]:
+    step = 256
+    for part in range(4):
+        for c in copies[1 + part]:
+            c.wait()
+
+        def project(nb, carry):
+            cols = pl.ds(pl.multiple_of(nb * step, step), step)
+            s = dot(xn_ref[...], w_ref[part, :, cols])
+            act_ref[part, :, cols] = silu(s).astype(BF)
+            return carry
+
+        lax.fori_loop(0, width // step, project, 0, unroll=True)
+    for c in copies[5]:
         c.wait()
-    step = 256
-
-    def project(i, carry):
-        c, nb = i // (width // step), i % (width // step)
-        cols = pl.ds(pl.multiple_of(nb * step, step), step)
-        s = dot(xn_ref[...], w_ref[c, :, cols])
-        act_ref[c, :, cols] = silu(s).astype(BF)
-        return carry
-
-    lax.fori_loop(0, 4 * (width // step), project, 0, unroll=2)
     scale = 1.0 / math.sqrt(width // z.heads)
     size = width // z.heads
     for u in range(z.mine):
@@ -306,7 +309,7 @@
             cols = slice(h * size, (h + 1) * size)
             normed = (y_ref[rows, cols] - mean) * factor * out_gain_ref[h : h + 1, :]
             z_ref[rows, cols] = (normed * act_ref[0, rows, cols].astype(F32)).astype(BF)
-    for c in copies[2]:
+    for c in copies[6]:
         c.wait()
     out_cols = width // z.mp
     for which, ref in ((1 - mp_pos, give_out), (mp_pos, own_out)):
@@ -331,6 +334,10 @@
     return lax.ppermute(x, ("parts", "bal", "mp"), pairs)
 
 
+def corner(x):
+    return lax.ppermute(x, ("parts", "bal"), [(i, 3 - i) for i in range(4)])
+
+
 def pack_kernel(e_ref, w_ref, o_ref, out_ref, sems):
     q = lax.axis_index("parts") * 2 + lax.axis_index("bal")
     m = lax.axis_index("mp")
@@ -342,9 +349,6 @@
 
     def add(src, dst):
         copies.append(pltpu.make_async_copy(src, dst, sems))
-
-    def at(x, size):
-        return pl.ds(pl.multiple_of(x * size, size), size)
 
     for c in range(4):
         add(w_ref.at[c, at(q, share), :], out_ref.at[c * share : (c + 1) * share, :])
@@ -371,6 +375,10 @@
         c.wait()
 
 
+def at(x, size):
+    return pl.ds(pl.multiple_of(x * size, size), size)
+
+
 def load_pieces(z):
     def load(refs, e_ref, w_ref, o_ref, sems):
         t, m = lax.axis_index("table"), lax.axis_index("mp")
@@ -379,29 +387,17 @@
         deep, cols = w_own.shape[1], w_own.shape[2]
         e_cols = e_own.shape[1]
         o_rows = o_own.shape[0]
-        groups = [[], [], []]
-
-        def add(g, src, dst):
-            groups[g].append(pltpu.make_async_copy(src, dst, sems.at[g]))
-
-        def at(x, size):
-            return pl.ds(pl.multiple_of(x * size, size), size)
-
-        add(0, e_own, e_ref.at[:, at(t, e_cols)])
-        for core, w, o in ((m, w_own, o_own), (1 - m, w_near, o_near)):
-            add(1, w, w_ref.at[:, at(t, deep), at(core, cols)])
-            add(2, o, o_ref.at[at(core, o_rows), at(t, e_cols)])
         share = deep // 4
         e_part = e_ref.shape[0] // 16
         o_part = o_rows // 8
         first = 4 * share
         along_b, along_p = p * 2 + 1 - b, (1 - p) * 2 + b
+        pieces = []
         for k in range(1, z.n):
             source = lax.rem(t + z.n - k, z.n)
-            block = refs[9:]
-            if k < 3:
-                both = refs[5 + (k - 1) * 2 : 5 + k * 2]
-                block = [ref.at[i] for i in range(4) for ref in both]
+            block = refs[PIECES[k - 1] : PIECES[k]]
+            if len(block) == 2:
+                block = [ref.at[i] for i in range(4) for ref in block]
             for i in range(4):
                 for core, ref in ((m, block[2 * i]), (1 - m, block[2 * i + 1])):
                     q = (
@@ -410,34 +406,58 @@
                         jnp.where(core == 0, along_p, along_b),
                         (1 - p) * 2 + 1 - b,
                     )[i]
-                    for c in range(4):
-                        add(
-                            1,
-                            ref.at[c * share : (c + 1) * share, :],
-                            w_ref.at[c, at(source * 4 + q, share), at(core, cols)],
-                        )
-                    for j in range(2):
-                        lanes = slice(j * e_cols, (j + 1) * e_cols)
-                        add(
-                            0,
-                            ref.at[first : first + e_part, lanes],
-                            e_ref.at[at((q * 2 + core) * 2 + j, e_part), at(source, e_cols)],
-                        )
-                        add(
-                            2,
-                            ref.at[first + e_part : first + e_part + o_part, lanes],
-                            o_ref.at[at(core * 8 + q * 2 + j, o_part), at(source, e_cols)],
-                        )
+                    pieces.append((ref, source, q, core))
+        groups = [[] for _ in range(6)]
+
+        def add(g, src, dst):
+            groups[g].append(pltpu.make_async_copy(src, dst, sems.at[g]))
+
+        add(0, e_own, e_ref.at[:, at(t, e_cols)])
+        for ref, source, q, core in pieces:
+            for j in range(2):
+                lanes = slice(j * e_cols, (j + 1) * e_cols)
+                rows = at((q * 2 + core) * 2 + j, e_part)
+                add(0, ref.at[first : first + e_part, lanes], e_ref.at[rows, at(source, e_cols)])
+        for c in range(4):
+            for core, w in ((m, w_own), (1 - m, w_near)):
+                add(1 + c, w.at[c], w_ref.at[c, at(t, deep), at(core, cols)])
+            for ref, source, q, core in pieces:
+                add(
+                    1 + c,
+                    ref.at[c * share : (c + 1) * share, :],
+                    w_ref.at[c, at(source * 4 + q, share), at(core, cols)],
+                )
+        for core, o in ((m, o_own), (1 - m, o_near)):
+            add(5, o, o_ref.at[at(core, o_rows), at(t, e_cols)])
+        for ref, source, q, core in pieces:
+            for j in range(2):
+                lanes = slice(j * e_cols, (j + 1) * e_cols)
+                rows = at(core * 8 + q * 2 + j, o_part)
+                add(
+                    5,
+                    ref.at[first + e_part : first + e_part + o_part, lanes],
+                    o_ref.at[rows, at(source, e_cols)],
+                )
         return groups
 
     return load
 
 
 def load_whole(refs, e_ref, w_ref, o_ref, sems):
-    return [
-        [pltpu.make_async_copy(src, dst, sems.at[i])]
-        for i, (src, dst) in enumerate(zip(refs, (e_ref, w_ref, o_ref)))
-    ]
+    e, w, o = refs
+    groups = [[pltpu.make_async_copy(e, e_ref, sems.at[0])]]
+    groups += [[pltpu.make_async_copy(w.at[c], w_ref.at[c], sems.at[1 + c])] for c in range(4)]
+    return groups + [[pltpu.make_async_copy(o, o_ref, sems.at[5])]]
+
+
+def finish_kernel(own_ref, got_ref, out_ref):
+    mp_pos = lax.axis_index("mp")
+    tokens = own_ref.shape[0]
+    out_ref[at(mp_pos, tokens), :] = own_ref[...]
+    out_ref[at(1 - mp_pos, tokens), :] = got_ref[...]
+
+
+PIECES = (5, 7, 9, 17)
 
 
 def body(
@@ -466,7 +486,7 @@
         in_specs=[sspec(), vspec(), vspec(), vspec()],
         out_specs=[vspec()] * (z.n - 1),
         scratch_shapes=[pltpu.VMEM((z.rows, z.width), BF)],
-        compiler_params=params(),
+        compiler_params=params(20),
         cost_estimate=cost(7),
         name="send_rows",
     )
@@ -479,7 +499,7 @@
         in_specs=[sspec(), vspec(), vspec(), vspec()],
         out_specs=[vspec()] * 2,
         scratch_shapes=[pltpu.VMEM((z.rows, z.width), BF)],
-        compiler_params=params(),
+        compiler_params=params(20),
         cost_estimate=cost(7),
         name="keep_rows",
     )
@@ -489,7 +509,7 @@
         out_shape=jax.ShapeDtypeStruct((z.mine, z.heads, z.length, z.length), F32),
         in_specs=[sspec(), sspec(), sspec(), vspec()],
         out_specs=vspec(),
-        compiler_params=params(),
+        compiler_params=params(14),
         cost_estimate=cost(7),
         name="bias",
     )
@@ -498,7 +518,7 @@
         out_shape=[jax.ShapeDtypeStruct((z.tokens // z.mp, z.width), BF)] * 2,
         in_specs=[vspec()] * (z.n + 1),
         out_specs=[vspec()] * 2,
-        compiler_params=params(),
+        compiler_params=params(12),
         cost_estimate=cost(3),
         name="place_rows",
     )
@@ -523,10 +543,10 @@
         pack = pl.pallas_call(
             pack_kernel,
             out_shape=jax.ShapeDtypeStruct((rows, qkvu_proj.shape[2]), BF),
-            in_specs=[pl.BlockSpec(memory_space=pl.ANY)] * 3,
+            in_specs=[pl.BlockSpec(memory_space=pltpu.HBM)] * 3,
             out_specs=vspec(),
             scratch_shapes=[pltpu.SemaphoreType.DMA],
-            compiler_params=params(),
+            compiler_params=params(4),
             name="pack",
         )(embed_proj, qkvu_proj, out_proj)
         merge = pl.pallas_call(
@@ -535,7 +555,7 @@
             in_specs=[pl.BlockSpec(memory_space=pl.ANY)] * 4,
             out_specs=vspec(),
             scratch_shapes=[pltpu.SemaphoreType.DMA],
-            compiler_params=params(),
+            compiler_params=params(6),
             cost_estimate=cost(2),
             name="merge",
         )
@@ -545,33 +565,33 @@
         sent, small_in = fence(sent, (pos_bias, time_bias, out_gain))
         table, gains = biases(*small_in)
         r1, sent, table, w_near, o_near = fence(r1, sent, table, w_near, o_near)
+        b1, a1 = cross(r1, False), cross(r1, True)
+        got1 = swap(sent[0], "table", z.n, 1)
         r2 = hop(r1)
-        got1 = swap(sent[0], "table", z.n, 1)
-        a1, b1 = cross(r1, True), cross(r1, False)
         bias = make_bias(table, plan, lengths, time_bucket)
-        r1, r2, got1, a1, b1, bias, sent, plan1 = fence(r1, r2, got1, a1, b1, bias, sent, plan)
+        r1, r2, got1, a1, b1, bias, sent, plan1, gains = fence(
+            r1, r2, got1, a1, b1, bias, sent, plan, gains
+        )
+        b2, a2, d1 = cross(r2, False), cross(r2, True), cross(b1, True)
+        got3 = swap(sent[2], "table", z.n, 3)
         r3 = hop(r2)
-        got3 = swap(sent[2], "table", z.n, 3)
-        a2, b2, d1 = cross(r2, True), cross(r2, False), cross(b1, True)
         own, route = keep_rows(plan1, hist_ids, table_rows, scale)
         r1, a1, b1, d1, r2, r3, a2, b2, got3, own, route, sent = fence(
             r1, a1, b1, d1, r2, r3, a2, b2, got3, own, route, sent
         )
+        a3, b3, d2 = cross(r3, True), cross(r3, False), cross(b2, True)
         got2 = swap(sent[1], "table", z.n, 2)
-        a3, b3, d2 = cross(r3, True), cross(r3, False), cross(b2, True)
         chunk1 = merge(r1, a1, b1, d1)
         near1 = near(chunk1)
-        a3, b3, d2, chunk1, near1, got2, r2, a2, b2, r3 = fence(
-            a3, b3, d2, chunk1, near1, got2, r2, a2, b2, r3
-        )
+        a3, b3, r2, a2, b2, d2, near1, got2, r3 = fence(a3, b3, r2, a2, b2, d2, near1, got2, r3)
         d3 = cross(b3, True)
         keep, give = place_rows(own, route, got1, got2, got3)
         back = near(give)
         chunk2 = merge(r2, a2, b2, d2)
         near2 = near(chunk2)
+        r3n, a3n, b3n = near(r3), near(a3), near(b3)
         weights = [embed_proj, qkvu_proj, out_proj, w_near, o_near, chunk1, near1, chunk2, near2]
-        for v in (r3, a3, b3, d3):
-            weights += [v, near(v)]
+        weights += [r3, r3n, a3, a3n, b3, b3n, d3, near(d3)]
         load = load_pieces(z)
     else:
         table, gains = biases(pos_bias, time_bias, out_gain)
@@ -595,7 +615,9 @@
     out_own, out_give = pl.pallas_call(
         functools.partial(layer_kernel, z, load, len(weights)),
         out_shape=[jax.ShapeDtypeStruct((tokens, out_cols), BF)] * 2,
-        in_specs=[sspec(), sspec()] + [vspec()] * 5 + [pl.BlockSpec(memory_space=pl.ANY)] * len(weights),
+        in_specs=[sspec(), sspec()]
+        + [vspec()] * 4
+        + [pl.BlockSpec(memory_space=pl.ANY)] * (1 + len(weights)),
         out_specs=[vspec()] * 2,
         scratch_shapes=[
             pltpu.VMEM((z.width, width), BF),
@@ -607,17 +629,21 @@
             pltpu.VMEM((4, tokens, width), BF),
             pltpu.VMEM((tokens, width), F32),
             pltpu.VMEM((tokens, width), BF),
-            pltpu.SemaphoreType.DMA((3,)),
+            pltpu.VMEM(bias.shape, F32),
+            pltpu.SemaphoreType.DMA((7,)),
         ],
-        compiler_params=params(),
+        compiler_params=params(44),
         name="layer",
     )(plan, lengths, keep, back, in_gain.reshape(1, width), gains, bias, *weights)
     out_got = swap(out_give, "mp", z.mp)
-    out = jnp.where(
-        mp_pos == 0,
-        jnp.concatenate([out_own, out_got], 0),
-        jnp.concatenate([out_got, out_own], 0),
-    )
+    out = pl.pallas_call(
+        finish_kernel,
+        out_shape=jax.ShapeDtypeStruct((z.mp * tokens, out_cols), BF),
+        in_specs=[vspec()] * 2,
+        out_specs=vspec(),
+        compiler_params=params(8),
+        name="finish",
+    )(out_own, out_got)
     return out.reshape(z.pair, z.length, out_cols)
 
 

time: 110 us -> 98.8 us (0.90)
  Pallas kernels: 49.6 us -> 32.7 us
  waiting for transfers between devices: 29 us -> 34.7 us
  local copies, waits for them, and re-layouts: 4.23 us -> 7.91 us
  other arithmetic: 2.75 us -> 0.15 us
    unnamed x58 -> x40, local copies, waits for them, and re-layouts: 2.9 us -> 7.84 us
    pallas_call x1, Pallas kernels: 18.7 us -> 14.5 us  [body(): pl.pallas_call(functools.partial(layer_kernel, z, load, len(weights)), ou...]
    ppermute x17, waiting for transfers between devices: 27.8 us -> 31.1 us  [swap(): return lax.ppermute(x, axis, [(i, (i + k) % size) for i in range(size)])]
    select_n x1 -> x0, other arithmetic: 2.6 us -> none  [body(): jnp.where(mp_pos == 0, jnp.concatenate([out_own, out_got], 0), jnp.concat...]
    pallas_call x1, Pallas kernels: 3.03 us -> 0.59 us  [body(): chunk2 = merge(r2, a2, b2, d2)]
    ppermute x9, waiting for transfers between devices: 1.2 us -> 3.59 us  [cross(): return lax.ppermute(x, ('parts', 'bal', 'mp'), pairs)]
    pallas_call x1, Pallas kernels: 2.83 us -> 0.57 us  [body(): keep, give = place_rows(own, route, got1, got2, got3)]
    pallas_call x1, Pallas kernels: 7.02 us -> 4.93 us  [body(): bias = make_bias(table, plan, lengths, time_bucket)]
  transfers between devices with their start and end apart: 26 -> 26, of which waited for: 9 -> 9; matrix products, arithmetic and copies ran while one was open for 1% -> 0% of each run, Pallas kernels for 23% -> 16%
where the time goes in v4:
time: 98.8 us; the launch traced here: 98.6 us
  waiting for transfers between devices  34.7 us (35%)
  Pallas kernels  32.7 us (33%)
  starting transfers between devices  22.9 us (23%)
  local copies, waits for them, and re-layouts  7.91 us (8%)
    ppermute x17, waiting for transfers between devices, swap(): return lax.ppermute(x, axis, [(i, (i + k) % size) for i in range(size)])  31.1 us
    pallas_call x1, Pallas kernels, body(): pl.pallas_call(functools.partial(layer_kernel, z, load, len(weights)), ou...  14.5 us
    ppermute x17, starting transfers between devices, swap(): return lax.ppermute(x, axis, [(i, (i + k) % size) for i in range(size)])  13.1 us
    ppermute x9, starting transfers between devices, cross(): return lax.ppermute(x, ('parts', 'bal', 'mp'), pairs)  9.73 us
    unnamed x40, local copies, waits for them, and re-layouts  7.84 us
    pallas_call x1, Pallas kernels, body(): sent = send_rows(plan, hist_ids, table_rows, scale)  5.53 us
    pallas_call x1, Pallas kernels, body(): bias = make_bias(table, plan, lengths, time_bucket)  4.93 us
    pallas_call x1, Pallas kernels, body(): own, route = keep_rows(plan1, hist_ids, table_rows, scale)  4.54 us
  transfers between devices with their start and end apart: 26, of which 9 were waited for; matrix products, arithmetic and copies ran while one was open for 0% of the time, Pallas kernels for 16%

profile of v4, /device:TPU:0, one launch (start us, length us, event | category | flops | bytes accessed | tf_op | source)
XLA Modules:
  0.0 98.6 jit_solution(5506398853073882623)
XLA Ops:
  0.5 1.2 %copy-done.1 = bf16[4,256,512]{2,1,0:T(8,128)(2,1)S(1)} copy-done((bf16[4,256,512]{2,1,0:T(8,128)(2,1)S(1)}, bf16[4,256,512]{2,1,0:T(8,128)(2,1)}, u32[]{:S(2)}) %copy-start.1) | copy-done | bytes 1048600
  1.7 0.9 copy-done.4
  2.7 0.9 copy-done.6
  4.0 3.1 %collective-permute-start = (bf16[352,512]{1,0:T(8,128)(2,1)S(1)}, bf16[352,512]{1,0:T(8,128)(2,1)S(1)}, u32[]{:S(2)}, u32[]{:S(2)}) collective-permute-start(bf16[352,512]{1,0:T(8,128)(2,1)S(1)} %pack.1), channel_id=1, source_target_pairs={{0,4},{4,8},{8,12},{12,0},{1,5},{5,9},{9,13},{13,1},{2,6},{6,10},{... | collective-permute-start | bytes 1081352 | tf_op jit(solution)/shard_map/ppermute | solution.py:325
  7.1 1.6 %copy-done.11 = bf16[2048,512]{1,0:T(8,128)(2,1)S(1)} copy-done((bf16[2048,512]{1,0:T(8,128)(2,1)S(1)}, bf16[2048,512]{1,0:T(8,128)(2,1)}, u32[]{:S(2)}) %copy-start.11) | copy-done | bytes 2097176
  8.7 5.5 %send_rows.1 = (bf16[256,512]{1,0:T(8,128)(2,1)S(1)}, bf16[256,512]{1,0:T(8,128)(2,1)S(1)}, bf16[256,512]{1,0:T(8,128)(2,1)S(1)}) custom-call(s32[32]{0:T(128)S(1)} %copy-done.9, s32[32,256]{1,0:T(8,128)S(1)} %copy-done.13, bf16[2048,512]{1,0:T(8,128)(2,1)S(1)} %copy-done.11, f32[16,128]{1,0:T(8,128)S(1)} %bitcast.5), custom_call_target="tpu_custom_call" | custom-call | flops 6300000256 | bytes 14000000 | tf_op jit(solution)/shard_map/send_rows/pallas_call | solution.py:563
  14.4 1.1 %collective-permute-done.1 = f32[4,176]{1,0:T(4,128)S(1)} collective-permute-done((f32[4,176]{1,0:T(4,128)S(1)}, f32[4,176]{1,0:T(4,128)S(1)}, u32[]{:S(2)}, u32[]{:S(2)}) %collective-permute-start.1) | collective-permute-done | bytes 2848 | tf_op jit(solution)/shard_map/ppermute | solution.py:325
  15.7 2.0 %collective-permute-done.refs_0_ = bf16[352,512]{1,0:T(8,128)(2,1)S(1)} collective-permute-done((bf16[352,512]{1,0:T(8,128)(2,1)S(1)}, bf16[352,512]{1,0:T(8,128)(2,1)S(1)}, u32[]{:S(2)}, u32[]{:S(2)}) %collective-permute-start) | collective-permute-done | bytes 360480 | tf_op jit(solution)/shard_map/ppermute | solution.py:325
  17.7 1.5 %collective-permute-start.7 = (bf16[352,512]{1,0:T(8,128)(2,1)S(1)}, bf16[352,512]{1,0:T(8,128)(2,1)S(1)}, u32[]{:S(2)}, u32[]{:S(2)}) collective-permute-start(bf16[352,512]{1,0:T(8,128)(2,1)S(1)} %collective-permute-done.refs_0_), channel_id=1, source_target_pairs={{0,16},{1,3},{2,18},{3,1},{16,0},{17,19},{18,2},{19,17},{4,20},{5,... | collective-permute-start | bytes 1081352 | tf_op jit(solution)/shard_map/ppermute | solution.py:334
  19.2 1.5 %collective-permute-start.6 = (bf16[352,512]{1,0:T(8,128)(2,1)S(1)}, bf16[352,512]{1,0:T(8,128)(2,1)S(1)}, u32[]{:S(2)}, u32[]{:S(2)}) collective-permute-start(bf16[352,512]{1,0:T(8,128)(2,1)S(1)} %collective-permute-done.refs_0_), channel_id=1, source_target_pairs={{0,2},{1,17},{2,0},{3,19},{16,18},{17,1},{18,16},{19,3},{4,6},{5,2... | collective-permute-start | bytes 1081352 | tf_op jit(solution)/shard_map/ppermute | solution.py:334
  20.7 1.3 %collective-permute-start.5 = (bf16[256,512]{1,0:T(8,128)(2,1)S(1)}, bf16[256,512]{1,0:T(8,128)(2,1)S(1)}, u32[]{:S(2)}, u32[]{:S(2)}) collective-permute-start(bf16[256,512]{1,0:T(8,128)(2,1)S(1)} %get-tuple-element.68), channel_id=1, source_target_pairs={{0,4},{4,8},{8,12},{12,0},{1,5},{5,9},{9,13},{13,1},{2,6},{6,10},{... | collective-permute-start | bytes 786440 | tf_op jit(solution)/shard_map/ppermute | solution.py:325
  22.0 4.9 %bias.1.bias_hbm = f32[2,8,256,256]{3,2,1,0:T(8,128)S(1)} custom-call(f32[8,48]{1,0:T(8,128)S(1)} %slice.8.small_ref, s32[32]{0:T(128)S(1)} %copy-done.9, s32[8]{0:T(128)S(1)} %copy-done.10, s32[8,256]{1,0:T(8,128)S(1)} %copy-done.14), custom_call_target="tpu_custom_call" | custom-call | flops 6300000256 | bytes 14000000 | tf_op jit(solution)/shard_map/bias/pallas_call | solution.py:571
  27.0 1.9 %copy-done = f32[2,8,256,256]{3,2,1,0:T(8,128)} copy-done((f32[2,8,256,256]{3,2,1,0:T(8,128)}, f32[2,8,256,256]{3,2,1,0:T(8,128)S(1)}, u32[]{:S(2)}) %copy-start) | copy-done | bytes 4194328
  28.9 8.2 %collective-permute-done.5.refs_0_ = bf16[256,512]{1,0:T(8,128)(2,1)S(1)} collective-permute-done((bf16[256,512]{1,0:T(8,128)(2,1)S(1)}, bf16[256,512]{1,0:T(8,128)(2,1)S(1)}, u32[]{:S(2)}, u32[]{:S(2)}) %collective-permute-start.5) | collective-permute-done | bytes 262176 | tf_op jit(solution)/shard_map/ppermute | solution.py:325
  37.7 0.8 collective-permute-start.10
  38.5 3.8 %collective-permute-start.12 = (bf16[256,512]{1,0:T(8,128)(2,1)S(1)}, bf16[256,512]{1,0:T(8,128)(2,1)S(1)}, u32[]{:S(2)}, u32[]{:S(2)}) collective-permute-start(bf16[256,512]{1,0:T(8,128)(2,1)S(1)} %get-tuple-element.76), channel_id=1, source_target_pairs={{0,12},{4,0},{8,4},{12,8},{1,13},{5,1},{9,5},{13,9},{2,14},{6,2},{... | collective-permute-start | bytes 786440 | tf_op jit(solution)/shard_map/ppermute | solution.py:325
  42.3 1.2 %collective-permute-start.8 = (bf16[352,512]{1,0:T(8,128)(2,1)S(1)}, bf16[352,512]{1,0:T(8,128)(2,1)S(1)}, u32[]{:S(2)}, u32[]{:S(2)}) collective-permute-start(bf16[352,512]{1,0:T(8,128)(2,1)S(1)} %collective-permute-done.7.refs_2_), channel_id=1, source_target_pairs={{0,2},{1,17},{2,0},{3,19},{16,18},{17,1},{18,16},{19,3},{4,6},{5,2... | collective-permute-start | bytes 1081352 | tf_op jit(solution)/shard_map/ppermute | solution.py:334
  43.6 4.5 %keep_rows.1 = (bf16[512,512]{1,0:T(8,128)(2,1)S(1)}, bf16[512,768]{1,0:T(8,128)(2,1)S(1)}) custom-call(s32[32]{0:T(128)S(1)} %copy-done.9, s32[32,256]{1,0:T(8,128)S(1)} %copy-done.13, bf16[2048,512]{1,0:T(8,128)(2,1)S(1)} %copy-done.12, f32[16,128]{1,0:T(8,128)S(1)} %bitcast.6), custom_call_target="tpu_custom_call" | custom-call | flops 6300000256 | bytes 14000000 | tf_op jit(solution)/shard_map/keep_rows/pallas_call | solution.py:578
  48.1 3.7 %collective-permute-done.12.refs_2_ = bf16[256,512]{1,0:T(8,128)(2,1)S(1)} collective-permute-done((bf16[256,512]{1,0:T(8,128)(2,1)S(1)}, bf16[256,512]{1,0:T(8,128)(2,1)S(1)}, u32[]{:S(2)}, u32[]{:S(2)}) %collective-permute-start.12) | collective-permute-done | bytes 262176 | tf_op jit(solution)/shard_map/ppermute | solution.py:325
  52.5 1.1 %collective-permute-start.15 = (bf16[352,512]{1,0:T(8,128)(2,1)S(1)}, bf16[352,512]{1,0:T(8,128)(2,1)S(1)}, u32[]{:S(2)}, u32[]{:S(2)}) collective-permute-start(bf16[352,512]{1,0:T(8,128)(2,1)S(1)} %collective-permute-done.11.refs_2_), channel_id=1, source_target_pairs={{0,2},{1,17},{2,0},{3,19},{16,18},{17,1},{18,16},{19,3},{4,6},{5,2... | collective-permute-start | bytes 1081352 | tf_op jit(solution)/shard_map/ppermute | solution.py:334
  53.6 1.5 %collective-permute-start.14 = (bf16[352,512]{1,0:T(8,128)(2,1)S(1)}, bf16[352,512]{1,0:T(8,128)(2,1)S(1)}, u32[]{:S(2)}, u32[]{:S(2)}) collective-permute-start(bf16[352,512]{1,0:T(8,128)(2,1)S(1)} %collective-permute-done.9.refs_9_), channel_id=1, source_target_pairs={{0,16},{1,3},{2,18},{3,1},{16,0},{17,19},{18,2},{19,17},{4,20},{5,... | collective-permute-start | bytes 1081352 | tf_op jit(solution)/shard_map/ppermute | solution.py:334
  55.7 2.4 %collective-permute-start.17 = (bf16[256,512]{1,0:T(8,128)(2,1)S(1)}, bf16[256,512]{1,0:T(8,128)(2,1)S(1)}, u32[]{:S(2)}, u32[]{:S(2)}) collective-permute-start(bf16[256,512]{1,0:T(8,128)(2,1)S(1)} %get-tuple-element.92), channel_id=1, source_target_pairs={{0,8},{4,12},{8,0},{12,4},{1,9},{5,13},{9,1},{13,5},{2,10},{6,14},... | collective-permute-start | bytes 786440 | tf_op jit(solution)/shard_map/ppermute | solution.py:325
  58.1 11.9 %collective-permute-done.17.refs_1_ = bf16[256,512]{1,0:T(8,128)(2,1)S(1)} collective-permute-done((bf16[256,512]{1,0:T(8,128)(2,1)S(1)}, bf16[256,512]{1,0:T(8,128)(2,1)S(1)}, u32[]{:S(2)}, u32[]{:S(2)}) %collective-permute-start.17) | collective-permute-done | bytes 262176 | tf_op jit(solution)/shard_map/ppermute | solution.py:325
  70.7 1.0 %collective-permute-start.23 = (bf16[352,512]{1,0:T(8,128)(2,1)S(1)}, bf16[352,512]{1,0:T(8,128)(2,1)S(1)}, u32[]{:S(2)}, u32[]{:S(2)}) collective-permute-start(bf16[352,512]{1,0:T(8,128)(2,1)S(1)} %collective-permute-done.14.refs_13_), channel_id=1, source_target_pairs={{0,2},{1,17},{2,0},{3,19},{16,18},{17,1},{18,16},{19,3},{4,6},{5,2... | collective-permute-start | bytes 1081352 | tf_op jit(solution)/shard_map/ppermute | solution.py:334
  72.3 0.8 collective-permute-start.18
  73.6 0.7 collective-permute-done.18.got_ref
  74.6 3.6 %collective-permute-done.23.refs_15_ = bf16[352,512]{1,0:T(8,128)(2,1)S(1)} collective-permute-done((bf16[352,512]{1,0:T(8,128)(2,1)S(1)}, bf16[352,512]{1,0:T(8,128)(2,1)S(1)}, u32[]{:S(2)}, u32[]{:S(2)}) %collective-permute-start.23) | collective-permute-done | bytes 360480 | tf_op jit(solution)/shard_map/ppermute | solution.py:334
  78.2 1.7 %collective-permute-done.24.refs_16_ = bf16[352,512]{1,0:T(8,128)(2,1)S(1)} collective-permute-done((bf16[352,512]{1,0:T(8,128)(2,1)S(1)}, bf16[352,512]{1,0:T(8,128)(2,1)S(1)}, u32[]{:S(2)}, u32[]{:S(2)}) %collective-permute-start.24) | collective-permute-done | bytes 360480 | tf_op jit(solution)/shard_map/ppermute | solution.py:325
  79.9 1.1 %copy-done.16 = bf16[4,352,512]{2,1,0:T(8,128)(2,1)} copy-done((bf16[4,352,512]{2,1,0:T(8,128)(2,1)}, bf16[4,352,512]{2,1,0:T(8,128)(2,1)S(1)}, u32[]{:S(2)}) %copy-start.16) | copy-done | bytes 1441816
  81.0 14.5 %layer.1 = (bf16[512,512]{1,0:T(8,128)(2,1)S(1)}, bf16[512,512]{1,0:T(8,128)(2,1)S(1)}) custom-call(s32[32]{0:T(128)S(1)} %copy-done.9, s32[8]{0:T(128)S(1)} %copy-done.10, bf16[256,512]{1,0:T(8,128)(2,1)S(1)} %get-tuple-element.95.keep_ref, bf16[256,512]{1,0:T(8,128)(2,1)S(1)} %collective-permute-done.18.got_ref, f32[1,1024]{1,0:T(1,128)S(1)} %bitcast.4, ...), custom_call_target="tpu_custom_call" | custom-call | tf_op jit(solution)/shard_map/layer/pallas_call | solution.py:615
  95.7 1.8 %collective-permute-done.25.got_ref = bf16[512,512]{1,0:T(8,128)(2,1)S(1)} collective-permute-done((bf16[512,512]{1,0:T(8,128)(2,1)S(1)}, bf16[512,512]{1,0:T(8,128)(2,1)S(1)}, u32[]{:S(2)}, u32[]{:S(2)}) %collective-permute-start.25) | collective-permute-done | bytes 524320 | tf_op jit(solution)/shard_map/ppermute | solution.py:325
  97.5 1.0 %finish.1 = bf16[1024,512]{1,0:T(8,128)(2,1)} custom-call(bf16[512,512]{1,0:T(8,128)(2,1)S(1)} %get-tuple-element.109.own_ref, bf16[512,512]{1,0:T(8,128)(2,1)S(1)} %collective-permute-done.25.got_ref), custom_call_target="tpu_custom_call" | custom-call | tf_op jit(solution)/shard_map/finish/pallas_call | solution.py:639
  (73 shorter events, 5.3 us)
Async XLA Ops:
  0.0 17.7 %collective-permute-start.2 = (bf16[4,256,512]{2,1,0:T(8,128)(2,1)}, bf16[4,256,512]{2,1,0:T(8,128)(2,1)S(1)}, u32[]{:S(2)}, u32[]{:S(2)}) collective-permute-start(bf16[4,256,512]{2,1,0:T(8,128)(2,1)} %refs_1_.1), channel_id=1, source_target_pairs={{0,1},{1,0},{2,3},{3,2},{4,5},{5,4},{6,7},{7,6},{8,9},{9,8},{10,11... | collective-permute-start | bytes 3145736 | tf_op jit(solution)/shard_map/ppermute | solution.py:325
  0.5 15.2 %collective-permute-start.3 = (bf16[512,256]{1,0:T(8,128)(2,1)}, bf16[512,256]{1,0:T(8,128)(2,1)S(1)}, u32[]{:S(2)}, u32[]{:S(2)}) collective-permute-start(bf16[512,256]{1,0:T(8,128)(2,1)} %refs_2_.1), channel_id=1, source_target_pairs={{0,1},{1,0},{2,3},{3,2},{4,5},{5,4},{6,7},{7,6},{8,9},{9,8},{10,11... | collective-permute-start | bytes 786440 | tf_op jit(solution)/shard_map/ppermute | solution.py:325
  4.0 13.7 %collective-permute-start = (bf16[352,512]{1,0:T(8,128)(2,1)S(1)}, bf16[352,512]{1,0:T(8,128)(2,1)S(1)}, u32[]{:S(2)}, u32[]{:S(2)}) collective-permute-start(bf16[352,512]{1,0:T(8,128)(2,1)S(1)} %pack.1), channel_id=1, source_target_pairs={{0,4},{4,8},{8,12},{12,0},{1,5},{5,9},{9,13},{13,1},{2,6},{6,10},{... | collective-permute-start | bytes 1081352 | tf_op jit(solution)/shard_map/ppermute | solution.py:325
  8.7 13.3 %copy-start.10 = (s32[8]{0:T(128)S(1)}, s32[8]{0:T(128)}, u32[]{:S(2)}) copy-start(s32[8]{0:T(128)} %lens_ref.3) | copy-start | bytes 100
  8.7 13.3 %copy-start.14 = (s32[8,256]{1,0:T(8,128)S(1)}, s32[8,256]{1,0:T(8,128)}, u32[]{:S(2)}) copy-start(s32[8,256]{1,0:T(8,128)} %time_ref.1) | copy-start | bytes 24580
  14.4 1.2 %collective-permute-start.1 = (f32[4,176]{1,0:T(4,128)S(1)}, f32[4,176]{1,0:T(4,128)S(1)}, u32[]{:S(2)}, u32[]{:S(2)}) collective-permute-start(f32[4,176]{1,0:T(4,128)S(1)} %pad_maximum_fusion), channel_id=1, source_target_pairs={{0,1},{1,0},{2,3},{3,2},{4,5},{5,4},{6,7},{7,6},{8,9},{9,8},{10,11... | collective-permute-start | bytes 8456 | tf_op jit(solution)/shard_map/ppermute | solution.py:325
  15.7 27.9 %copy-start.12 = (bf16[2048,512]{1,0:T(8,128)(2,1)S(1)}, bf16[2048,512]{1,0:T(8,128)(2,1)}, u32[]{:S(2)}) copy-start(bf16[2048,512]{1,0:T(8,128)(2,1)} %table_ref.3) | copy-start | bytes 6291460
  17.7 19.4 %collective-permute-start.7 = (bf16[352,512]{1,0:T(8,128)(2,1)S(1)}, bf16[352,512]{1,0:T(8,128)(2,1)S(1)}, u32[]{:S(2)}, u32[]{:S(2)}) collective-permute-start(bf16[352,512]{1,0:T(8,128)(2,1)S(1)} %collective-permute-done.refs_0_), channel_id=1, source_target_pairs={{0,16},{1,3},{2,18},{3,1},{16,0},{17,19},{18,2},{19,17},{4,20},{5,... | collective-permute-start | bytes 1081352 | tf_op jit(solution)/shard_map/ppermute | solution.py:334
  19.2 17.9 %collective-permute-start.6 = (bf16[352,512]{1,0:T(8,128)(2,1)S(1)}, bf16[352,512]{1,0:T(8,128)(2,1)S(1)}, u32[]{:S(2)}, u32[]{:S(2)}) collective-permute-start(bf16[352,512]{1,0:T(8,128)(2,1)S(1)} %collective-permute-done.refs_0_), channel_id=1, source_target_pairs={{0,2},{1,17},{2,0},{3,19},{16,18},{17,1},{18,16},{19,3},{4,6},{5,2... | collective-permute-start | bytes 1081352 | tf_op jit(solution)/shard_map/ppermute | solution.py:334
  20.7 16.4 %collective-permute-start.4 = (bf16[352,512]{1,0:T(8,128)(2,1)S(1)}, bf16[352,512]{1,0:T(8,128)(2,1)S(1)}, u32[]{:S(2)}, u32[]{:S(2)}) collective-permute-start(bf16[352,512]{1,0:T(8,128)(2,1)S(1)} %collective-permute-done.refs_0_), channel_id=1, source_target_pairs={{0,4},{4,8},{8,12},{12,0},{1,5},{5,9},{9,13},{13,1},{2,6},{6,10},{... | collective-permute-start | bytes 1081352 | tf_op jit(solution)/shard_map/ppermute | solution.py:325
  20.7 16.4 %collective-permute-start.5 = (bf16[256,512]{1,0:T(8,128)(2,1)S(1)}, bf16[256,512]{1,0:T(8,128)(2,1)S(1)}, u32[]{:S(2)}, u32[]{:S(2)}) collective-permute-start(bf16[256,512]{1,0:T(8,128)(2,1)S(1)} %get-tuple-element.68), channel_id=1, source_target_pairs={{0,4},{4,8},{8,12},{12,0},{1,5},{5,9},{9,13},{13,1},{2,6},{6,10},{... | collective-permute-start | bytes 786440 | tf_op jit(solution)/shard_map/ppermute | solution.py:325
  37.1 14.7 %collective-permute-start.11 = (bf16[352,512]{1,0:T(8,128)(2,1)S(1)}, bf16[352,512]{1,0:T(8,128)(2,1)S(1)}, u32[]{:S(2)}, u32[]{:S(2)}) collective-permute-start(bf16[352,512]{1,0:T(8,128)(2,1)S(1)} %collective-permute-done.4.refs_0_), channel_id=1, source_target_pairs={{0,16},{1,3},{2,18},{3,1},{16,0},{17,19},{18,2},{19,17},{4,20},{5,... | collective-permute-start | bytes 1081352 | tf_op jit(solution)/shard_map/ppermute | solution.py:334
  37.7 14.2 %collective-permute-start.10 = (bf16[352,512]{1,0:T(8,128)(2,1)S(1)}, bf16[352,512]{1,0:T(8,128)(2,1)S(1)}, u32[]{:S(2)}, u32[]{:S(2)}) collective-permute-start(bf16[352,512]{1,0:T(8,128)(2,1)S(1)} %collective-permute-done.4.refs_0_), channel_id=1, source_target_pairs={{0,2},{1,17},{2,0},{3,19},{16,18},{17,1},{18,16},{19,3},{4,6},{5,2... | collective-permute-start | bytes 1081352 | tf_op jit(solution)/shard_map/ppermute | solution.py:334
  38.5 13.4 %collective-permute-start.9 = (bf16[352,512]{1,0:T(8,128)(2,1)S(1)}, bf16[352,512]{1,0:T(8,128)(2,1)S(1)}, u32[]{:S(2)}, u32[]{:S(2)}) collective-permute-start(bf16[352,512]{1,0:T(8,128)(2,1)S(1)} %collective-permute-done.4.refs_0_), channel_id=1, source_target_pairs={{0,4},{4,8},{8,12},{12,0},{1,5},{5,9},{9,13},{13,1},{2,6},{6,10},{... | collective-permute-start | bytes 1081352 | tf_op jit(solution)/shard_map/ppermute | solution.py:325
  38.5 13.4 %collective-permute-start.12 = (bf16[256,512]{1,0:T(8,128)(2,1)S(1)}, bf16[256,512]{1,0:T(8,128)(2,1)S(1)}, u32[]{:S(2)}, u32[]{:S(2)}) collective-permute-start(bf16[256,512]{1,0:T(8,128)(2,1)S(1)} %get-tuple-element.76), channel_id=1, source_target_pairs={{0,12},{4,0},{8,4},{12,8},{1,13},{5,1},{9,5},{13,9},{2,14},{6,2},{... | collective-permute-start | bytes 786440 | tf_op jit(solution)/shard_map/ppermute | solution.py:325
  42.3 9.5 %collective-permute-start.8 = (bf16[352,512]{1,0:T(8,128)(2,1)S(1)}, bf16[352,512]{1,0:T(8,128)(2,1)S(1)}, u32[]{:S(2)}, u32[]{:S(2)}) collective-permute-start(bf16[352,512]{1,0:T(8,128)(2,1)S(1)} %collective-permute-done.7.refs_2_), channel_id=1, source_target_pairs={{0,2},{1,17},{2,0},{3,19},{16,18},{17,1},{18,16},{19,3},{4,6},{5,2... | collective-permute-start | bytes 1081352 | tf_op jit(solution)/shard_map/ppermute | solution.py:334
  52.5 17.5 %collective-permute-start.16 = (bf16[4,352,512]{2,1,0:T(8,128)(2,1)S(1)}, bf16[4,352,512]{2,1,0:T(8,128)(2,1)S(1)}, u32[]{:S(2)}, u32[]{:S(2)}) collective-permute-start(bf16[4,352,512]{2,1,0:T(8,128)(2,1)S(1)} %merge.2.refs_5_), channel_id=1, source_target_pairs={{0,1},{1,0},{2,3},{3,2},{4,5},{5,4},{6,7},{7,6},{8,9},{9,8},{10,11... | collective-permute-start | bytes 4325384 | tf_op jit(solution)/shard_map/ppermute | solution.py:325
  52.5 17.4 %collective-permute-start.15 = (bf16[352,512]{1,0:T(8,128)(2,1)S(1)}, bf16[352,512]{1,0:T(8,128)(2,1)S(1)}, u32[]{:S(2)}, u32[]{:S(2)}) collective-permute-start(bf16[352,512]{1,0:T(8,128)(2,1)S(1)} %collective-permute-done.11.refs_2_), channel_id=1, source_target_pairs={{0,2},{1,17},{2,0},{3,19},{16,18},{17,1},{18,16},{19,3},{4,6},{5,2... | collective-permute-start | bytes 1081352 | tf_op jit(solution)/shard_map/ppermute | solution.py:334
  53.6 16.4 %collective-permute-start.14 = (bf16[352,512]{1,0:T(8,128)(2,1)S(1)}, bf16[352,512]{1,0:T(8,128)(2,1)S(1)}, u32[]{:S(2)}, u32[]{:S(2)}) collective-permute-start(bf16[352,512]{1,0:T(8,128)(2,1)S(1)} %collective-permute-done.9.refs_9_), channel_id=1, source_target_pairs={{0,16},{1,3},{2,18},{3,1},{16,0},{17,19},{18,2},{19,17},{4,20},{5,... | collective-permute-start | bytes 1081352 | tf_op jit(solution)/shard_map/ppermute | solution.py:334
  55.2 14.8 %collective-permute-start.13 = (bf16[352,512]{1,0:T(8,128)(2,1)S(1)}, bf16[352,512]{1,0:T(8,128)(2,1)S(1)}, u32[]{:S(2)}, u32[]{:S(2)}) collective-permute-start(bf16[352,512]{1,0:T(8,128)(2,1)S(1)} %collective-permute-done.9.refs_9_), channel_id=1, source_target_pairs={{0,2},{1,17},{2,0},{3,19},{16,18},{17,1},{18,16},{19,3},{4,6},{5,2... | collective-permute-start | bytes 1081352 | tf_op jit(solution)/shard_map/ppermute | solution.py:334
  55.7 14.3 %collective-permute-start.17 = (bf16[256,512]{1,0:T(8,128)(2,1)S(1)}, bf16[256,512]{1,0:T(8,128)(2,1)S(1)}, u32[]{:S(2)}, u32[]{:S(2)}) collective-permute-start(bf16[256,512]{1,0:T(8,128)(2,1)S(1)} %get-tuple-element.92), channel_id=1, source_target_pairs={{0,8},{4,12},{8,0},{12,4},{1,9},{5,13},{9,1},{13,5},{2,10},{6,14},... | collective-permute-start | bytes 786440 | tf_op jit(solution)/shard_map/ppermute | solution.py:325
  70.6 10.4 %copy-start.2 = (bf16[4,256,512]{2,1,0:T(8,128)(2,1)S(1)}, bf16[4,256,512]{2,1,0:T(8,128)(2,1)}, u32[]{:S(2)}) copy-start(bf16[4,256,512]{2,1,0:T(8,128)(2,1)} %refs_1_.1) | copy-start | bytes 3145732
  70.6 10.4 %copy-start.5 = (bf16[512,256]{1,0:T(8,128)(2,1)S(1)}, bf16[512,256]{1,0:T(8,128)(2,1)}, u32[]{:S(2)}) copy-start(bf16[512,256]{1,0:T(8,128)(2,1)} %refs_0_.1) | copy-start | bytes 786436
  70.6 10.4 %copy-start.7 = (bf16[512,256]{1,0:T(8,128)(2,1)S(1)}, bf16[512,256]{1,0:T(8,128)(2,1)}, u32[]{:S(2)}) copy-start(bf16[512,256]{1,0:T(8,128)(2,1)} %refs_2_.1) | copy-start | bytes 786436
  70.6 9.2 %collective-permute-start.19 = (bf16[4,352,512]{2,1,0:T(8,128)(2,1)S(1)}, bf16[4,352,512]{2,1,0:T(8,128)(2,1)S(1)}, u32[]{:S(2)}, u32[]{:S(2)}) collective-permute-start(bf16[4,352,512]{2,1,0:T(8,128)(2,1)S(1)} %merge.3.refs_7_), channel_id=1, source_target_pairs={{0,1},{1,0},{2,3},{3,2},{4,5},{5,4},{6,7},{7,6},{8,9},{9,8},{10,11... | collective-permute-start | bytes 4325384 | tf_op jit(solution)/shard_map/ppermute | solution.py:325
  70.7 7.5 %collective-permute-start.23 = (bf16[352,512]{1,0:T(8,128)(2,1)S(1)}, bf16[352,512]{1,0:T(8,128)(2,1)S(1)}, u32[]{:S(2)}, u32[]{:S(2)}) collective-permute-start(bf16[352,512]{1,0:T(8,128)(2,1)S(1)} %collective-permute-done.14.refs_13_), channel_id=1, source_target_pairs={{0,2},{1,17},{2,0},{3,19},{16,18},{17,1},{18,16},{19,3},{4,6},{5,2... | collective-permute-start | bytes 1081352 | tf_op jit(solution)/shard_map/ppermute | solution.py:334
  72.3 2.0 %collective-permute-start.18 = (bf16[256,512]{1,0:T(8,128)(2,1)S(1)}, bf16[256,512]{1,0:T(8,128)(2,1)S(1)}, u32[]{:S(2)}, u32[]{:S(2)}) collective-permute-start(bf16[256,512]{1,0:T(8,128)(2,1)S(1)} %get-tuple-element.96), channel_id=1, source_target_pairs={{0,1},{1,0},{2,3},{3,2},{4,5},{5,4},{6,7},{7,6},{8,9},{9,8},{10,11... | collective-permute-start | bytes 786440 | tf_op jit(solution)/shard_map/ppermute | solution.py:325
  73.1 5.1 %collective-permute-start.22 = (bf16[352,512]{1,0:T(8,128)(2,1)S(1)}, bf16[352,512]{1,0:T(8,128)(2,1)S(1)}, u32[]{:S(2)}, u32[]{:S(2)}) collective-permute-start(bf16[352,512]{1,0:T(8,128)(2,1)S(1)} %collective-permute-done.14.refs_13_), channel_id=1, source_target_pairs={{0,1},{1,0},{2,3},{3,2},{4,5},{5,4},{6,7},{7,6},{8,9},{9,8},{10,11... | collective-permute-start | bytes 1081352 | tf_op jit(solution)/shard_map/ppermute | solution.py:325
  73.2 5.0 %collective-permute-start.20 = (bf16[352,512]{1,0:T(8,128)(2,1)S(1)}, bf16[352,512]{1,0:T(8,128)(2,1)S(1)}, u32[]{:S(2)}, u32[]{:S(2)}) collective-permute-start(bf16[352,512]{1,0:T(8,128)(2,1)S(1)} %collective-permute-done.9.refs_9_), channel_id=1, source_target_pairs={{0,1},{1,0},{2,3},{3,2},{4,5},{5,4},{6,7},{7,6},{8,9},{9,8},{10,11... | collective-permute-start | bytes 1081352 | tf_op jit(solution)/shard_map/ppermute | solution.py:325
  74.3 3.9 %collective-permute-start.21 = (bf16[352,512]{1,0:T(8,128)(2,1)S(1)}, bf16[352,512]{1,0:T(8,128)(2,1)S(1)}, u32[]{:S(2)}, u32[]{:S(2)}) collective-permute-start(bf16[352,512]{1,0:T(8,128)(2,1)S(1)} %collective-permute-done.13.refs_11_), channel_id=1, source_target_pairs={{0,1},{1,0},{2,3},{3,2},{4,5},{5,4},{6,7},{7,6},{8,9},{9,8},{10,11... | collective-permute-start | bytes 1081352 | tf_op jit(solution)/shard_map/ppermute | solution.py:325
  78.2 1.7 %collective-permute-start.24 = (bf16[352,512]{1,0:T(8,128)(2,1)S(1)}, bf16[352,512]{1,0:T(8,128)(2,1)S(1)}, u32[]{:S(2)}, u32[]{:S(2)}) collective-permute-start(bf16[352,512]{1,0:T(8,128)(2,1)S(1)} %collective-permute-done.23.refs_15_), channel_id=1, source_target_pairs={{0,1},{1,0},{2,3},{3,2},{4,5},{5,4},{6,7},{7,6},{8,9},{9,8},{10,11... | collective-permute-start | bytes 1081352 | tf_op jit(solution)/shard_map/ppermute | solution.py:325
  95.5 2.0 %collective-permute-start.25 = (bf16[512,512]{1,0:T(8,128)(2,1)S(1)}, bf16[512,512]{1,0:T(8,128)(2,1)S(1)}, u32[]{:S(2)}, u32[]{:S(2)}) collective-permute-start(bf16[512,512]{1,0:T(8,128)(2,1)S(1)} %get-tuple-element.110), channel_id=1, source_target_pairs={{0,1},{1,0},{2,3},{3,2},{4,5},{5,4},{6,7},{7,6},{8,9},{9,8},{10,11... | collective-permute-start | bytes 1572872 | tf_op jit(solution)/shard_map/ppermute | solution.py:325
  (14 other events, 47.0 us)

commit v5 on v4

--- a/solution.py
+++ b/solution.py
@@ -13,6 +13,7 @@
 F32 = jnp.float32
 MIB = 1024 * 1024
 FAR = -1e30
+ROW_BLOCKS = 1
 
 
 def buckets_of(length, buckets):
@@ -225,7 +226,9 @@
                 term = jnp.zeros((block, size), F32)
                 for b in range(tbuckets):
                     term = jnp.where(diff == b, small_ref[h, buckets + b], term)
-                bias_ref[u, h, rows, :] = jnp.where(valid, bias_ref[u, h, rows, :] + term, FAR)
+                bias_ref[u, h, rows, :] = jnp.where(
+                    valid, 0.5 * (bias_ref[u, h, rows, :] + term), FAR
+                )
 
 
 def silu(s):
@@ -281,27 +284,31 @@
         lax.fori_loop(0, width // step, project, 0, unroll=True)
     for c in copies[5]:
         c.wait()
-    scale = 1.0 / math.sqrt(width // z.heads)
+    scale = 0.5 / math.sqrt(width // z.heads)
     size = width // z.heads
     for u in range(z.mine):
         user = member(z, plan_ref, table_pos, bal_pos * z.pair + mp_pos * z.mine + u)
         inverse = 1.0 / jnp.full((1, z.length), lens_ref[user], jnp.int32).astype(F32)
         rows = slice(u * z.length, (u + 1) * z.length)
 
-        def attend(h, carry):
-            total, square = carry
-            cols = pl.ds(pl.multiple_of(h * size, size), size)
-            s = dot_nt(act_ref[2, rows, cols], act_ref[3, rows, cols]) * scale + bias_ref[u, h]
-            a = (silu(s) * inverse).astype(BF)
-            y = dot(a, act_ref[1, rows, cols])
-            y_ref[rows, cols] = y
-            return (
-                total + jnp.sum(y, axis=1, keepdims=True),
-                square + jnp.sum(y * y, axis=1, keepdims=True),
-            )
-
-        zero = jnp.zeros((z.length, 1), F32)
-        total, square = lax.fori_loop(0, z.heads, attend, (zero, zero), unroll=4)
+        block = z.length // ROW_BLOCKS
+        total = [jnp.zeros((block, 1), F32) for _ in range(ROW_BLOCKS)]
+        square = [jnp.zeros((block, 1), F32) for _ in range(ROW_BLOCKS)]
+        for h in range(z.heads):
+            cols = slice(h * size, (h + 1) * size)
+            for part in range(ROW_BLOCKS):
+                first = u * z.length + part * block
+                mine = slice(first, first + block)
+                keys = slice(u * z.length, first + block)
+                seen = (part + 1) * block
+                s = dot_nt(act_ref[2, mine, cols], act_ref[3, keys, cols]) * scale
+                s = s + bias_ref[u, h, part * block : seen, :seen]
+                a = ((s + s * jnp.tanh(s)) * inverse[:, :seen]).astype(BF)
+                y = dot(a, act_ref[1, keys, cols])
+                y_ref[mine, cols] = y
+                total[part] = total[part] + jnp.sum(y, axis=1, keepdims=True)
+                square[part] = square[part] + jnp.sum(y * y, axis=1, keepdims=True)
+        total, square = jnp.concatenate(total, 0), jnp.concatenate(square, 0)
         mean = total / width
         var = square / width - mean * mean
         factor = lax.rsqrt(var + epsilon)
@@ -546,7 +553,7 @@
             in_specs=[pl.BlockSpec(memory_space=pltpu.HBM)] * 3,
             out_specs=vspec(),
             scratch_shapes=[pltpu.SemaphoreType.DMA],
-            compiler_params=params(4),
+            compiler_params=params(60),
             name="pack",
         )(embed_proj, qkvu_proj, out_proj)
         merge = pl.pallas_call(
@@ -569,15 +576,15 @@
         got1 = swap(sent[0], "table", z.n, 1)
         r2 = hop(r1)
         bias = make_bias(table, plan, lengths, time_bucket)
-        r1, r2, got1, a1, b1, bias, sent, plan1, gains = fence(
-            r1, r2, got1, a1, b1, bias, sent, plan, gains
+        r1, a1, b1, r2, got1, bias, sent, plan1, gains = fence(
+            r1, a1, b1, r2, got1, bias, sent, plan, gains
         )
         b2, a2, d1 = cross(r2, False), cross(r2, True), cross(b1, True)
         got3 = swap(sent[2], "table", z.n, 3)
         r3 = hop(r2)
         own, route = keep_rows(plan1, hist_ids, table_rows, scale)
-        r1, a1, b1, d1, r2, r3, a2, b2, got3, own, route, sent = fence(
-            r1, a1, b1, d1, r2, r3, a2, b2, got3, own, route, sent
+        r1, a1, b1, d1, r2, a2, b2, r3, got3, own, route, sent = fence(
+            r1, a1, b1, d1, r2, a2, b2, r3, got3, own, route, sent
         )
         a3, b3, d2 = cross(r3, True), cross(r3, False), cross(b2, True)
         got2 = swap(sent[1], "table", z.n, 2)
@@ -632,7 +639,7 @@
             pltpu.VMEM(bias.shape, F32),
             pltpu.SemaphoreType.DMA((7,)),
         ],
-        compiler_params=params(44),
+        compiler_params=params(36),
         name="layer",
     )(plan, lengths, keep, back, in_gain.reshape(1, width), gains, bias, *weights)
     out_got = swap(out_give, "mp", z.mp)

time: 98.8 us -> 94.4 us (0.955)
  local copies, waits for them, and re-layouts: 7.91 us -> 1.72 us
  waiting for transfers between devices: 34.7 us -> 37.3 us
  starting transfers between devices: 22.9 us -> 21.5 us
    unnamed x40 -> x28, local copies, waits for them, and re-layouts: 7.84 us -> 1.65 us
    ppermute x17, waiting for transfers between devices: 31.1 us -> 33.6 us  [swap(): return lax.ppermute(x, axis, [(i, (i + k) % size) for i in range(size)])]
    ppermute x17, starting transfers between devices: 13.1 us -> 10.8 us  [swap(): return lax.ppermute(x, axis, [(i, (i + k) % size) for i in range(size)])]
    pallas_call x1, Pallas kernels: 0.36 us -> 1.67 us  [body(): pl.pallas_call(pack_kernel, out_shape=jax.ShapeDtypeStruct((rows, qkvu_pr...]
  transfers between devices with their start and end apart: 26 -> 26, of which waited for: 9 -> 9; matrix products, arithmetic and copies ran while one was open for 0% -> 0% of each run, Pallas kernels for 16% -> 18%
where the time goes in v5:
time: 94.4 us; the launch traced here: 94.2 us
  waiting for transfers between devices  37.3 us (40%)
  Pallas kernels  33.4 us (35%)
  starting transfers between devices  21.5 us (23%)
  local copies, waits for them, and re-layouts  1.72 us (2%)
    ppermute x17, waiting for transfers between devices, swap(): return lax.ppermute(x, axis, [(i, (i + k) % size) for i in range(size)])  33.6 us
    pallas_call x1, Pallas kernels, body(): pl.pallas_call(functools.partial(layer_kernel, z, load, len(weights)), ou...  13.8 us
    ppermute x17, starting transfers between devices, swap(): return lax.ppermute(x, axis, [(i, (i + k) % size) for i in range(size)])  10.8 us
    ppermute x9, starting transfers between devices, cross(): return lax.ppermute(x, ('parts', 'bal', 'mp'), pairs)  10.7 us
    pallas_call x1, Pallas kernels, body(): sent = send_rows(plan, hist_ids, table_rows, scale)  5.52 us
    pallas_call x1, Pallas kernels, body(): bias = make_bias(table, plan, lengths, time_bucket)  5.03 us
    pallas_call x1, Pallas kernels, body(): own, route = keep_rows(plan1, hist_ids, table_rows, scale)  4.54 us
    ppermute x9, waiting for transfers between devices, cross(): return lax.ppermute(x, ('parts', 'bal', 'mp'), pairs)  3.64 us
  transfers between devices with their start and end apart: 26, of which 9 were waited for; matrix products, arithmetic and copies ran while one was open for 0% of the time, Pallas kernels for 18%

profile of v5, /device:TPU:0, one launch (start us, length us, event | category | flops | bytes accessed | tf_op | source)
XLA Modules:
  0.0 94.2 jit_solution(2396870569010430508)
XLA Ops:
  0.6 1.7 %pack.1 = bf16[352,512]{1,0:T(8,128)(2,1)} custom-call(bf16[512,256]{1,0:T(8,128)(2,1)} %refs_0_.1, bf16[4,256,512]{2,1,0:T(8,128)(2,1)} %refs_1_.1, bf16[512,256]{1,0:T(8,128)(2,1)} %refs_2_.1), custom_call_target="tpu_custom_call" | custom-call | tf_op jit(solution)/shard_map/pack/pallas_call | solution.py:550
  2.3 3.1 %collective-permute-start = (bf16[352,512]{1,0:T(8,128)(2,1)}, bf16[352,512]{1,0:T(8,128)(2,1)S(1)}, u32[]{:S(2)}, u32[]{:S(2)}) collective-permute-start(bf16[352,512]{1,0:T(8,128)(2,1)} %pack.1), channel_id=1, source_target_pairs={{0,4},{4,8},{8,12},{12,0},{1,5},{5,9},{9,13},{13,1},{2,6},{6,10},{... | collective-permute-start | bytes 1081352 | tf_op jit(solution)/shard_map/ppermute | solution.py:332
  5.4 1.6 %copy-done.6 = bf16[2048,512]{1,0:T(8,128)(2,1)S(1)} copy-done((bf16[2048,512]{1,0:T(8,128)(2,1)S(1)}, bf16[2048,512]{1,0:T(8,128)(2,1)}, u32[]{:S(2)}) %copy-start.6) | copy-done | bytes 2097176
  7.0 5.5 %send_rows.1 = (bf16[256,512]{1,0:T(8,128)(2,1)S(1)}, bf16[256,512]{1,0:T(8,128)(2,1)S(1)}, bf16[256,512]{1,0:T(8,128)(2,1)S(1)}) custom-call(s32[32]{0:T(128)S(1)} %copy-done.4, s32[32,256]{1,0:T(8,128)S(1)} %copy-done.8, bf16[2048,512]{1,0:T(8,128)(2,1)S(1)} %copy-done.6, f32[16,128]{1,0:T(8,128)S(1)} %bitcast.5), custom_call_target="tpu_custom_call" | custom-call | flops 6300000256 | bytes 14000000 | tf_op jit(solution)/shard_map/send_rows/pallas_call | solution.py:570
  12.6 1.1 %collective-permute-done.1 = f32[4,176]{1,0:T(4,128)S(1)} collective-permute-done((f32[4,176]{1,0:T(4,128)S(1)}, f32[4,176]{1,0:T(4,128)S(1)}, u32[]{:S(2)}, u32[]{:S(2)}) %collective-permute-start.1) | collective-permute-done | bytes 2848 | tf_op jit(solution)/shard_map/ppermute | solution.py:332
  13.9 2.3 %collective-permute-done.refs_0_ = bf16[352,512]{1,0:T(8,128)(2,1)S(1)} collective-permute-done((bf16[352,512]{1,0:T(8,128)(2,1)}, bf16[352,512]{1,0:T(8,128)(2,1)S(1)}, u32[]{:S(2)}, u32[]{:S(2)}) %collective-permute-start) | collective-permute-done | bytes 360480 | tf_op jit(solution)/shard_map/ppermute | solution.py:332
  16.2 1.5 %collective-permute-start.5 = (bf16[352,512]{1,0:T(8,128)(2,1)S(1)}, bf16[352,512]{1,0:T(8,128)(2,1)S(1)}, u32[]{:S(2)}, u32[]{:S(2)}) collective-permute-start(bf16[352,512]{1,0:T(8,128)(2,1)S(1)} %collective-permute-done.refs_0_), channel_id=1, source_target_pairs={{0,16},{1,3},{2,18},{3,1},{16,0},{17,19},{18,2},{19,17},{4,20},{5,... | collective-permute-start | bytes 1081352 | tf_op jit(solution)/shard_map/ppermute | solution.py:341
  17.8 1.5 %collective-permute-start.4 = (bf16[352,512]{1,0:T(8,128)(2,1)S(1)}, bf16[352,512]{1,0:T(8,128)(2,1)S(1)}, u32[]{:S(2)}, u32[]{:S(2)}) collective-permute-start(bf16[352,512]{1,0:T(8,128)(2,1)S(1)} %collective-permute-done.refs_0_), channel_id=1, source_target_pairs={{0,2},{1,17},{2,0},{3,19},{16,18},{17,1},{18,16},{19,3},{4,6},{5,2... | collective-permute-start | bytes 1081352 | tf_op jit(solution)/shard_map/ppermute | solution.py:341
  19.3 1.3 %collective-permute-start.7 = (bf16[256,512]{1,0:T(8,128)(2,1)S(1)}, bf16[256,512]{1,0:T(8,128)(2,1)S(1)}, u32[]{:S(2)}, u32[]{:S(2)}) collective-permute-start(bf16[256,512]{1,0:T(8,128)(2,1)S(1)} %get-tuple-element.68), channel_id=1, source_target_pairs={{0,4},{4,8},{8,12},{12,0},{1,5},{5,9},{9,13},{13,1},{2,6},{6,10},{... | collective-permute-start | bytes 786440 | tf_op jit(solution)/shard_map/ppermute | solution.py:332
  20.6 5.0 %bias.1.bias_hbm = f32[2,8,256,256]{3,2,1,0:T(8,128)S(1)} custom-call(f32[8,48]{1,0:T(8,128)S(1)} %slice.8.small_ref, s32[32]{0:T(128)S(1)} %copy-done.4, s32[8]{0:T(128)S(1)} %copy-done.5, s32[8,256]{1,0:T(8,128)S(1)} %copy-done.9), custom_call_target="tpu_custom_call" | custom-call | flops 6300000256 | bytes 14000000 | tf_op jit(solution)/shard_map/bias/pallas_call | solution.py:578
  25.6 7.9 %collective-permute-done.7.refs_0_ = bf16[256,512]{1,0:T(8,128)(2,1)S(1)} collective-permute-done((bf16[256,512]{1,0:T(8,128)(2,1)S(1)}, bf16[256,512]{1,0:T(8,128)(2,1)S(1)}, u32[]{:S(2)}, u32[]{:S(2)}) %collective-permute-start.7) | collective-permute-done | bytes 262176 | tf_op jit(solution)/shard_map/ppermute | solution.py:332
  33.6 1.3 %collective-permute-start.10 = (bf16[352,512]{1,0:T(8,128)(2,1)S(1)}, bf16[352,512]{1,0:T(8,128)(2,1)S(1)}, u32[]{:S(2)}, u32[]{:S(2)}) collective-permute-start(bf16[352,512]{1,0:T(8,128)(2,1)S(1)} %collective-permute-done.6.refs_0_), channel_id=1, source_target_pairs={{0,16},{1,3},{2,18},{3,1},{16,0},{17,19},{18,2},{19,17},{4,20},{5,... | collective-permute-start | bytes 1081352 | tf_op jit(solution)/shard_map/ppermute | solution.py:341
  35.0 1.5 %collective-permute-start.9 = (bf16[352,512]{1,0:T(8,128)(2,1)S(1)}, bf16[352,512]{1,0:T(8,128)(2,1)S(1)}, u32[]{:S(2)}, u32[]{:S(2)}) collective-permute-start(bf16[352,512]{1,0:T(8,128)(2,1)S(1)} %collective-permute-done.6.refs_0_), channel_id=1, source_target_pairs={{0,2},{1,17},{2,0},{3,19},{16,18},{17,1},{18,16},{19,3},{4,6},{5,2... | collective-permute-start | bytes 1081352 | tf_op jit(solution)/shard_map/ppermute | solution.py:341
  36.4 3.7 %collective-permute-start.12 = (bf16[256,512]{1,0:T(8,128)(2,1)S(1)}, bf16[256,512]{1,0:T(8,128)(2,1)S(1)}, u32[]{:S(2)}, u32[]{:S(2)}) collective-permute-start(bf16[256,512]{1,0:T(8,128)(2,1)S(1)} %get-tuple-element.76), channel_id=1, source_target_pairs={{0,12},{4,0},{8,4},{12,8},{1,13},{5,1},{9,5},{13,9},{2,14},{6,2},{... | collective-permute-start | bytes 786440 | tf_op jit(solution)/shard_map/ppermute | solution.py:332
  40.2 0.5 collective-permute-start.8
  40.7 4.5 %keep_rows.1 = (bf16[512,512]{1,0:T(8,128)(2,1)S(1)}, bf16[512,768]{1,0:T(8,128)(2,1)S(1)}) custom-call(s32[32]{0:T(128)S(1)} %copy-done.4, s32[32,256]{1,0:T(8,128)S(1)} %copy-done.8, bf16[2048,512]{1,0:T(8,128)(2,1)S(1)} %copy-done.7, f32[16,128]{1,0:T(8,128)S(1)} %bitcast.6), custom_call_target="tpu_custom_call" | custom-call | flops 6300000256 | bytes 14000000 | tf_op jit(solution)/shard_map/keep_rows/pallas_call | solution.py:585
  45.3 4.8 %collective-permute-done.12.refs_2_ = bf16[256,512]{1,0:T(8,128)(2,1)S(1)} collective-permute-done((bf16[256,512]{1,0:T(8,128)(2,1)S(1)}, bf16[256,512]{1,0:T(8,128)(2,1)S(1)}, u32[]{:S(2)}, u32[]{:S(2)}) %collective-permute-start.12) | collective-permute-done | bytes 262176 | tf_op jit(solution)/shard_map/ppermute | solution.py:332
  50.1 0.6 merge.2.refs_5_
  50.8 0.7 collective-permute-start.15
  51.5 1.0 %collective-permute-start.14 = (bf16[352,512]{1,0:T(8,128)(2,1)S(1)}, bf16[352,512]{1,0:T(8,128)(2,1)S(1)}, u32[]{:S(2)}, u32[]{:S(2)}) collective-permute-start(bf16[352,512]{1,0:T(8,128)(2,1)S(1)} %collective-permute-done.11.refs_9_), channel_id=1, source_target_pairs={{0,16},{1,3},{2,18},{3,1},{16,0},{17,19},{18,2},{19,17},{4,20},{5,... | collective-permute-start | bytes 1081352 | tf_op jit(solution)/shard_map/ppermute | solution.py:341
  52.5 1.0 %collective-permute-start.13 = (bf16[352,512]{1,0:T(8,128)(2,1)S(1)}, bf16[352,512]{1,0:T(8,128)(2,1)S(1)}, u32[]{:S(2)}, u32[]{:S(2)}) collective-permute-start(bf16[352,512]{1,0:T(8,128)(2,1)S(1)} %collective-permute-done.11.refs_9_), channel_id=1, source_target_pairs={{0,2},{1,17},{2,0},{3,19},{16,18},{17,1},{18,16},{19,3},{4,6},{5,2... | collective-permute-start | bytes 1081352 | tf_op jit(solution)/shard_map/ppermute | solution.py:341
  53.5 0.9 collective-permute-start.17
  54.4 13.1 %collective-permute-done.17.refs_1_ = bf16[256,512]{1,0:T(8,128)(2,1)S(1)} collective-permute-done((bf16[256,512]{1,0:T(8,128)(2,1)S(1)}, bf16[256,512]{1,0:T(8,128)(2,1)S(1)}, u32[]{:S(2)}, u32[]{:S(2)}) %collective-permute-start.17) | collective-permute-done | bytes 262176 | tf_op jit(solution)/shard_map/ppermute | solution.py:332
  67.5 0.6 merge.3.refs_7_
  68.2 1.6 %collective-permute-start.23 = (bf16[352,512]{1,0:T(8,128)(2,1)S(1)}, bf16[352,512]{1,0:T(8,128)(2,1)S(1)}, u32[]{:S(2)}, u32[]{:S(2)}) collective-permute-start(bf16[352,512]{1,0:T(8,128)(2,1)S(1)} %collective-permute-done.14.refs_13_), channel_id=1, source_target_pairs={{0,2},{1,17},{2,0},{3,19},{16,18},{17,1},{18,16},{19,3},{4,6},{5,2... | collective-permute-start | bytes 1081352 | tf_op jit(solution)/shard_map/ppermute | solution.py:341
  69.8 0.6 place_rows.1
  71.0 0.9 %collective-permute-done.18.got_ref = bf16[256,512]{1,0:T(8,128)(2,1)S(1)} collective-permute-done((bf16[256,512]{1,0:T(8,128)(2,1)S(1)}, bf16[256,512]{1,0:T(8,128)(2,1)S(1)}, u32[]{:S(2)}, u32[]{:S(2)}) %collective-permute-start.18) | collective-permute-done | bytes 262176 | tf_op jit(solution)/shard_map/ppermute | solution.py:332
  72.1 3.6 %collective-permute-done.23.refs_15_ = bf16[352,512]{1,0:T(8,128)(2,1)S(1)} collective-permute-done((bf16[352,512]{1,0:T(8,128)(2,1)S(1)}, bf16[352,512]{1,0:T(8,128)(2,1)S(1)}, u32[]{:S(2)}, u32[]{:S(2)}) %collective-permute-start.23) | collective-permute-done | bytes 360480 | tf_op jit(solution)/shard_map/ppermute | solution.py:341
  75.7 1.7 %collective-permute-done.24.refs_16_ = bf16[352,512]{1,0:T(8,128)(2,1)S(1)} collective-permute-done((bf16[352,512]{1,0:T(8,128)(2,1)S(1)}, bf16[352,512]{1,0:T(8,128)(2,1)S(1)}, u32[]{:S(2)}, u32[]{:S(2)}) %collective-permute-start.24) | collective-permute-done | bytes 360480 | tf_op jit(solution)/shard_map/ppermute | solution.py:332
  77.4 13.8 %layer.1 = (bf16[512,512]{1,0:T(8,128)(2,1)S(1)}, bf16[512,512]{1,0:T(8,128)(2,1)S(1)}) custom-call(s32[32]{0:T(128)S(1)} %copy-done.4, s32[8]{0:T(128)S(1)} %copy-done.5, bf16[256,512]{1,0:T(8,128)(2,1)S(1)} %get-tuple-element.95.keep_ref, bf16[256,512]{1,0:T(8,128)(2,1)S(1)} %collective-permute-done.18.got_ref, f32[1,1024]{1,0:T(1,128)S(1)} %bitcast.4, ...), custom_call_target="tpu_custom_call" | custom-call | tf_op jit(solution)/shard_map/layer/pallas_call | solution.py:622
  91.4 1.8 %collective-permute-done.25.got_ref = bf16[512,512]{1,0:T(8,128)(2,1)S(1)} collective-permute-done((bf16[512,512]{1,0:T(8,128)(2,1)S(1)}, bf16[512,512]{1,0:T(8,128)(2,1)S(1)}, u32[]{:S(2)}, u32[]{:S(2)}) %collective-permute-start.25) | collective-permute-done | bytes 524320 | tf_op jit(solution)/shard_map/ppermute | solution.py:332
  93.2 1.0 %finish.1 = bf16[1024,512]{1,0:T(8,128)(2,1)} custom-call(bf16[512,512]{1,0:T(8,128)(2,1)S(1)} %get-tuple-element.109.own_ref, bf16[512,512]{1,0:T(8,128)(2,1)S(1)} %collective-permute-done.25.got_ref), custom_call_target="tpu_custom_call" | custom-call | tf_op jit(solution)/shard_map/finish/pallas_call | solution.py:646
  (61 shorter events, 2.2 us)
Async XLA Ops:
  0.0 16.2 %collective-permute-start.2 = (bf16[4,256,512]{2,1,0:T(8,128)(2,1)}, bf16[4,256,512]{2,1,0:T(8,128)(2,1)S(1)}, u32[]{:S(2)}, u32[]{:S(2)}) collective-permute-start(bf16[4,256,512]{2,1,0:T(8,128)(2,1)} %refs_1_.1), channel_id=1, source_target_pairs={{0,1},{1,0},{2,3},{3,2},{4,5},{5,4},{6,7},{7,6},{8,9},{9,8},{10,11... | collective-permute-start | bytes 3145736 | tf_op jit(solution)/shard_map/ppermute | solution.py:332
  0.5 13.4 %collective-permute-start.3 = (bf16[512,256]{1,0:T(8,128)(2,1)}, bf16[512,256]{1,0:T(8,128)(2,1)S(1)}, u32[]{:S(2)}, u32[]{:S(2)}) collective-permute-start(bf16[512,256]{1,0:T(8,128)(2,1)} %refs_2_.1), channel_id=1, source_target_pairs={{0,1},{1,0},{2,3},{3,2},{4,5},{5,4},{6,7},{7,6},{8,9},{9,8},{10,11... | collective-permute-start | bytes 786440 | tf_op jit(solution)/shard_map/ppermute | solution.py:332
  2.3 13.9 %collective-permute-start = (bf16[352,512]{1,0:T(8,128)(2,1)}, bf16[352,512]{1,0:T(8,128)(2,1)S(1)}, u32[]{:S(2)}, u32[]{:S(2)}) collective-permute-start(bf16[352,512]{1,0:T(8,128)(2,1)} %pack.1), channel_id=1, source_target_pairs={{0,4},{4,8},{8,12},{12,0},{1,5},{5,9},{9,13},{13,1},{2,6},{6,10},{... | collective-permute-start | bytes 1081352 | tf_op jit(solution)/shard_map/ppermute | solution.py:332
  7.0 13.6 %copy-start.5 = (s32[8]{0:T(128)S(1)}, s32[8]{0:T(128)}, u32[]{:S(2)}) copy-start(s32[8]{0:T(128)} %lens_ref.3) | copy-start | bytes 100
  7.0 13.6 %copy-start.9 = (s32[8,256]{1,0:T(8,128)S(1)}, s32[8,256]{1,0:T(8,128)}, u32[]{:S(2)}) copy-start(s32[8,256]{1,0:T(8,128)} %time_ref.1) | copy-start | bytes 24580
  12.6 1.2 %collective-permute-start.1 = (f32[4,176]{1,0:T(4,128)S(1)}, f32[4,176]{1,0:T(4,128)S(1)}, u32[]{:S(2)}, u32[]{:S(2)}) collective-permute-start(f32[4,176]{1,0:T(4,128)S(1)} %pad_maximum_fusion), channel_id=1, source_target_pairs={{0,1},{1,0},{2,3},{3,2},{4,5},{5,4},{6,7},{7,6},{8,9},{9,8},{10,11... | collective-permute-start | bytes 8456 | tf_op jit(solution)/shard_map/ppermute | solution.py:332
  13.9 26.8 %copy-start.7 = (bf16[2048,512]{1,0:T(8,128)(2,1)S(1)}, bf16[2048,512]{1,0:T(8,128)(2,1)}, u32[]{:S(2)}) copy-start(bf16[2048,512]{1,0:T(8,128)(2,1)} %table_ref.3) | copy-start | bytes 6291460
  16.2 17.3 %collective-permute-start.6 = (bf16[352,512]{1,0:T(8,128)(2,1)S(1)}, bf16[352,512]{1,0:T(8,128)(2,1)S(1)}, u32[]{:S(2)}, u32[]{:S(2)}) collective-permute-start(bf16[352,512]{1,0:T(8,128)(2,1)S(1)} %collective-permute-done.refs_0_), channel_id=1, source_target_pairs={{0,4},{4,8},{8,12},{12,0},{1,5},{5,9},{9,13},{13,1},{2,6},{6,10},{... | collective-permute-start | bytes 1081352 | tf_op jit(solution)/shard_map/ppermute | solution.py:332
  16.2 17.3 %collective-permute-start.5 = (bf16[352,512]{1,0:T(8,128)(2,1)S(1)}, bf16[352,512]{1,0:T(8,128)(2,1)S(1)}, u32[]{:S(2)}, u32[]{:S(2)}) collective-permute-start(bf16[352,512]{1,0:T(8,128)(2,1)S(1)} %collective-permute-done.refs_0_), channel_id=1, source_target_pairs={{0,16},{1,3},{2,18},{3,1},{16,0},{17,19},{18,2},{19,17},{4,20},{5,... | collective-permute-start | bytes 1081352 | tf_op jit(solution)/shard_map/ppermute | solution.py:341
  17.8 15.8 %collective-permute-start.4 = (bf16[352,512]{1,0:T(8,128)(2,1)S(1)}, bf16[352,512]{1,0:T(8,128)(2,1)S(1)}, u32[]{:S(2)}, u32[]{:S(2)}) collective-permute-start(bf16[352,512]{1,0:T(8,128)(2,1)S(1)} %collective-permute-done.refs_0_), channel_id=1, source_target_pairs={{0,2},{1,17},{2,0},{3,19},{16,18},{17,1},{18,16},{19,3},{4,6},{5,2... | collective-permute-start | bytes 1081352 | tf_op jit(solution)/shard_map/ppermute | solution.py:341
  19.3 14.3 %collective-permute-start.7 = (bf16[256,512]{1,0:T(8,128)(2,1)S(1)}, bf16[256,512]{1,0:T(8,128)(2,1)S(1)}, u32[]{:S(2)}, u32[]{:S(2)}) collective-permute-start(bf16[256,512]{1,0:T(8,128)(2,1)S(1)} %get-tuple-element.68), channel_id=1, source_target_pairs={{0,4},{4,8},{8,12},{12,0},{1,5},{5,9},{9,13},{13,1},{2,6},{6,10},{... | collective-permute-start | bytes 786440 | tf_op jit(solution)/shard_map/ppermute | solution.py:332
  33.5 16.5 %collective-permute-start.11 = (bf16[352,512]{1,0:T(8,128)(2,1)S(1)}, bf16[352,512]{1,0:T(8,128)(2,1)S(1)}, u32[]{:S(2)}, u32[]{:S(2)}) collective-permute-start(bf16[352,512]{1,0:T(8,128)(2,1)S(1)} %collective-permute-done.6.refs_0_), channel_id=1, source_target_pairs={{0,4},{4,8},{8,12},{12,0},{1,5},{5,9},{9,13},{13,1},{2,6},{6,10},{... | collective-permute-start | bytes 1081352 | tf_op jit(solution)/shard_map/ppermute | solution.py:332
  33.6 16.5 %collective-permute-start.10 = (bf16[352,512]{1,0:T(8,128)(2,1)S(1)}, bf16[352,512]{1,0:T(8,128)(2,1)S(1)}, u32[]{:S(2)}, u32[]{:S(2)}) collective-permute-start(bf16[352,512]{1,0:T(8,128)(2,1)S(1)} %collective-permute-done.6.refs_0_), channel_id=1, source_target_pairs={{0,16},{1,3},{2,18},{3,1},{16,0},{17,19},{18,2},{19,17},{4,20},{5,... | collective-permute-start | bytes 1081352 | tf_op jit(solution)/shard_map/ppermute | solution.py:341
  35.0 15.1 %collective-permute-start.9 = (bf16[352,512]{1,0:T(8,128)(2,1)S(1)}, bf16[352,512]{1,0:T(8,128)(2,1)S(1)}, u32[]{:S(2)}, u32[]{:S(2)}) collective-permute-start(bf16[352,512]{1,0:T(8,128)(2,1)S(1)} %collective-permute-done.6.refs_0_), channel_id=1, source_target_pairs={{0,2},{1,17},{2,0},{3,19},{16,18},{17,1},{18,16},{19,3},{4,6},{5,2... | collective-permute-start | bytes 1081352 | tf_op jit(solution)/shard_map/ppermute | solution.py:341
  36.4 13.6 %collective-permute-start.12 = (bf16[256,512]{1,0:T(8,128)(2,1)S(1)}, bf16[256,512]{1,0:T(8,128)(2,1)S(1)}, u32[]{:S(2)}, u32[]{:S(2)}) collective-permute-start(bf16[256,512]{1,0:T(8,128)(2,1)S(1)} %get-tuple-element.76), channel_id=1, source_target_pairs={{0,12},{4,0},{8,4},{12,8},{1,13},{5,1},{9,5},{13,9},{2,14},{6,2},{... | collective-permute-start | bytes 786440 | tf_op jit(solution)/shard_map/ppermute | solution.py:332
  40.2 9.9 %collective-permute-start.8 = (bf16[352,512]{1,0:T(8,128)(2,1)S(1)}, bf16[352,512]{1,0:T(8,128)(2,1)S(1)}, u32[]{:S(2)}, u32[]{:S(2)}) collective-permute-start(bf16[352,512]{1,0:T(8,128)(2,1)S(1)} %collective-permute-done.5.refs_2_), channel_id=1, source_target_pairs={{0,2},{1,17},{2,0},{3,19},{16,18},{17,1},{18,16},{19,3},{4,6},{5,2... | collective-permute-start | bytes 1081352 | tf_op jit(solution)/shard_map/ppermute | solution.py:341
  50.7 16.8 %collective-permute-start.16 = (bf16[4,352,512]{2,1,0:T(8,128)(2,1)S(1)}, bf16[4,352,512]{2,1,0:T(8,128)(2,1)S(1)}, u32[]{:S(2)}, u32[]{:S(2)}) collective-permute-start(bf16[4,352,512]{2,1,0:T(8,128)(2,1)S(1)} %merge.2.refs_5_), channel_id=1, source_target_pairs={{0,1},{1,0},{2,3},{3,2},{4,5},{5,4},{6,7},{7,6},{8,9},{9,8},{10,11... | collective-permute-start | bytes 4325384 | tf_op jit(solution)/shard_map/ppermute | solution.py:332
  50.8 16.7 %collective-permute-start.15 = (bf16[352,512]{1,0:T(8,128)(2,1)S(1)}, bf16[352,512]{1,0:T(8,128)(2,1)S(1)}, u32[]{:S(2)}, u32[]{:S(2)}) collective-permute-start(bf16[352,512]{1,0:T(8,128)(2,1)S(1)} %collective-permute-done.10.refs_2_), channel_id=1, source_target_pairs={{0,2},{1,17},{2,0},{3,19},{16,18},{17,1},{18,16},{19,3},{4,6},{5,2... | collective-permute-start | bytes 1081352 | tf_op jit(solution)/shard_map/ppermute | solution.py:341
  51.5 15.9 %collective-permute-start.14 = (bf16[352,512]{1,0:T(8,128)(2,1)S(1)}, bf16[352,512]{1,0:T(8,128)(2,1)S(1)}, u32[]{:S(2)}, u32[]{:S(2)}) collective-permute-start(bf16[352,512]{1,0:T(8,128)(2,1)S(1)} %collective-permute-done.11.refs_9_), channel_id=1, source_target_pairs={{0,16},{1,3},{2,18},{3,1},{16,0},{17,19},{18,2},{19,17},{4,20},{5,... | collective-permute-start | bytes 1081352 | tf_op jit(solution)/shard_map/ppermute | solution.py:341
  52.5 14.9 %collective-permute-start.13 = (bf16[352,512]{1,0:T(8,128)(2,1)S(1)}, bf16[352,512]{1,0:T(8,128)(2,1)S(1)}, u32[]{:S(2)}, u32[]{:S(2)}) collective-permute-start(bf16[352,512]{1,0:T(8,128)(2,1)S(1)} %collective-permute-done.11.refs_9_), channel_id=1, source_target_pairs={{0,2},{1,17},{2,0},{3,19},{16,18},{17,1},{18,16},{19,3},{4,6},{5,2... | collective-permute-start | bytes 1081352 | tf_op jit(solution)/shard_map/ppermute | solution.py:341
  53.5 13.9 %collective-permute-start.17 = (bf16[256,512]{1,0:T(8,128)(2,1)S(1)}, bf16[256,512]{1,0:T(8,128)(2,1)S(1)}, u32[]{:S(2)}, u32[]{:S(2)}) collective-permute-start(bf16[256,512]{1,0:T(8,128)(2,1)S(1)} %get-tuple-element.92), channel_id=1, source_target_pairs={{0,8},{4,12},{8,0},{12,4},{1,9},{5,13},{9,1},{13,5},{2,10},{6,14},... | collective-permute-start | bytes 786440 | tf_op jit(solution)/shard_map/ppermute | solution.py:332
  68.1 9.3 %copy-start = (bf16[4,256,512]{2,1,0:T(8,128)(2,1)S(1)}, bf16[4,256,512]{2,1,0:T(8,128)(2,1)}, u32[]{:S(2)}) copy-start(bf16[4,256,512]{2,1,0:T(8,128)(2,1)} %refs_1_.1) | copy-start | bytes 3145732
  68.1 9.3 %copy-start.1 = (bf16[512,256]{1,0:T(8,128)(2,1)S(1)}, bf16[512,256]{1,0:T(8,128)(2,1)}, u32[]{:S(2)}) copy-start(bf16[512,256]{1,0:T(8,128)(2,1)} %refs_0_.1) | copy-start | bytes 786436
  68.1 9.3 %copy-start.2 = (bf16[512,256]{1,0:T(8,128)(2,1)S(1)}, bf16[512,256]{1,0:T(8,128)(2,1)}, u32[]{:S(2)}) copy-start(bf16[512,256]{1,0:T(8,128)(2,1)} %refs_2_.1) | copy-start | bytes 786436
  68.1 9.2 %collective-permute-start.19 = (bf16[4,352,512]{2,1,0:T(8,128)(2,1)S(1)}, bf16[4,352,512]{2,1,0:T(8,128)(2,1)S(1)}, u32[]{:S(2)}, u32[]{:S(2)}) collective-permute-start(bf16[4,352,512]{2,1,0:T(8,128)(2,1)S(1)} %merge.3.refs_7_), channel_id=1, source_target_pairs={{0,1},{1,0},{2,3},{3,2},{4,5},{5,4},{6,7},{7,6},{8,9},{9,8},{10,11... | collective-permute-start | bytes 4325384 | tf_op jit(solution)/shard_map/ppermute | solution.py:332
  68.2 7.5 %collective-permute-start.23 = (bf16[352,512]{1,0:T(8,128)(2,1)S(1)}, bf16[352,512]{1,0:T(8,128)(2,1)S(1)}, u32[]{:S(2)}, u32[]{:S(2)}) collective-permute-start(bf16[352,512]{1,0:T(8,128)(2,1)S(1)} %collective-permute-done.14.refs_13_), channel_id=1, source_target_pairs={{0,2},{1,17},{2,0},{3,19},{16,18},{17,1},{18,16},{19,3},{4,6},{5,2... | collective-permute-start | bytes 1081352 | tf_op jit(solution)/shard_map/ppermute | solution.py:341
  70.3 1.6 %collective-permute-start.18 = (bf16[256,512]{1,0:T(8,128)(2,1)S(1)}, bf16[256,512]{1,0:T(8,128)(2,1)S(1)}, u32[]{:S(2)}, u32[]{:S(2)}) collective-permute-start(bf16[256,512]{1,0:T(8,128)(2,1)S(1)} %get-tuple-element.96), channel_id=1, source_target_pairs={{0,1},{1,0},{2,3},{3,2},{4,5},{5,4},{6,7},{7,6},{8,9},{9,8},{10,11... | collective-permute-start | bytes 786440 | tf_op jit(solution)/shard_map/ppermute | solution.py:332
  70.4 5.3 %collective-permute-start.22 = (bf16[352,512]{1,0:T(8,128)(2,1)S(1)}, bf16[352,512]{1,0:T(8,128)(2,1)S(1)}, u32[]{:S(2)}, u32[]{:S(2)}) collective-permute-start(bf16[352,512]{1,0:T(8,128)(2,1)S(1)} %collective-permute-done.14.refs_13_), channel_id=1, source_target_pairs={{0,1},{1,0},{2,3},{3,2},{4,5},{5,4},{6,7},{7,6},{8,9},{9,8},{10,11... | collective-permute-start | bytes 1081352 | tf_op jit(solution)/shard_map/ppermute | solution.py:332
  70.9 4.8 %collective-permute-start.20 = (bf16[352,512]{1,0:T(8,128)(2,1)S(1)}, bf16[352,512]{1,0:T(8,128)(2,1)S(1)}, u32[]{:S(2)}, u32[]{:S(2)}) collective-permute-start(bf16[352,512]{1,0:T(8,128)(2,1)S(1)} %collective-permute-done.11.refs_9_), channel_id=1, source_target_pairs={{0,1},{1,0},{2,3},{3,2},{4,5},{5,4},{6,7},{7,6},{8,9},{9,8},{10,11... | collective-permute-start | bytes 1081352 | tf_op jit(solution)/shard_map/ppermute | solution.py:332
  71.9 3.8 %collective-permute-start.21 = (bf16[352,512]{1,0:T(8,128)(2,1)S(1)}, bf16[352,512]{1,0:T(8,128)(2,1)S(1)}, u32[]{:S(2)}, u32[]{:S(2)}) collective-permute-start(bf16[352,512]{1,0:T(8,128)(2,1)S(1)} %collective-permute-done.13.refs_11_), channel_id=1, source_target_pairs={{0,1},{1,0},{2,3},{3,2},{4,5},{5,4},{6,7},{7,6},{8,9},{9,8},{10,11... | collective-permute-start | bytes 1081352 | tf_op jit(solution)/shard_map/ppermute | solution.py:332
  75.7 1.7 %collective-permute-start.24 = (bf16[352,512]{1,0:T(8,128)(2,1)S(1)}, bf16[352,512]{1,0:T(8,128)(2,1)S(1)}, u32[]{:S(2)}, u32[]{:S(2)}) collective-permute-start(bf16[352,512]{1,0:T(8,128)(2,1)S(1)} %collective-permute-done.23.refs_15_), channel_id=1, source_target_pairs={{0,1},{1,0},{2,3},{3,2},{4,5},{5,4},{6,7},{7,6},{8,9},{9,8},{10,11... | collective-permute-start | bytes 1081352 | tf_op jit(solution)/shard_map/ppermute | solution.py:332
  91.2 2.0 %collective-permute-start.25 = (bf16[512,512]{1,0:T(8,128)(2,1)S(1)}, bf16[512,512]{1,0:T(8,128)(2,1)S(1)}, u32[]{:S(2)}, u32[]{:S(2)}) collective-permute-start(bf16[512,512]{1,0:T(8,128)(2,1)S(1)} %get-tuple-element.110), channel_id=1, source_target_pairs={{0,1},{1,0},{2,3},{3,2},{4,5},{5,4},{6,7},{7,6},{8,9},{9,8},{10,11... | collective-permute-start | bytes 1572872 | tf_op jit(solution)/shard_map/ppermute | solution.py:332
  (8 other events, 43.6 us)

commit v6 on v5

--- a/solution.py
+++ b/solution.py
@@ -236,8 +236,12 @@
     return half + half * jnp.tanh(half)
 
 
+def arrived(ref, sem):
+    pltpu.make_async_copy(ref, ref, sem).wait()
+
+
 def layer_kernel(
-    z, load, n_weights, plan_ref, lens_ref, keep_ref, got_ref, gain_ref, out_gain_ref, bias_hbm, *refs
+    z, load, group, n_weights, plan_ref, lens_ref, keep_ref, got_ref, gain_ref, out_gain_ref, bias_hbm, *refs
 ):
     weights = refs[:n_weights]
     own_out, give_out = refs[n_weights : n_weights + 2]
@@ -247,9 +251,9 @@
     mp_pos = lax.axis_index("mp")
     width = x_ref.shape[1]
     copies = load(weights, e_ref, w_ref, o_ref, sems)
-    copies.insert(5, [pltpu.make_async_copy(bias_hbm, bias_ref, sems.at[6])])
-    for group in copies:
-        for c in group:
+    copies.insert(2, [pltpu.make_async_copy(bias_hbm, bias_ref, sems.at[3])])
+    for batch in copies:
+        for c in batch:
             c.start()
     for u in range(z.mine):
         near = pl.multiple_of(u * z.length + mp_pos * z.half, z.half)
@@ -257,13 +261,16 @@
         rows = slice(u * z.half, (u + 1) * z.half)
         emb_ref[pl.ds(near, z.half), :] = keep_ref[rows, :]
         emb_ref[pl.ds(far, z.half), :] = got_ref[rows, :]
-    for c in copies[0]:
-        c.wait()
+    arrived(e_ref, sems.at[0])
     tokens = z.mine * z.length
     block = 256
     for r in range(0, tokens, block):
         rows = slice(r, r + block)
-        x = dot(emb_ref[rows, :], e_ref[...]).astype(BF)
+        x = []
+        for first in range(0, 2 * width, 2 * group):
+            e = [e_ref[:, first + j * group : first + (j + 1) * group] for j in range(2)]
+            x.append(dot(emb_ref[rows, :], jnp.concatenate(e, axis=0)))
+        x = jnp.concatenate(x, axis=1).astype(BF)
         x_ref[rows, :] = x
         x = x.astype(F32)
         mean = jnp.mean(x, axis=1, keepdims=True)
@@ -271,19 +278,19 @@
         var = jnp.mean(centred * centred, axis=1, keepdims=True)
         xn_ref[rows, :] = (centred * lax.rsqrt(var + epsilon) * gain_ref[...]).astype(BF)
     step = 256
+    arrived(w_ref, sems.at[1])
+    share = w_ref.shape[1] // 4
     for part in range(4):
-        for c in copies[1 + part]:
-            c.wait()
 
         def project(nb, carry):
             cols = pl.ds(pl.multiple_of(nb * step, step), step)
-            s = dot(xn_ref[...], w_ref[part, :, cols])
+            w = w_ref[:, part * share : (part + 1) * share, cols].reshape(width, step)
+            s = dot(xn_ref[...], w)
             act_ref[part, :, cols] = silu(s).astype(BF)
             return carry
 
         lax.fori_loop(0, width // step, project, 0, unroll=True)
-    for c in copies[5]:
-        c.wait()
+    arrived(bias_ref, sems.at[3])
     scale = 0.5 / math.sqrt(width // z.heads)
     size = width // z.heads
     for u in range(z.mine):
@@ -316,13 +323,22 @@
             cols = slice(h * size, (h + 1) * size)
             normed = (y_ref[rows, cols] - mean) * factor * out_gain_ref[h : h + 1, :]
             z_ref[rows, cols] = (normed * act_ref[0, rows, cols].astype(F32)).astype(BF)
-    for c in copies[6]:
-        c.wait()
+    arrived(o_ref, sems.at[2])
     out_cols = width // z.mp
     for which, ref in ((1 - mp_pos, give_out), (mp_pos, own_out)):
         for nb in range(out_cols // step):
             cols = pl.ds(pl.multiple_of(which * out_cols + nb * step, step), step)
-            term = dot(z_ref[...], o_ref[:, cols])
+            if group <= out_cols:
+                first = which * 2 * out_cols + nb * step // group * 2 * group + nb * step % group
+            else:
+                first = which * out_cols + nb * step
+            deep = o_ref.shape[0] // z.mp
+            o = []
+            for core in range(z.mp):
+                for j in range(2):
+                    lanes = pl.ds(pl.multiple_of(first + j * group, step), step)
+                    o.append(o_ref[core * deep : (core + 1) * deep, lanes])
+            term = dot(z_ref[...], jnp.concatenate(o, axis=0))
             ref[:, nb * step : (nb + 1) * step] = (
                 term + x_ref[:, cols].astype(F32)
             ).astype(BF)
@@ -362,9 +378,9 @@
     first = 4 * share
     for j in range(2):
         lanes = slice(j * cols, (j + 1) * cols)
-        add(e_ref.at[at((q * 2 + m) * 2 + j, e_part), :], out_ref.at[first : first + e_part, lanes])
+        add(e_ref.at[at(j * 8 + q * 2 + m, e_part), :], out_ref.at[first : first + e_part, lanes])
         add(
-            o_ref.at[at(q * 2 + j, o_part), :],
+            o_ref.at[at(j * 4 + q, o_part), :],
             out_ref.at[first + e_part : first + e_part + o_part, lanes],
         )
     for c in copies:
@@ -391,11 +407,10 @@
         t, m = lax.axis_index("table"), lax.axis_index("mp")
         p, b = lax.axis_index("parts"), lax.axis_index("bal")
         e_own, w_own, o_own, w_near, o_near = refs[:5]
-        deep, cols = w_own.shape[1], w_own.shape[2]
+        share, cols = w_own.shape[2], w_own.shape[3]
         e_cols = e_own.shape[1]
         o_rows = o_own.shape[0]
-        share = deep // 4
-        e_part = e_ref.shape[0] // 16
+        e_part = e_ref.shape[0] // 8
         o_part = o_rows // 8
         first = 4 * share
         along_b, along_p = p * 2 + 1 - b, (1 - p) * 2 + b
@@ -414,37 +429,34 @@
                         (1 - p) * 2 + 1 - b,
                     )[i]
                     pieces.append((ref, source, q, core))
-        groups = [[] for _ in range(6)]
+        groups = [[] for _ in range(3)]
 
         def add(g, src, dst):
             groups[g].append(pltpu.make_async_copy(src, dst, sems.at[g]))
 
-        add(0, e_own, e_ref.at[:, at(t, e_cols)])
+        def half(t, j):
+            return at(t * 2 + j, e_cols)
+
+        e_rows, o_deep = e_ref.shape[0], o_rows // 2
+        for j in range(2):
+            add(0, e_own.at[j * e_rows : (j + 1) * e_rows, :], e_ref.at[:, half(t, j)])
         for ref, source, q, core in pieces:
+            rows = at(q * 2 + core, e_part)
+            add(0, ref.at[first : first + e_part, :], e_ref.at[rows, at(source, 2 * e_cols)])
+        for core, w in ((m, w_own), (1 - m, w_near)):
+            for c in range(4):
+                rows = slice(c * share, (c + 1) * share)
+                add(1, w.at[c], w_ref.at[at(t, 4), rows, at(core, cols)])
+        for ref, source, q, core in pieces:
+            add(1, ref.at[:first, :], w_ref.at[source * 4 + q, :, at(core, cols)])
+        for core, o in ((m, o_own), (1 - m, o_near)):
             for j in range(2):
-                lanes = slice(j * e_cols, (j + 1) * e_cols)
-                rows = at((q * 2 + core) * 2 + j, e_part)
-                add(0, ref.at[first : first + e_part, lanes], e_ref.at[rows, at(source, e_cols)])
-        for c in range(4):
-            for core, w in ((m, w_own), (1 - m, w_near)):
-                add(1 + c, w.at[c], w_ref.at[c, at(t, deep), at(core, cols)])
-            for ref, source, q, core in pieces:
-                add(
-                    1 + c,
-                    ref.at[c * share : (c + 1) * share, :],
-                    w_ref.at[c, at(source * 4 + q, share), at(core, cols)],
-                )
-        for core, o in ((m, o_own), (1 - m, o_near)):
-            add(5, o, o_ref.at[at(core, o_rows), at(t, e_cols)])
+                rows = slice(j * o_deep, (j + 1) * o_deep)
+                add(2, o.at[rows, :], o_ref.at[at(core, o_deep), half(t, j)])
         for ref, source, q, core in pieces:
-            for j in range(2):
-                lanes = slice(j * e_cols, (j + 1) * e_cols)
-                rows = at(core * 8 + q * 2 + j, o_part)
-                add(
-                    5,
-                    ref.at[first + e_part : first + e_part + o_part, lanes],
-                    o_ref.at[rows, at(source, e_cols)],
-                )
+            last = first + e_part + o_part
+            rows = at(core * 4 + q, o_part)
+            add(2, ref.at[first + e_part : last, :], o_ref.at[rows, at(source, 2 * e_cols)])
         return groups
 
     return load
@@ -452,9 +464,26 @@
 
 def load_whole(refs, e_ref, w_ref, o_ref, sems):
     e, w, o = refs
-    groups = [[pltpu.make_async_copy(e, e_ref, sems.at[0])]]
-    groups += [[pltpu.make_async_copy(w.at[c], w_ref.at[c], sems.at[1 + c])] for c in range(4)]
-    return groups + [[pltpu.make_async_copy(o, o_ref, sems.at[5])]]
+    groups = [[], [], []]
+
+    def add(g, src, dst):
+        groups[g].append(pltpu.make_async_copy(src, dst, sems.at[g]))
+
+    width, share = w_ref.shape[2], w_ref.shape[1] // 4
+    e_rows, o_deep = e_ref.shape[0], o_ref.shape[0] // 2
+    for j in range(2):
+        lanes = slice(j * width, (j + 1) * width)
+        add(0, e.at[j * e_rows : (j + 1) * e_rows, :], e_ref.at[:, lanes])
+        for core in range(2):
+            rows = slice((core * 2 + j) * o_deep, (core * 2 + j + 1) * o_deep)
+            add(2, o.at[rows, :], o_ref.at[core * o_deep : (core + 1) * o_deep, lanes])
+    for c in range(4):
+        add(1, w.at[c], w_ref.at[:, c * share : (c + 1) * share, :])
+    return groups
+
+
+def blocks(w, count):
+    return w.reshape(w.shape[0], count, w.shape[1] // count, w.shape[2])
 
 
 def finish_kernel(own_ref, got_ref, out_ref):
@@ -597,7 +626,9 @@
         chunk2 = merge(r2, a2, b2, d2)
         near2 = near(chunk2)
         r3n, a3n, b3n = near(r3), near(a3), near(b3)
-        weights = [embed_proj, qkvu_proj, out_proj, w_near, o_near, chunk1, near1, chunk2, near2]
+        w_own, w_near = blocks(qkvu_proj, 4), blocks(w_near, 4)
+        group = embed_proj.shape[1]
+        weights = [embed_proj, w_own, out_proj, w_near, o_near, chunk1, near1, chunk2, near2]
         weights += [r3, r3n, a3, a3n, b3, b3n, d3, near(d3)]
         load = load_pieces(z)
     else:
@@ -610,26 +641,26 @@
         o_full = lax.all_gather(out_proj, "table", axis=1, tiled=True)
         weights = [
             lax.all_gather(embed_proj, "table", axis=1, tiled=True),
-            lax.all_gather(q_full, "mp", axis=2, tiled=True),
+            blocks(lax.all_gather(q_full, "mp", axis=2, tiled=True), 16),
             lax.all_gather(o_full, "mp", axis=0, tiled=True),
         ]
-        load = load_whole
+        load, group = load_whole, width
         keep, give = place_rows(own, route, *got)
         back = swap(give, "mp", z.mp)
 
     tokens = z.mine * z.length
     out_cols = width // z.mp
     out_own, out_give = pl.pallas_call(
-        functools.partial(layer_kernel, z, load, len(weights)),
+        functools.partial(layer_kernel, z, load, group, len(weights)),
         out_shape=[jax.ShapeDtypeStruct((tokens, out_cols), BF)] * 2,
         in_specs=[sspec(), sspec()]
         + [vspec()] * 4
         + [pl.BlockSpec(memory_space=pl.ANY)] * (1 + len(weights)),
         out_specs=[vspec()] * 2,
         scratch_shapes=[
-            pltpu.VMEM((z.width, width), BF),
-            pltpu.VMEM((4, width, width), BF),
-            pltpu.VMEM((width, width), BF),
+            pltpu.VMEM((z.width // 2, 2 * width), BF),
+            pltpu.VMEM((16, width // 4, width), BF),
+            pltpu.VMEM((width // 2, 2 * width), BF),
             pltpu.VMEM((tokens, z.width), BF),
             pltpu.VMEM((tokens, width), BF),
             pltpu.VMEM((tokens, width), BF),
@@ -637,7 +668,7 @@
             pltpu.VMEM((tokens, width), F32),
             pltpu.VMEM((tokens, width), BF),
             pltpu.VMEM(bias.shape, F32),
-            pltpu.SemaphoreType.DMA((7,)),
+            pltpu.SemaphoreType.DMA((4,)),
         ],
         compiler_params=params(36),
         name="layer",

time: 94.4 us -> 92.8 us (0.983)
  Pallas kernels: 33.4 us -> 31.7 us
    pallas_call x1, Pallas kernels: 13.8 us -> 12.1 us  [body(): pl.pallas_call(functools.partial(layer_kernel, z, load, group, len(weight...]
  transfers between devices with their start and end apart: 26 -> 26, of which waited for: 9 -> 9; matrix products, arithmetic and copies ran while one was open for 0% -> 0% of each run, Pallas kernels for 18% -> 19%
where the time goes in v6:
time: 92.8 us; the launch traced here: 92.6 us
  waiting for transfers between devices  37.3 us (40%)
  Pallas kernels  31.7 us (34%)
  starting transfers between devices  21.5 us (23%)
  local copies, waits for them, and re-layouts  1.72 us (2%)
    ppermute x17, waiting for transfers between devices, swap(): return lax.ppermute(x, axis, [(i, (i + k) % size) for i in range(size)])  33.6 us
    pallas_call x1, Pallas kernels, body(): pl.pallas_call(functools.partial(layer_kernel, z, load, group, len(weight...  12.1 us
    ppermute x17, starting transfers between devices, swap(): return lax.ppermute(x, axis, [(i, (i + k) % size) for i in range(size)])  10.8 us
    ppermute x9, starting transfers between devices, cross(): return lax.ppermute(x, ('parts', 'bal', 'mp'), pairs)  10.7 us
    pallas_call x1, Pallas kernels, body(): sent = send_rows(plan, hist_ids, table_rows, scale)  5.52 us
    pallas_call x1, Pallas kernels, body(): bias = make_bias(table, plan, lengths, time_bucket)  5.03 us
    pallas_call x1, Pallas kernels, body(): own, route = keep_rows(plan1, hist_ids, table_rows, scale)  4.54 us
    ppermute x9, waiting for transfers between devices, cross(): return lax.ppermute(x, ('parts', 'bal', 'mp'), pairs)  3.64 us
  transfers between devices with their start and end apart: 26, of which 9 were waited for; matrix products, arithmetic and copies ran while one was open for 0% of the time, Pallas kernels for 19%

profile of v6, /device:TPU:0, one launch (start us, length us, event | category | flops | bytes accessed | tf_op | source)
XLA Modules:
  0.0 92.6 jit_solution(717988461969482113)
XLA Ops:
  0.6 1.7 %pack.1 = bf16[352,512]{1,0:T(8,128)(2,1)} custom-call(bf16[512,256]{1,0:T(8,128)(2,1)} %refs_0_.1, bf16[4,256,512]{2,1,0:T(8,128)(2,1)} %w_ref.1, bf16[512,256]{1,0:T(8,128)(2,1)} %refs_2_.1), custom_call_target="tpu_custom_call" | custom-call | tf_op jit(solution)/shard_map/pack/pallas_call | solution.py:579
  2.3 3.1 %collective-permute-start = (bf16[352,512]{1,0:T(8,128)(2,1)}, bf16[352,512]{1,0:T(8,128)(2,1)S(1)}, u32[]{:S(2)}, u32[]{:S(2)}) collective-permute-start(bf16[352,512]{1,0:T(8,128)(2,1)} %pack.1), channel_id=1, source_target_pairs={{0,4},{4,8},{8,12},{12,0},{1,5},{5,9},{9,13},{13,1},{2,6},{6,10},{... | collective-permute-start | bytes 1081352 | tf_op jit(solution)/shard_map/ppermute | solution.py:348
  5.4 1.6 %copy-done.6 = bf16[2048,512]{1,0:T(8,128)(2,1)S(1)} copy-done((bf16[2048,512]{1,0:T(8,128)(2,1)S(1)}, bf16[2048,512]{1,0:T(8,128)(2,1)}, u32[]{:S(2)}) %copy-start.6) | copy-done | bytes 2097176
  7.0 5.5 %send_rows.1 = (bf16[256,512]{1,0:T(8,128)(2,1)S(1)}, bf16[256,512]{1,0:T(8,128)(2,1)S(1)}, bf16[256,512]{1,0:T(8,128)(2,1)S(1)}) custom-call(s32[32]{0:T(128)S(1)} %copy-done.4, s32[32,256]{1,0:T(8,128)S(1)} %copy-done.8, bf16[2048,512]{1,0:T(8,128)(2,1)S(1)} %copy-done.6, f32[16,128]{1,0:T(8,128)S(1)} %bitcast.9), custom_call_target="tpu_custom_call" | custom-call | flops 6300000256 | bytes 14000000 | tf_op jit(solution)/shard_map/send_rows/pallas_call | solution.py:599
  12.6 1.1 %collective-permute-done.1 = f32[4,176]{1,0:T(4,128)S(1)} collective-permute-done((f32[4,176]{1,0:T(4,128)S(1)}, f32[4,176]{1,0:T(4,128)S(1)}, u32[]{:S(2)}, u32[]{:S(2)}) %collective-permute-start.1) | collective-permute-done | bytes 2848 | tf_op jit(solution)/shard_map/ppermute | solution.py:348
  13.9 2.3 %collective-permute-done.refs_0_ = bf16[352,512]{1,0:T(8,128)(2,1)S(1)} collective-permute-done((bf16[352,512]{1,0:T(8,128)(2,1)}, bf16[352,512]{1,0:T(8,128)(2,1)S(1)}, u32[]{:S(2)}, u32[]{:S(2)}) %collective-permute-start) | collective-permute-done | bytes 360480 | tf_op jit(solution)/shard_map/ppermute | solution.py:348
  16.2 1.5 %collective-permute-start.5 = (bf16[352,512]{1,0:T(8,128)(2,1)S(1)}, bf16[352,512]{1,0:T(8,128)(2,1)S(1)}, u32[]{:S(2)}, u32[]{:S(2)}) collective-permute-start(bf16[352,512]{1,0:T(8,128)(2,1)S(1)} %collective-permute-done.refs_0_), channel_id=1, source_target_pairs={{0,16},{1,3},{2,18},{3,1},{16,0},{17,19},{18,2},{19,17},{4,20},{5,... | collective-permute-start | bytes 1081352 | tf_op jit(solution)/shard_map/ppermute | solution.py:357
  17.8 1.5 %collective-permute-start.4 = (bf16[352,512]{1,0:T(8,128)(2,1)S(1)}, bf16[352,512]{1,0:T(8,128)(2,1)S(1)}, u32[]{:S(2)}, u32[]{:S(2)}) collective-permute-start(bf16[352,512]{1,0:T(8,128)(2,1)S(1)} %collective-permute-done.refs_0_), channel_id=1, source_target_pairs={{0,2},{1,17},{2,0},{3,19},{16,18},{17,1},{18,16},{19,3},{4,6},{5,2... | collective-permute-start | bytes 1081352 | tf_op jit(solution)/shard_map/ppermute | solution.py:357
  19.3 1.3 %collective-permute-start.7 = (bf16[256,512]{1,0:T(8,128)(2,1)S(1)}, bf16[256,512]{1,0:T(8,128)(2,1)S(1)}, u32[]{:S(2)}, u32[]{:S(2)}) collective-permute-start(bf16[256,512]{1,0:T(8,128)(2,1)S(1)} %get-tuple-element.68), channel_id=1, source_target_pairs={{0,4},{4,8},{8,12},{12,0},{1,5},{5,9},{9,13},{13,1},{2,6},{6,10},{... | collective-permute-start | bytes 786440 | tf_op jit(solution)/shard_map/ppermute | solution.py:348
  20.6 5.0 %bias.1.bias_hbm = f32[2,8,256,256]{3,2,1,0:T(8,128)S(1)} custom-call(f32[8,48]{1,0:T(8,128)S(1)} %slice.8.small_ref, s32[32]{0:T(128)S(1)} %copy-done.4, s32[8]{0:T(128)S(1)} %copy-done.5, s32[8,256]{1,0:T(8,128)S(1)} %copy-done.9), custom_call_target="tpu_custom_call" | custom-call | flops 6300000256 | bytes 14000000 | tf_op jit(solution)/shard_map/bias/pallas_call | solution.py:607
  25.6 7.9 %collective-permute-done.7.refs_0_ = bf16[256,512]{1,0:T(8,128)(2,1)S(1)} collective-permute-done((bf16[256,512]{1,0:T(8,128)(2,1)S(1)}, bf16[256,512]{1,0:T(8,128)(2,1)S(1)}, u32[]{:S(2)}, u32[]{:S(2)}) %collective-permute-start.7) | collective-permute-done | bytes 262176 | tf_op jit(solution)/shard_map/ppermute | solution.py:348
  33.6 1.3 %collective-permute-start.10 = (bf16[352,512]{1,0:T(8,128)(2,1)S(1)}, bf16[352,512]{1,0:T(8,128)(2,1)S(1)}, u32[]{:S(2)}, u32[]{:S(2)}) collective-permute-start(bf16[352,512]{1,0:T(8,128)(2,1)S(1)} %collective-permute-done.6.refs_0_), channel_id=1, source_target_pairs={{0,16},{1,3},{2,18},{3,1},{16,0},{17,19},{18,2},{19,17},{4,20},{5,... | collective-permute-start | bytes 1081352 | tf_op jit(solution)/shard_map/ppermute | solution.py:357
  35.0 1.5 %collective-permute-start.9 = (bf16[352,512]{1,0:T(8,128)(2,1)S(1)}, bf16[352,512]{1,0:T(8,128)(2,1)S(1)}, u32[]{:S(2)}, u32[]{:S(2)}) collective-permute-start(bf16[352,512]{1,0:T(8,128)(2,1)S(1)} %collective-permute-done.6.refs_0_), channel_id=1, source_target_pairs={{0,2},{1,17},{2,0},{3,19},{16,18},{17,1},{18,16},{19,3},{4,6},{5,2... | collective-permute-start | bytes 1081352 | tf_op jit(solution)/shard_map/ppermute | solution.py:357
  36.4 3.7 %collective-permute-start.12 = (bf16[256,512]{1,0:T(8,128)(2,1)S(1)}, bf16[256,512]{1,0:T(8,128)(2,1)S(1)}, u32[]{:S(2)}, u32[]{:S(2)}) collective-permute-start(bf16[256,512]{1,0:T(8,128)(2,1)S(1)} %get-tuple-element.76), channel_id=1, source_target_pairs={{0,12},{4,0},{8,4},{12,8},{1,13},{5,1},{9,5},{13,9},{2,14},{6,2},{... | collective-permute-start | bytes 786440 | tf_op jit(solution)/shard_map/ppermute | solution.py:348
  40.2 0.5 collective-permute-start.8
  40.7 4.5 %keep_rows.1 = (bf16[512,512]{1,0:T(8,128)(2,1)S(1)}, bf16[512,768]{1,0:T(8,128)(2,1)S(1)}) custom-call(s32[32]{0:T(128)S(1)} %copy-done.4, s32[32,256]{1,0:T(8,128)S(1)} %copy-done.8, bf16[2048,512]{1,0:T(8,128)(2,1)S(1)} %copy-done.7, f32[16,128]{1,0:T(8,128)S(1)} %bitcast.10), custom_call_target="tpu_custom_call" | custom-call | flops 6300000256 | bytes 14000000 | tf_op jit(solution)/shard_map/keep_rows/pallas_call | solution.py:614
  45.3 4.8 %collective-permute-done.12.refs_2_ = bf16[256,512]{1,0:T(8,128)(2,1)S(1)} collective-permute-done((bf16[256,512]{1,0:T(8,128)(2,1)S(1)}, bf16[256,512]{1,0:T(8,128)(2,1)S(1)}, u32[]{:S(2)}, u32[]{:S(2)}) %collective-permute-start.12) | collective-permute-done | bytes 262176 | tf_op jit(solution)/shard_map/ppermute | solution.py:348
  50.1 0.6 merge.2.refs_5_
  50.8 0.7 collective-permute-start.15
  51.5 1.0 %collective-permute-start.14 = (bf16[352,512]{1,0:T(8,128)(2,1)S(1)}, bf16[352,512]{1,0:T(8,128)(2,1)S(1)}, u32[]{:S(2)}, u32[]{:S(2)}) collective-permute-start(bf16[352,512]{1,0:T(8,128)(2,1)S(1)} %collective-permute-done.11.refs_9_), channel_id=1, source_target_pairs={{0,16},{1,3},{2,18},{3,1},{16,0},{17,19},{18,2},{19,17},{4,20},{5,... | collective-permute-start | bytes 1081352 | tf_op jit(solution)/shard_map/ppermute | solution.py:357
  52.5 1.0 %collective-permute-start.13 = (bf16[352,512]{1,0:T(8,128)(2,1)S(1)}, bf16[352,512]{1,0:T(8,128)(2,1)S(1)}, u32[]{:S(2)}, u32[]{:S(2)}) collective-permute-start(bf16[352,512]{1,0:T(8,128)(2,1)S(1)} %collective-permute-done.11.refs_9_), channel_id=1, source_target_pairs={{0,2},{1,17},{2,0},{3,19},{16,18},{17,1},{18,16},{19,3},{4,6},{5,2... | collective-permute-start | bytes 1081352 | tf_op jit(solution)/shard_map/ppermute | solution.py:357
  53.5 0.9 collective-permute-start.17
  54.4 13.1 %collective-permute-done.17.refs_1_ = bf16[256,512]{1,0:T(8,128)(2,1)S(1)} collective-permute-done((bf16[256,512]{1,0:T(8,128)(2,1)S(1)}, bf16[256,512]{1,0:T(8,128)(2,1)S(1)}, u32[]{:S(2)}, u32[]{:S(2)}) %collective-permute-start.17) | collective-permute-done | bytes 262176 | tf_op jit(solution)/shard_map/ppermute | solution.py:348
  67.5 0.6 merge.3.refs_7_
  68.2 1.6 %collective-permute-start.23 = (bf16[352,512]{1,0:T(8,128)(2,1)S(1)}, bf16[352,512]{1,0:T(8,128)(2,1)S(1)}, u32[]{:S(2)}, u32[]{:S(2)}) collective-permute-start(bf16[352,512]{1,0:T(8,128)(2,1)S(1)} %collective-permute-done.14.refs_13_), channel_id=1, source_target_pairs={{0,2},{1,17},{2,0},{3,19},{16,18},{17,1},{18,16},{19,3},{4,6},{5,2... | collective-permute-start | bytes 1081352 | tf_op jit(solution)/shard_map/ppermute | solution.py:357
  69.8 0.6 place_rows.1
  71.0 0.9 %collective-permute-done.18.got_ref = bf16[256,512]{1,0:T(8,128)(2,1)S(1)} collective-permute-done((bf16[256,512]{1,0:T(8,128)(2,1)S(1)}, bf16[256,512]{1,0:T(8,128)(2,1)S(1)}, u32[]{:S(2)}, u32[]{:S(2)}) %collective-permute-start.18) | collective-permute-done | bytes 262176 | tf_op jit(solution)/shard_map/ppermute | solution.py:348
  72.1 3.6 %collective-permute-done.23.refs_15_ = bf16[352,512]{1,0:T(8,128)(2,1)S(1)} collective-permute-done((bf16[352,512]{1,0:T(8,128)(2,1)S(1)}, bf16[352,512]{1,0:T(8,128)(2,1)S(1)}, u32[]{:S(2)}, u32[]{:S(2)}) %collective-permute-start.23) | collective-permute-done | bytes 360480 | tf_op jit(solution)/shard_map/ppermute | solution.py:357
  75.7 1.7 %collective-permute-done.24.refs_16_ = bf16[352,512]{1,0:T(8,128)(2,1)S(1)} collective-permute-done((bf16[352,512]{1,0:T(8,128)(2,1)S(1)}, bf16[352,512]{1,0:T(8,128)(2,1)S(1)}, u32[]{:S(2)}, u32[]{:S(2)}) %collective-permute-start.24) | collective-permute-done | bytes 360480 | tf_op jit(solution)/shard_map/ppermute | solution.py:348
  77.4 12.1 %layer.1 = (bf16[512,512]{1,0:T(8,128)(2,1)S(1)}, bf16[512,512]{1,0:T(8,128)(2,1)S(1)}) custom-call(s32[32]{0:T(128)S(1)} %copy-done.4, s32[8]{0:T(128)S(1)} %copy-done.5, bf16[256,512]{1,0:T(8,128)(2,1)S(1)} %get-tuple-element.95.keep_ref, bf16[256,512]{1,0:T(8,128)(2,1)S(1)} %collective-permute-done.18.got_ref, f32[1,1024]{1,0:T(1,128)S(1)} %bitcast.8, ...), custom_call_target="tpu_custom_call" | custom-call | tf_op jit(solution)/shard_map/layer/pallas_call | solution.py:653
  89.8 1.8 %collective-permute-done.25.got_ref = bf16[512,512]{1,0:T(8,128)(2,1)S(1)} collective-permute-done((bf16[512,512]{1,0:T(8,128)(2,1)S(1)}, bf16[512,512]{1,0:T(8,128)(2,1)S(1)}, u32[]{:S(2)}, u32[]{:S(2)}) %collective-permute-start.25) | collective-permute-done | bytes 524320 | tf_op jit(solution)/shard_map/ppermute | solution.py:348
  91.5 1.0 %finish.1 = bf16[1024,512]{1,0:T(8,128)(2,1)} custom-call(bf16[512,512]{1,0:T(8,128)(2,1)S(1)} %get-tuple-element.109.own_ref, bf16[512,512]{1,0:T(8,128)(2,1)S(1)} %collective-permute-done.25.got_ref), custom_call_target="tpu_custom_call" | custom-call | tf_op jit(solution)/shard_map/finish/pallas_call | solution.py:677
  (61 shorter events, 2.2 us)
Async XLA Ops:
  0.0 16.2 %collective-permute-start.2 = (bf16[4,256,512]{2,1,0:T(8,128)(2,1)}, bf16[4,256,512]{2,1,0:T(8,128)(2,1)S(1)}, u32[]{:S(2)}, u32[]{:S(2)}) collective-permute-start(bf16[4,256,512]{2,1,0:T(8,128)(2,1)} %w_ref.1), channel_id=1, source_target_pairs={{0,1},{1,0},{2,3},{3,2},{4,5},{5,4},{6,7},{7,6},{8,9},{9,8},{10,11... | collective-permute-start | bytes 3145736 | tf_op jit(solution)/shard_map/ppermute | solution.py:348
  0.5 13.4 %collective-permute-start.3 = (bf16[512,256]{1,0:T(8,128)(2,1)}, bf16[512,256]{1,0:T(8,128)(2,1)S(1)}, u32[]{:S(2)}, u32[]{:S(2)}) collective-permute-start(bf16[512,256]{1,0:T(8,128)(2,1)} %refs_2_.1), channel_id=1, source_target_pairs={{0,1},{1,0},{2,3},{3,2},{4,5},{5,4},{6,7},{7,6},{8,9},{9,8},{10,11... | collective-permute-start | bytes 786440 | tf_op jit(solution)/shard_map/ppermute | solution.py:348
  2.3 13.9 %collective-permute-start = (bf16[352,512]{1,0:T(8,128)(2,1)}, bf16[352,512]{1,0:T(8,128)(2,1)S(1)}, u32[]{:S(2)}, u32[]{:S(2)}) collective-permute-start(bf16[352,512]{1,0:T(8,128)(2,1)} %pack.1), channel_id=1, source_target_pairs={{0,4},{4,8},{8,12},{12,0},{1,5},{5,9},{9,13},{13,1},{2,6},{6,10},{... | collective-permute-start | bytes 1081352 | tf_op jit(solution)/shard_map/ppermute | solution.py:348
  7.0 13.6 %copy-start.5 = (s32[8]{0:T(128)S(1)}, s32[8]{0:T(128)}, u32[]{:S(2)}) copy-start(s32[8]{0:T(128)} %lens_ref.3) | copy-start | bytes 100
  7.0 13.6 %copy-start.9 = (s32[8,256]{1,0:T(8,128)S(1)}, s32[8,256]{1,0:T(8,128)}, u32[]{:S(2)}) copy-start(s32[8,256]{1,0:T(8,128)} %time_ref.1) | copy-start | bytes 24580
  12.6 1.2 %collective-permute-start.1 = (f32[4,176]{1,0:T(4,128)S(1)}, f32[4,176]{1,0:T(4,128)S(1)}, u32[]{:S(2)}, u32[]{:S(2)}) collective-permute-start(f32[4,176]{1,0:T(4,128)S(1)} %pad_maximum_fusion), channel_id=1, source_target_pairs={{0,1},{1,0},{2,3},{3,2},{4,5},{5,4},{6,7},{7,6},{8,9},{9,8},{10,11... | collective-permute-start | bytes 8456 | tf_op jit(solution)/shard_map/ppermute | solution.py:348
  13.9 26.8 %copy-start.7 = (bf16[2048,512]{1,0:T(8,128)(2,1)S(1)}, bf16[2048,512]{1,0:T(8,128)(2,1)}, u32[]{:S(2)}) copy-start(bf16[2048,512]{1,0:T(8,128)(2,1)} %table_ref.3) | copy-start | bytes 6291460
  16.2 17.3 %collective-permute-start.6 = (bf16[352,512]{1,0:T(8,128)(2,1)S(1)}, bf16[352,512]{1,0:T(8,128)(2,1)S(1)}, u32[]{:S(2)}, u32[]{:S(2)}) collective-permute-start(bf16[352,512]{1,0:T(8,128)(2,1)S(1)} %collective-permute-done.refs_0_), channel_id=1, source_target_pairs={{0,4},{4,8},{8,12},{12,0},{1,5},{5,9},{9,13},{13,1},{2,6},{6,10},{... | collective-permute-start | bytes 1081352 | tf_op jit(solution)/shard_map/ppermute | solution.py:348
  16.2 17.3 %collective-permute-start.5 = (bf16[352,512]{1,0:T(8,128)(2,1)S(1)}, bf16[352,512]{1,0:T(8,128)(2,1)S(1)}, u32[]{:S(2)}, u32[]{:S(2)}) collective-permute-start(bf16[352,512]{1,0:T(8,128)(2,1)S(1)} %collective-permute-done.refs_0_), channel_id=1, source_target_pairs={{0,16},{1,3},{2,18},{3,1},{16,0},{17,19},{18,2},{19,17},{4,20},{5,... | collective-permute-start | bytes 1081352 | tf_op jit(solution)/shard_map/ppermute | solution.py:357
  17.8 15.8 %collective-permute-start.4 = (bf16[352,512]{1,0:T(8,128)(2,1)S(1)}, bf16[352,512]{1,0:T(8,128)(2,1)S(1)}, u32[]{:S(2)}, u32[]{:S(2)}) collective-permute-start(bf16[352,512]{1,0:T(8,128)(2,1)S(1)} %collective-permute-done.refs_0_), channel_id=1, source_target_pairs={{0,2},{1,17},{2,0},{3,19},{16,18},{17,1},{18,16},{19,3},{4,6},{5,2... | collective-permute-start | bytes 1081352 | tf_op jit(solution)/shard_map/ppermute | solution.py:357
  19.3 14.3 %collective-permute-start.7 = (bf16[256,512]{1,0:T(8,128)(2,1)S(1)}, bf16[256,512]{1,0:T(8,128)(2,1)S(1)}, u32[]{:S(2)}, u32[]{:S(2)}) collective-permute-start(bf16[256,512]{1,0:T(8,128)(2,1)S(1)} %get-tuple-element.68), channel_id=1, source_target_pairs={{0,4},{4,8},{8,12},{12,0},{1,5},{5,9},{9,13},{13,1},{2,6},{6,10},{... | collective-permute-start | bytes 786440 | tf_op jit(solution)/shard_map/ppermute | solution.py:348
  33.5 16.5 %collective-permute-start.11 = (bf16[352,512]{1,0:T(8,128)(2,1)S(1)}, bf16[352,512]{1,0:T(8,128)(2,1)S(1)}, u32[]{:S(2)}, u32[]{:S(2)}) collective-permute-start(bf16[352,512]{1,0:T(8,128)(2,1)S(1)} %collective-permute-done.6.refs_0_), channel_id=1, source_target_pairs={{0,4},{4,8},{8,12},{12,0},{1,5},{5,9},{9,13},{13,1},{2,6},{6,10},{... | collective-permute-start | bytes 1081352 | tf_op jit(solution)/shard_map/ppermute | solution.py:348
  33.6 16.5 %collective-permute-start.10 = (bf16[352,512]{1,0:T(8,128)(2,1)S(1)}, bf16[352,512]{1,0:T(8,128)(2,1)S(1)}, u32[]{:S(2)}, u32[]{:S(2)}) collective-permute-start(bf16[352,512]{1,0:T(8,128)(2,1)S(1)} %collective-permute-done.6.refs_0_), channel_id=1, source_target_pairs={{0,16},{1,3},{2,18},{3,1},{16,0},{17,19},{18,2},{19,17},{4,20},{5,... | collective-permute-start | bytes 1081352 | tf_op jit(solution)/shard_map/ppermute | solution.py:357
  35.0 15.1 %collective-permute-start.9 = (bf16[352,512]{1,0:T(8,128)(2,1)S(1)}, bf16[352,512]{1,0:T(8,128)(2,1)S(1)}, u32[]{:S(2)}, u32[]{:S(2)}) collective-permute-start(bf16[352,512]{1,0:T(8,128)(2,1)S(1)} %collective-permute-done.6.refs_0_), channel_id=1, source_target_pairs={{0,2},{1,17},{2,0},{3,19},{16,18},{17,1},{18,16},{19,3},{4,6},{5,2... | collective-permute-start | bytes 1081352 | tf_op jit(solution)/shard_map/ppermute | solution.py:357
  36.4 13.6 %collective-permute-start.12 = (bf16[256,512]{1,0:T(8,128)(2,1)S(1)}, bf16[256,512]{1,0:T(8,128)(2,1)S(1)}, u32[]{:S(2)}, u32[]{:S(2)}) collective-permute-start(bf16[256,512]{1,0:T(8,128)(2,1)S(1)} %get-tuple-element.76), channel_id=1, source_target_pairs={{0,12},{4,0},{8,4},{12,8},{1,13},{5,1},{9,5},{13,9},{2,14},{6,2},{... | collective-permute-start | bytes 786440 | tf_op jit(solution)/shard_map/ppermute | solution.py:348
  40.2 9.9 %collective-permute-start.8 = (bf16[352,512]{1,0:T(8,128)(2,1)S(1)}, bf16[352,512]{1,0:T(8,128)(2,1)S(1)}, u32[]{:S(2)}, u32[]{:S(2)}) collective-permute-start(bf16[352,512]{1,0:T(8,128)(2,1)S(1)} %collective-permute-done.5.refs_2_), channel_id=1, source_target_pairs={{0,2},{1,17},{2,0},{3,19},{16,18},{17,1},{18,16},{19,3},{4,6},{5,2... | collective-permute-start | bytes 1081352 | tf_op jit(solution)/shard_map/ppermute | solution.py:357
  50.7 16.8 %collective-permute-start.16 = (bf16[4,352,512]{2,1,0:T(8,128)(2,1)S(1)}, bf16[4,352,512]{2,1,0:T(8,128)(2,1)S(1)}, u32[]{:S(2)}, u32[]{:S(2)}) collective-permute-start(bf16[4,352,512]{2,1,0:T(8,128)(2,1)S(1)} %merge.2.refs_5_), channel_id=1, source_target_pairs={{0,1},{1,0},{2,3},{3,2},{4,5},{5,4},{6,7},{7,6},{8,9},{9,8},{10,11... | collective-permute-start | bytes 4325384 | tf_op jit(solution)/shard_map/ppermute | solution.py:348
  50.8 16.7 %collective-permute-start.15 = (bf16[352,512]{1,0:T(8,128)(2,1)S(1)}, bf16[352,512]{1,0:T(8,128)(2,1)S(1)}, u32[]{:S(2)}, u32[]{:S(2)}) collective-permute-start(bf16[352,512]{1,0:T(8,128)(2,1)S(1)} %collective-permute-done.10.refs_2_), channel_id=1, source_target_pairs={{0,2},{1,17},{2,0},{3,19},{16,18},{17,1},{18,16},{19,3},{4,6},{5,2... | collective-permute-start | bytes 1081352 | tf_op jit(solution)/shard_map/ppermute | solution.py:357
  51.5 15.9 %collective-permute-start.14 = (bf16[352,512]{1,0:T(8,128)(2,1)S(1)}, bf16[352,512]{1,0:T(8,128)(2,1)S(1)}, u32[]{:S(2)}, u32[]{:S(2)}) collective-permute-start(bf16[352,512]{1,0:T(8,128)(2,1)S(1)} %collective-permute-done.11.refs_9_), channel_id=1, source_target_pairs={{0,16},{1,3},{2,18},{3,1},{16,0},{17,19},{18,2},{19,17},{4,20},{5,... | collective-permute-start | bytes 1081352 | tf_op jit(solution)/shard_map/ppermute | solution.py:357
  52.5 14.9 %collective-permute-start.13 = (bf16[352,512]{1,0:T(8,128)(2,1)S(1)}, bf16[352,512]{1,0:T(8,128)(2,1)S(1)}, u32[]{:S(2)}, u32[]{:S(2)}) collective-permute-start(bf16[352,512]{1,0:T(8,128)(2,1)S(1)} %collective-permute-done.11.refs_9_), channel_id=1, source_target_pairs={{0,2},{1,17},{2,0},{3,19},{16,18},{17,1},{18,16},{19,3},{4,6},{5,2... | collective-permute-start | bytes 1081352 | tf_op jit(solution)/shard_map/ppermute | solution.py:357
  53.5 13.9 %collective-permute-start.17 = (bf16[256,512]{1,0:T(8,128)(2,1)S(1)}, bf16[256,512]{1,0:T(8,128)(2,1)S(1)}, u32[]{:S(2)}, u32[]{:S(2)}) collective-permute-start(bf16[256,512]{1,0:T(8,128)(2,1)S(1)} %get-tuple-element.92), channel_id=1, source_target_pairs={{0,8},{4,12},{8,0},{12,4},{1,9},{5,13},{9,1},{13,5},{2,10},{6,14},... | collective-permute-start | bytes 786440 | tf_op jit(solution)/shard_map/ppermute | solution.py:348
  68.1 9.3 %copy-start = (bf16[4,256,512]{2,1,0:T(8,128)(2,1)S(1)}, bf16[4,256,512]{2,1,0:T(8,128)(2,1)}, u32[]{:S(2)}) copy-start(bf16[4,256,512]{2,1,0:T(8,128)(2,1)} %w_ref.1) | copy-start | bytes 3145732
  68.1 9.3 %copy-start.1 = (bf16[512,256]{1,0:T(8,128)(2,1)S(1)}, bf16[512,256]{1,0:T(8,128)(2,1)}, u32[]{:S(2)}) copy-start(bf16[512,256]{1,0:T(8,128)(2,1)} %refs_0_.1) | copy-start | bytes 786436
  68.1 9.3 %copy-start.2 = (bf16[512,256]{1,0:T(8,128)(2,1)S(1)}, bf16[512,256]{1,0:T(8,128)(2,1)}, u32[]{:S(2)}) copy-start(bf16[512,256]{1,0:T(8,128)(2,1)} %refs_2_.1) | copy-start | bytes 786436
  68.1 9.2 %collective-permute-start.19 = (bf16[4,352,512]{2,1,0:T(8,128)(2,1)S(1)}, bf16[4,352,512]{2,1,0:T(8,128)(2,1)S(1)}, u32[]{:S(2)}, u32[]{:S(2)}) collective-permute-start(bf16[4,352,512]{2,1,0:T(8,128)(2,1)S(1)} %merge.3.refs_7_), channel_id=1, source_target_pairs={{0,1},{1,0},{2,3},{3,2},{4,5},{5,4},{6,7},{7,6},{8,9},{9,8},{10,11... | collective-permute-start | bytes 4325384 | tf_op jit(solution)/shard_map/ppermute | solution.py:348
  68.2 7.5 %collective-permute-start.23 = (bf16[352,512]{1,0:T(8,128)(2,1)S(1)}, bf16[352,512]{1,0:T(8,128)(2,1)S(1)}, u32[]{:S(2)}, u32[]{:S(2)}) collective-permute-start(bf16[352,512]{1,0:T(8,128)(2,1)S(1)} %collective-permute-done.14.refs_13_), channel_id=1, source_target_pairs={{0,2},{1,17},{2,0},{3,19},{16,18},{17,1},{18,16},{19,3},{4,6},{5,2... | collective-permute-start | bytes 1081352 | tf_op jit(solution)/shard_map/ppermute | solution.py:357
  70.3 1.6 %collective-permute-start.18 = (bf16[256,512]{1,0:T(8,128)(2,1)S(1)}, bf16[256,512]{1,0:T(8,128)(2,1)S(1)}, u32[]{:S(2)}, u32[]{:S(2)}) collective-permute-start(bf16[256,512]{1,0:T(8,128)(2,1)S(1)} %get-tuple-element.96), channel_id=1, source_target_pairs={{0,1},{1,0},{2,3},{3,2},{4,5},{5,4},{6,7},{7,6},{8,9},{9,8},{10,11... | collective-permute-start | bytes 786440 | tf_op jit(solution)/shard_map/ppermute | solution.py:348
  70.4 5.3 %collective-permute-start.22 = (bf16[352,512]{1,0:T(8,128)(2,1)S(1)}, bf16[352,512]{1,0:T(8,128)(2,1)S(1)}, u32[]{:S(2)}, u32[]{:S(2)}) collective-permute-start(bf16[352,512]{1,0:T(8,128)(2,1)S(1)} %collective-permute-done.14.refs_13_), channel_id=1, source_target_pairs={{0,1},{1,0},{2,3},{3,2},{4,5},{5,4},{6,7},{7,6},{8,9},{9,8},{10,11... | collective-permute-start | bytes 1081352 | tf_op jit(solution)/shard_map/ppermute | solution.py:348
  70.9 4.8 %collective-permute-start.20 = (bf16[352,512]{1,0:T(8,128)(2,1)S(1)}, bf16[352,512]{1,0:T(8,128)(2,1)S(1)}, u32[]{:S(2)}, u32[]{:S(2)}) collective-permute-start(bf16[352,512]{1,0:T(8,128)(2,1)S(1)} %collective-permute-done.11.refs_9_), channel_id=1, source_target_pairs={{0,1},{1,0},{2,3},{3,2},{4,5},{5,4},{6,7},{7,6},{8,9},{9,8},{10,11... | collective-permute-start | bytes 1081352 | tf_op jit(solution)/shard_map/ppermute | solution.py:348
  71.9 3.8 %collective-permute-start.21 = (bf16[352,512]{1,0:T(8,128)(2,1)S(1)}, bf16[352,512]{1,0:T(8,128)(2,1)S(1)}, u32[]{:S(2)}, u32[]{:S(2)}) collective-permute-start(bf16[352,512]{1,0:T(8,128)(2,1)S(1)} %collective-permute-done.13.refs_11_), channel_id=1, source_target_pairs={{0,1},{1,0},{2,3},{3,2},{4,5},{5,4},{6,7},{7,6},{8,9},{9,8},{10,11... | collective-permute-start | bytes 1081352 | tf_op jit(solution)/shard_map/ppermute | solution.py:348
  75.7 1.7 %collective-permute-start.24 = (bf16[352,512]{1,0:T(8,128)(2,1)S(1)}, bf16[352,512]{1,0:T(8,128)(2,1)S(1)}, u32[]{:S(2)}, u32[]{:S(2)}) collective-permute-start(bf16[352,512]{1,0:T(8,128)(2,1)S(1)} %collective-permute-done.23.refs_15_), channel_id=1, source_target_pairs={{0,1},{1,0},{2,3},{3,2},{4,5},{5,4},{6,7},{7,6},{8,9},{9,8},{10,11... | collective-permute-start | bytes 1081352 | tf_op jit(solution)/shard_map/ppermute | solution.py:348
  89.6 2.0 %collective-permute-start.25 = (bf16[512,512]{1,0:T(8,128)(2,1)S(1)}, bf16[512,512]{1,0:T(8,128)(2,1)S(1)}, u32[]{:S(2)}, u32[]{:S(2)}) collective-permute-start(bf16[512,512]{1,0:T(8,128)(2,1)S(1)} %get-tuple-element.110), channel_id=1, source_target_pairs={{0,1},{1,0},{2,3},{3,2},{4,5},{5,4},{6,7},{7,6},{8,9},{9,8},{10,11... | collective-permute-start | bytes 1572872 | tf_op jit(solution)/shard_map/ppermute | solution.py:348
  (8 other events, 43.6 us)
